TPU v7x, 32 devices: a whole 2x2x4 slice. The times are simulated.
32 devices in a mesh: range: 32 (over z, y, x, core).
Axes of the slice: x: 2, y: 2, z: 4, core: 2. Of those that a mesh axis runs over, the one named last changes fastest.
Arguments:
- raw: bfloat16 [2, 64, 32, 8192], P(None, None, None, 'range'), may hold values from -40 to 40
- replica: bfloat16 [2, 128], replicated, may hold values from -1 to 1
- det_bin: int32 [1024], P('range'), may hold values from 0 to 31
- det_block: int32 [1024], P('range'), may hold values from 0 to 1
- det_beam: int32 [1024], P('range'), may hold values from 0 to 7
- det_owner: int32 [1024, 1], P('range'), may hold values from 0 to 31; in each aligned block of 32 rows (0 to 31, 32 to 63, ...) at most 2 rows name the same one
Outputs:
- tracked: float32 [2048, 256], P('range')
Inputs may be any that keep to these rules, and one draw needn't show every extreme that they name: `det_owner`: in each slab's detections no owner appears more than 2 times; some owner appears exactly 2 times.
All inputs are finite; a program needn't handle non-finite values.
Results may differ from a plain program's by a relative error of at most 0.025.
Values may be sent and summed in bfloat16 or wider, within the bound.
No kernel may reach another device: no remote copies, remote signals or barrier semaphores. Data moves between devices by JAX's collectives and lax.ppermute only.
A program may use at most 256 MiB of HBM per device.

v0:
```python
import functools
import math

import jax
import jax.numpy as jnp
import ml_dtypes
import numpy as np
from jax import lax
from jax.experimental import pallas as pl
from jax.experimental.pallas import tpu as pltpu
from jax.sharding import PartitionSpec as P

BLOCK = 128
BEAMS = 8
CAP = 2

F32 = jnp.float32
BF16 = jnp.bfloat16
VMEM = pltpu.VMEM
MIB = 1024 * 1024
NT = (((1,), (1,)), ((), ()))


def vmem_spec():
    return pl.BlockSpec(memory_space=VMEM)


def smem_spec():
    return pl.BlockSpec(memory_space=pltpu.SMEM)


def hbm_spec():
    return pl.BlockSpec(memory_space=pltpu.HBM)


SHORT = pl.CostEstimate(flops=1, bytes_accessed=1, transcendentals=0)


def params(mib=16):
    return pltpu.CompilerParams(vmem_limit_bytes=int(mib * MIB))


def dot(a, b):
    return jnp.dot(a, b, preferred_element_type=F32)


def dot_nt(a, b, precision=None):
    return lax.dot_general(a, b, NT, precision=precision, preferred_element_type=F32)


def iota(shape, axis):
    return lax.broadcasted_iota(jnp.int32, shape, axis)


def halo_kernel(raw_ref, a_ref, b_ref, mark_ref, sems):
    mark_ref[...] = jnp.zeros_like(mark_ref)
    count = sems.shape[0] // 2
    size = a_ref.shape[1] // count
    copies = []
    for part, out_ref in enumerate((a_ref, b_ref)):
        for j in range(count):
            start = part * a_ref.shape[1] + j * size
            copies.append(
                pltpu.make_async_copy(
                    raw_ref.at[:, start : start + size, :BLOCK],
                    out_ref.at[:, j * size : (j + 1) * size, :],
                    sems.at[part * count + j],
                )
            )
    for copy in copies:
        copy.start()
    for copy in copies:
        copy.wait()


def first_gates(raw):
    half = jax.ShapeDtypeStruct((2, raw.shape[1] // 2, BLOCK), BF16)
    return pl.pallas_call(
        halo_kernel,
        out_shape=[half, half, jax.ShapeDtypeStruct((8, 128), F32)],
        in_specs=[hbm_spec()],
        out_specs=[vmem_spec()] * 3,
        scratch_shapes=[pltpu.SemaphoreType.DMA((8,))],
        compiler_params=params(63),
    )(raw)


def correlation_matrix(rep_ref, out_ref):
    taps = rep_ref.shape[1]
    base = rep_ref[...].astype(F32)
    row = iota((taps, 2 * taps), 0)
    parts = []
    for i in range(2):
        line = jnp.concatenate([base[i : i + 1], jnp.zeros((1, taps), F32)], axis=1)
        skew = jnp.broadcast_to(line, (taps, 2 * taps))
        bit = 1
        while bit < taps:
            skew = jnp.where((row & bit) != 0, pltpu.roll(skew, bit, 1), skew)
            bit *= 2
        parts.append(skew.T)
    real_part, imag_part = parts
    out_ref[0] = jnp.concatenate([real_part, -imag_part], axis=1).astype(BF16)
    out_ref[1] = jnp.concatenate([imag_part, real_part], axis=1).astype(BF16)


def doppler_matrix(pulses, group):
    index = np.arange(pulses)
    angle = 2.0 * math.pi / pulses * (index[:, None] * index[None, :] % pulses)
    cosine = np.cos(angle) * pulses**-0.5
    sine = np.sin(angle) * pulses**-0.5
    table = np.stack([np.stack([cosine, -sine], 1), np.stack([sine, cosine], 1)], 0)
    full = np.einsum("ipod,ce->dociep", table, np.eye(group))
    shape = (pulses * 2 * group, 2 * group * pulses)
    return full.reshape(shape).astype(ml_dtypes.bfloat16)


def doppler_rows(total, dft):
    compressed = total.astype(BF16)
    rows, wide = compressed.shape
    half, gates = rows // 2, wide // 2
    stacked = jnp.concatenate(
        [
            jnp.concatenate([compressed[:half, :gates], compressed[half:, :gates]], axis=1),
            jnp.concatenate([compressed[:half, gates:], compressed[half:, gates:]], axis=1),
        ],
        axis=0,
    )
    both = dot(dft, stacked)
    lines = both.shape[0] // 8
    joined = jnp.concatenate(
        [both[:, :gates].reshape(lines, 8, gates), both[:, gates:].reshape(lines, 8, gates)],
        axis=1,
    )
    return joined.astype(BF16)


GROUP = 16


def half_of_bins(bins, mine):
    core = lax.axis_index("range") & 1
    return (core if mine else 1 - core) * (bins // 2)


def sent_bins(bins):
    return bins // 2 + 2


def spectra_first_kernel(raw_ref, rep_ref, dft_ref, _, s_ref, local_ref, taps_ref, *rest):
    *send_refs, buf, sems = rest
    bins, _, chans, gates = s_ref.shape
    size = GROUP * bins
    copies = [
        pltpu.make_async_copy(
            raw_ref.at[:, j * size : (j + 1) * size, :],
            buf.at[:, j * size : (j + 1) * size, :],
            sems.at[j],
        )
        for j in range(chans // GROUP)
    ]
    for copy in copies:
        copy.start()
    correlation_matrix(rep_ref, taps_ref)
    for j, copy in enumerate(copies):
        copy.wait()
        rows = slice(j * size, (j + 1) * size)
        total = dot(buf[0, rows, :], taps_ref[0]) + dot(buf[1, rows, :], taps_ref[1])
        out = doppler_rows(total, dft_ref[...])
        s_ref[:, :, j * GROUP : (j + 1) * GROUP, :] = out.reshape(bins, 2, GROUP, gates)
        later = jnp.concatenate([buf[0, rows, gates:], buf[1, rows, gates:]], axis=1)
        near = jnp.concatenate([taps_ref[0, :gates, :], taps_ref[1, :gates, :]], axis=0)
        local_ref[rows, :] = dot(later, near)
    base = half_of_bins(bins, False)
    half = chans // 2
    for part, send_ref in enumerate(send_refs):
        for k in range(send_ref.shape[0]):
            send_ref[k] = s_ref[lax.rem(base + k, bins), :, part * half : (part + 1) * half, :]


def spectra_last_kernel(part, local_ref, halo_ref, taps_ref, dft_ref, _, s_ref, send_ref):
    bins, _, chans, gates = s_ref.shape
    size = GROUP * bins
    far = jnp.concatenate([taps_ref[0, gates:, :], taps_ref[1, gates:, :]], axis=0)
    for j in range(chans // GROUP):
        rows = slice(j * size, (j + 1) * size)
        later = jnp.concatenate([halo_ref[0, rows, :], halo_ref[1, rows, :]], axis=1)
        start = part * chans * bins + j * size
        out = doppler_rows(local_ref[start : start + size, :] + dot(later, far), dft_ref[...])
        s_ref[:, :, j * GROUP : (j + 1) * GROUP, :] = out.reshape(bins, 2, GROUP, gates)
    base = half_of_bins(bins, False)
    for k in range(send_ref.shape[0]):
        send_ref[k] = s_ref[lax.rem(base + k, bins)]


def spectra_first(raw, replica, table, pulses, mark):
    _, rows, gates = raw.shape
    chans = rows // pulses
    taps = replica.shape[1]
    return pl.pallas_call(
        spectra_first_kernel,
        out_shape=[
            jax.ShapeDtypeStruct((pulses, 2, chans, BLOCK), BF16),
            jax.ShapeDtypeStruct((rows, 2 * BLOCK), F32),
            jax.ShapeDtypeStruct((2, 2 * taps, 2 * taps), BF16),
        ]
        + [jax.ShapeDtypeStruct((sent_bins(pulses), 2, chans // 2, BLOCK), BF16)] * 2,
        in_specs=[hbm_spec(), vmem_spec(), vmem_spec(), pl.BlockSpec(memory_space=pl.ANY)],
        out_specs=[vmem_spec()] * 5,
        scratch_shapes=[
            pltpu.VMEM(raw.shape, BF16),
            pltpu.SemaphoreType.DMA((chans // GROUP,)),
        ],
        compiler_params=params(),
        cost_estimate=SHORT,
    )(raw, replica, table, mark)


def spectra_last(part, local, halo, matrix, table, pulses, sums):
    chans = halo.shape[1] // pulses
    return pl.pallas_call(
        functools.partial(spectra_last_kernel, part),
        out_shape=[
            jax.ShapeDtypeStruct((pulses, 2, chans, BLOCK), BF16),
            jax.ShapeDtypeStruct((sent_bins(pulses), 2, chans, BLOCK), BF16),
        ],
        in_specs=[vmem_spec()] * 4 + [pl.BlockSpec(memory_space=pl.ANY)],
        out_specs=[vmem_spec()] * 2,
        compiler_params=params(),
        cost_estimate=SHORT,
    )(local, halo, matrix, table, sums)


def cross_kernel(count_refs, *refs):
    s_refs, rest = refs[:count_refs], refs[count_refs:]
    before_ref = rest[0] if len(rest) == 2 else None
    out_ref = rest[-1]
    held, _, _, gates = s_refs[0].shape
    chans = sum(ref.shape[2] for ref in s_refs)
    count = out_ref.shape[0]
    base = half_of_bins(held, True) if held == 2 * count else 0

    def write(e, block):
        out_ref[e] = block if before_ref is None else block + before_ref[e]

    @pl.loop(0, count // 2, unroll=2)
    def _(step):
        e = step * 2
        each = []
        for k in range(4):
            where = lax.rem(base + e + k, held)
            each.append(
                [jnp.concatenate([ref[where, o] for ref in s_refs], axis=0) for o in range(2)]
            )
        left = jnp.concatenate(
            [jnp.concatenate([re, im], axis=1) for re, im in each], axis=0
        )
        right = jnp.concatenate(
            [
                jnp.concatenate(pieces, axis=1)
                for re, im in each[:2]
                for pieces in ((re, im), (-im, re))
            ],
            axis=0,
        )
        both = dot_nt(left, right)
        write(e, both[: 3 * chans, : 2 * chans])
        write(e + 1, both[chans:, 2 * chans :])


def cross(spectra, bins, before=None):
    chans = sum(value.shape[2] for value in spectra)
    data = spectra if before is None else spectra + [before]
    return pl.pallas_call(
        functools.partial(cross_kernel, len(spectra)),
        out_shape=jax.ShapeDtypeStruct((bins // 2, 3 * chans, 2 * chans), F32),
        in_specs=[vmem_spec()] * len(data),
        out_specs=vmem_spec(),
        compiler_params=params(),
        cost_estimate=SHORT,
    )(*data)


U_BITS, V_BITS = (2, 4), (4, 2)


def partner(value, bits):
    count = lax.axis_size("range")
    return lax.ppermute(value, "range", [(i, i ^ bits[i & 1]) for i in range(count)])


def slot_of(core, x, y, z):
    return (4 * z + ((2 * y + (x ^ y)) ^ (3 * (z & 1)))) ^ (15 * core)


def parts_of(index):
    return index & 1, (index >> 1) & 1, (index >> 2) & 1, (index >> 3) & 3


def bin_of(index):
    core, x, y, z = parts_of(index)
    return core * 16 + slot_of(core, x, y, z)


def index_of(bin_id):
    core = bin_id >> 4
    path = (bin_id & 15) ^ (15 * core)
    z = path >> 2
    turned = (path & 3) ^ (3 * (z & 1))
    y = turned >> 1
    x = (turned & 1) ^ y
    return z * 8 + y * 4 + x * 2 + core


def uv_parts():
    core, x, y, z = parts_of(lax.axis_index("range"))
    return core, jnp.where(core == 0, x, y), jnp.where(core == 0, y, x), z


def uv_slot(core, u, v, z):
    return slot_of(core, jnp.where(core == 0, u, v), jnp.where(core == 0, v, u), z)


def packed(block):
    chans = block.shape[0]
    lower = iota((chans, chans), 0) >= iota((chans, chans), 1)
    swapped = pltpu.roll(block, chans, 1)
    mixed = jnp.where(lower, block[:, :chans], swapped[:, :chans])
    return jnp.concatenate([mixed[: chans // 2], mixed[chans // 2 :]], axis=1)


def sent_rows(keep_ref):
    return 5 * keep_ref.shape[1] // 6


def upper_rows(keep_ref, e):
    block = keep_ref.shape[1] // 3
    end = sent_rows(keep_ref) // 2 + block // 2
    return jnp.concatenate([packed(keep_ref[e, :block]), keep_ref[e, block:end]], axis=0)


def lower_rows(keep_ref, e):
    return keep_ref[e, sent_rows(keep_ref) // 2 + keep_ref.shape[1] // 6 :]


def first_kernel(keep_ref, a_ref, b_ref):
    core, u, v, z = uv_parts()
    for k in range(8):
        a_ref[k] = upper_rows(keep_ref, uv_slot(core, 1 - u, k // 4, k % 4))
        b_ref[k] = lower_rows(keep_ref, uv_slot(core, k // 4, 1 - v, k % 4))


def second_kernel(keep_ref, a1_ref, b1_ref, a_ref, b_ref):
    core, u, v, z = uv_parts()
    for k in range(4):
        e = uv_slot(core, u, 1 - v, k)
        a_ref[k] = upper_rows(keep_ref, e) + a1_ref[(1 - v) * 4 + k]
        e = uv_slot(core, 1 - u, v, k)
        b_ref[k] = lower_rows(keep_ref, e) + b1_ref[(1 - u) * 4 + k]


def line_sum(keep_ref, a1_ref, b1_ref, a2_ref, b2_ref, flip):
    core, u, v, z = uv_parts()
    z = z ^ flip
    e = uv_slot(core, u, v, z)
    upper = upper_rows(keep_ref, e) + a1_ref[v * 4 + z] + a2_ref[z]
    lower = lower_rows(keep_ref, e) + b1_ref[u * 4 + z] + b2_ref[z]
    return upper, lower


FLIPS = (2, 3, 1)


def line_kernel(*refs):
    half = sent_rows(refs[0]) // 2
    for flip, out_ref in zip(FLIPS, refs[5:]):
        upper, lower = line_sum(*refs[:5], flip)
        out_ref[:half] = upper
        out_ref[half:] = lower


def own_kernel(*refs):
    z1_ref, z2_ref, z3_ref, out_ref, packed_ref = refs[5:]
    half = sent_rows(refs[0]) // 2
    upper, lower = line_sum(*refs[:5], 0)
    upper = upper + z1_ref[:half] + (z2_ref[:half] + z3_ref[:half])
    out_ref[:half] = upper
    packed_ref[...] = upper[: packed_ref.shape[0]]
    out_ref[half:] = lower + z1_ref[half:] + (z2_ref[half:] + z3_ref[half:])


def summed(kernel, data, shapes):
    return pl.pallas_call(
        kernel,
        out_shape=[jax.ShapeDtypeStruct(shape, F32) for shape in shapes],
        in_specs=[vmem_spec()] * len(data),
        out_specs=[vmem_spec()] * len(shapes),
        compiler_params=params(),
    )(*data)


def bin_sums(keep):
    _, full, wide = keep.shape
    rows = 5 * full // 6
    half = rows // 2
    data = [keep]
    a, b = summed(first_kernel, data, [(8, half, wide)] * 2)
    data += [partner(a, U_BITS), partner(b, V_BITS)]
    a, b = summed(second_kernel, data, [(4, half, wide)] * 2)
    data += [partner(a, V_BITS), partner(b, U_BITS)]
    sends = summed(line_kernel, data, [(rows, wide)] * 3)
    data += [partner(value, (8 * flip, 8 * flip)) for flip, value in zip(FLIPS, sends)]
    own, packed = summed(own_kernel, data, [(rows, wide), (rows // 5, wide)])
    bit = 32
    while bit < lax.axis_size("range"):
        own = own + partner(own, (bit, bit))
        packed = packed + partner(packed, (bit, bit))
        bit *= 2
    return own, packed


def from_bin(value, offset):
    count = lax.axis_size("range")
    pairs = []
    for i in range(count):
        target = index_of((bin_of(i) - offset) % 32) | (i & ~31)
        pairs.append((i, target))
    return lax.ppermute(value, "range", pairs)


def turn(value):
    half = value.shape[1] // 2
    rolled = pltpu.roll(value, half, 1)
    return jnp.where(iota(value.shape, 1) < half, -rolled, rolled)


def embed(value):
    return jnp.concatenate([value, turn(value)], axis=0)


def mul(a, b):
    return jnp.dot(a, embed(b), precision=lax.Precision.HIGHEST, preferred_element_type=F32)


def mul_conj(a, b):
    half = a.shape[1] // 2
    stacked = jnp.concatenate([a, -turn(a)], axis=0)
    both = dot_nt(stacked, b, lax.Precision.HIGHEST)
    rows = a.shape[0]
    return jnp.concatenate([both[:rows], both[rows:]], axis=1)


def conj_mul(a, b):
    half = a.shape[1] // 2
    both = lax.dot_general(
        a, b, (((0,), (0,)), ((), ())),
        precision=lax.Precision.HIGHEST, preferred_element_type=F32,
    )
    return both[:half] - turn(both[half:])


def reciprocal(x):
    value = pl.reciprocal(x, approx=True)
    for _ in range(2):
        value = value * (2.0 - x * value)
    return value


def pivot_inverse(p):
    def times(x, y):
        return x[0] * y[0] - x[1] * y[1], x[0] * y[1] + x[1] * y[0]

    def conj(x):
        return x[0], -x[1]

    def plus(x, y):
        return x[0] + y[0], x[1] + y[1]

    def scaled(x, s):
        return x[0] * s, x[1] * s

    def square(x):
        return x[0] * x[0] + x[1] * x[1]

    def two(a, b, d):
        inv = reciprocal(a * d - square(b))
        return d * inv, scaled(b, -inv), a * inv

    a, d = p[0][0], p[1][1]
    b = p[0][1]
    ea, eb, ed = two(a, b, d)
    f = [[p[0][2], p[0][3]], [p[1][2], p[1][3]]]
    w = [
        [plus(scaled(f[0][j], ea), times(eb, f[1][j])) for j in range(2)],
        [plus(times(conj(eb), f[0][j]), scaled(f[1][j], ed)) for j in range(2)],
    ]

    def inner(i, j):
        return plus(times(conj(f[0][i]), w[0][j]), times(conj(f[1][i]), w[1][j]))

    ha = p[2][2] - inner(0, 0)[0]
    hd = p[3][3] - inner(1, 1)[0]
    cross = inner(0, 1)
    hb = (p[2][3][0] - cross[0], p[2][3][1] - cross[1])
    ga, gb, gd = two(ha, hb, hd)
    v = [
        [
            plus(scaled(w[i][0], ga), times(w[i][1], conj(gb))),
            plus(times(w[i][0], gb), scaled(w[i][1], gd)),
        ]
        for i in range(2)
    ]
    top = [
        [plus(times(v[i][0], conj(w[j][0])), times(v[i][1], conj(w[j][1]))) for j in range(2)]
        for i in range(2)
    ]
    zero = None
    out = [[None] * 4 for _ in range(4)]
    out[0][0] = (ea + top[0][0][0], zero)
    out[1][1] = (ed + top[1][1][0], zero)
    out[0][1] = plus(eb, top[0][1])
    out[2][2], out[3][3], out[2][3] = (ga, zero), (gd, zero), gb
    for i in range(2):
        for j in range(2):
            out[i][2 + j] = (-v[i][j][0], -v[i][j][1])
    for i in range(4):
        for j in range(i):
            out[i][j] = conj(out[j][i])
    return out


def invert(matrix, w_ref, l_ref):
    chans, width = matrix.shape
    sub = 8
    tiles = [matrix[t * sub : (t + 1) * sub, :] for t in range(chans // sub)]
    lane = iota((sub, width), 1)
    low = jnp.bitwise_and(lane, chans - 1)
    first_half = lane < chans

    def spin(value):
        rolled = pltpu.roll(value, chans, 1)
        return jnp.where(first_half, -rolled, rolled)

    def column(value, k):
        return jnp.broadcast_to(value[:, k : k + 1], (sub, width))

    def combine(terms):
        while len(terms) > 1:
            terms = [
                terms[i] + terms[i + 1] if i + 1 < len(terms) else terms[i]
                for i in range(0, len(terms), 2)
            ]
        return terms[0]

    for k in range(0, chans, 4):
        t, r = divmod(k, sub)
        lines = [jnp.broadcast_to(tiles[t][r + i : r + i + 1, :], (sub, width)) for i in range(4)]
        pivot = [[None] * 4 for _ in range(4)]
        for i in range(4):
            pivot[i][i] = column(lines[i], k + i)
            for j in range(i + 1, 4):
                pivot[i][j] = column(lines[i], k + j), column(lines[i], chans + k + j)
        cleared = (low >= k) & (low < k + 4)
        unit = [
            jnp.where(cleared, jnp.where(lane == k + i, 1.0, 0.0), lines[i]) for i in range(4)
        ]
        spun = [spin(u) for u in unit]
        p = pivot_inverse(pivot)
        fresh_lines, fresh_spun = [], []
        for i in range(4):
            terms, other = [], []
            for j in range(4):
                re, im = p[i][j]
                terms.append(re * unit[j])
                other.append(re * spun[j])
                if im is not None:
                    terms.append(im * spun[j])
                    other.append(-(im * unit[j]))
            fresh_lines.append(combine(terms))
            fresh_spun.append(combine(other))
            w_ref[k + i : k + i + 1, :] = fresh_lines[i][:1]
            l_ref[k + i : k + i + 1, :] = unit[i][:1]
        for s in range(t if r == 0 else t + 1, len(tiles)):
            tile = tiles[s]
            terms = []
            for i in range(4):
                terms.append(column(tile, k + i) * fresh_lines[i])
                terms.append(column(tile, chans + k + i) * fresh_spun[i])
            tiles[s] = jnp.where(cleared, 0.0, tile) - combine(terms)
    shape = (chans, width)
    done = jnp.bitwise_and(iota(shape, 1), chans - 1) < (iota(shape, 0) // 4 + 1) * 4
    return conj_mul(jnp.where(done, w_ref[...], 0.0), jnp.where(done, l_ref[...], 0.0))


def unpacked(ref, scale):
    half, wide = ref.shape[0], ref.shape[1]
    piece = ref[...] * scale
    swapped = pltpu.roll(piece, wide // 2, 1)
    return jnp.concatenate([piece, swapped], axis=0)[:, : wide // 2]


def hermitian(mixed, across):
    i, j = iota(mixed.shape, 0), iota(mixed.shape, 1)
    real_part = jnp.where(i >= j, mixed, across)
    imag_part = jnp.where(i < j, mixed, jnp.where(i > j, -across, 0.0))
    return jnp.concatenate([real_part, imag_part], axis=1)


def middle_kernel(total, packed_ref, steer_ref, inv_ref, t_ref, w_ref, l_ref):
    chans = inv_ref.shape[0]
    mixed = unpacked(packed_ref, F32(1.0 / total))
    twice = jnp.concatenate([mixed, mixed], axis=1)
    across = jnp.concatenate([twice, twice], axis=0).T[:chans, :chans]
    inverse = invert(hermitian(mixed, across), w_ref, l_ref)
    inv_ref[...] = inverse
    t_ref[...] = mul(steer_ref[...], inverse)


def outer_kernel(total, own_ref, left_ref, right_ref, steer_ref, inv_ref, t_ref, out_ref,
                 work, keep, w_ref, l_ref):
    chans = inv_ref.shape[0]
    scale = F32(1.0 / total)
    half = chans // 2
    m_left = unpacked(left_ref.at[:half], scale)
    m_right = unpacked(right_ref, scale)
    ml = left_ref[half : half + chans] * scale
    rl = left_ref[half + chans :] * scale
    rm = own_ref[half : half + chans] * scale
    pair = jnp.concatenate([m_left, m_right], axis=1)
    square = jnp.concatenate([pair, pair], axis=0).T
    inv_mid = inv_ref[...]
    t = t_ref[...]
    h = mul(inv_mid, ml)
    g = mul(rm, inv_mid)
    work[...] = hermitian(m_left, square[:chans, :chans]) - conj_mul(ml, h)
    s_rl = rl - mul(rm, h)
    s_rr = hermitian(m_right, square[chans:, :chans]) - mul_conj(g, rm)
    rhs_left = -mul(t, ml)
    rhs_right = -mul_conj(t, rm)
    keep[0] = s_rl
    keep[1] = s_rr
    keep[2] = h
    keep[3] = g
    keep[4, 0:BEAMS] = rhs_left
    keep[4, BEAMS : 2 * BEAMS] = rhs_right

    @pl.loop(0, 2)
    def _(stage):
        work[...] = invert(work[...], w_ref, l_ref)

        @pl.when(stage == 0)
        def _():
            inverse = work[...]
            s_rl = keep[0]
            both = mul(jnp.concatenate([s_rl, keep[4, 0:BEAMS]], axis=0), inverse)
            k, y_left = both[:chans], both[chans:]
            work[...] = keep[1] - mul_conj(k, s_rl)
            keep[0] = k
            keep[4, BEAMS : 2 * BEAMS] = keep[4, BEAMS : 2 * BEAMS] - mul_conj(y_left, s_rl)
            keep[4, 0:BEAMS] = y_left
            keep[4, 2 * BEAMS : 3 * BEAMS] = t_ref[...] - mul_conj(y_left, keep[2])
            keep[3] = keep[3] - mul_conj(k, keep[2])

        @pl.when(stage == 1)
        def _():
            y_right = mul(keep[4, BEAMS : 2 * BEAMS], work[...])
            y_left = keep[4, 0:BEAMS] - mul(y_right, keep[0])
            y_mid = keep[4, 2 * BEAMS : 3 * BEAMS] - mul(y_right, keep[3])
            quad = jnp.sum(steer_ref[...] * y_mid, axis=1, keepdims=True)
            y = jnp.concatenate([y_left, y_mid, y_right], axis=1) / jnp.sqrt(quad)
            real_lane = lax.rem(iota(y.shape, 1), 2 * chans) < chans
            mine = jnp.where(real_lane, y, -y).astype(BF16)
            for c in range(out_ref.shape[0]):
                out_ref[c] = mine


def steering(chans):
    index = np.arange(chans)
    sines = -0.8 + 1.6 * np.arange(BEAMS) / (BEAMS - 1)
    angle = math.pi * sines[:, None] * index[None, :]
    return np.concatenate([np.cos(angle), -np.sin(angle)], axis=1).astype(np.float32)


def solve_middle(packed, steer, total):
    half, wide = packed.shape
    return pl.pallas_call(
        functools.partial(middle_kernel, total),
        out_shape=[
            jax.ShapeDtypeStruct((2 * half, wide), F32),
            jax.ShapeDtypeStruct((BEAMS, wide), F32),
        ],
        in_specs=[vmem_spec()] * 2,
        out_specs=[vmem_spec()] * 2,
        scratch_shapes=[pltpu.VMEM((2 * half, wide), F32)] * 2,
        compiler_params=params(),
    )(packed, steer)


def solve_outer(own, left, right, steer, inverse, t, total, copies):
    chans, wide = inverse.shape
    return pl.pallas_call(
        functools.partial(outer_kernel, total),
        out_shape=jax.ShapeDtypeStruct((copies, BEAMS, 3 * wide), BF16),
        in_specs=[vmem_spec()] * 6,
        out_specs=vmem_spec(),
        scratch_shapes=[
            pltpu.VMEM((chans, wide), F32), pltpu.VMEM((5, chans, wide), F32),
            pltpu.VMEM((chans, wide), F32), pltpu.VMEM((chans, wide), F32),
        ],
        compiler_params=params(),
    )(own, left, right, steer, inverse, t)


def beam_kernel(bin_ref, block_ref, beam_ref, owner_ref, s0_ref, upper_ref, lower_ref, w_ref,
                out_ref, both_ref, rows_ref, seen_ref):
    bins, wide, gates = s0_ref.shape
    devices = seen_ref.shape[0]
    count = bin_ref.shape[0]
    rows_ref[...] = jnp.zeros_like(rows_ref)

    @pl.loop(0, devices)
    def _(i):
        seen_ref[i] = 0

    w = w_ref[...].astype(F32).reshape(bins * BEAMS, 3 * wide)
    for k in range(3):
        lanes = slice(k * wide, (k + 1) * wide)
        part = w[:, lanes]
        both_ref[:, 0:BEAMS, lanes] = part.reshape(bins, BEAMS, wide)
        both_ref[:, BEAMS:, lanes] = turn(part).reshape(bins, BEAMS, wide)

    def detection(j, carry):
        bin_id = bin_ref[j]
        beam_id = beam_ref[j]
        owner = owner_ref[j]
        rank = seen_ref[owner]
        seen_ref[owner] = rank + 1
        left = both_ref[index_of(bin_id)].astype(BF16)
        bands = [lax.rem(bin_id + bins - 1 + k, bins) for k in range(3)]
        first = block_ref[j] == 0
        pieces = []
        for b in bands:
            later = [upper_ref[b, 0], lower_ref[b, 0], upper_ref[b, 1], lower_ref[b, 1]]
            pieces.append(jnp.where(first, s0_ref[b], jnp.concatenate(later, axis=0)))
        window = jnp.concatenate(pieces, axis=0)
        both = dot(left, window)
        line = jnp.concatenate([both[:BEAMS], both[BEAMS:]], axis=1)
        chosen = jnp.where(iota(line.shape, 0) == beam_id, line, 0.0)
        row = owner * CAP + rank
        rows_ref[pl.ds(row, 1), :] = jnp.sum(chosen, axis=0, keepdims=True)
        return carry

    lax.fori_loop(0, count, detection, 0, unroll=32)
    out_ref[...] = rows_ref[...].astype(BF16)


def beam_rows(det_bin, det_block, det_beam, owners, s0, s1, weight, devices):
    bins, wide, gates = s0.shape
    return pl.pallas_call(
        beam_kernel,
        out_shape=jax.ShapeDtypeStruct((devices * CAP, 2 * gates), BF16),
        in_specs=[smem_spec()] * 4 + [vmem_spec()] * 4,
        out_specs=vmem_spec(),
        scratch_shapes=[
            pltpu.VMEM((bins, 2 * BEAMS, 3 * wide), F32),
            pltpu.VMEM((devices * CAP, 2 * gates), F32),
            pltpu.SMEM((devices,), jnp.int32),
        ],
        compiler_params=params(),
    )(det_bin, det_block, det_beam, owners, s0, *s1, weight)


def on_device(raw, replica, det_bin, det_block, det_beam, det_owner):
    devices = lax.axis_size("range")
    _, chans, pulses, gates = raw.shape
    bins = pulses
    flat = raw.reshape(2, chans * pulses, gates)
    before = [(source, source - 1) for source in range(1, devices)]
    *slices, mark = first_gates(flat)
    halos = [lax.ppermute(value, "range", before) for value in slices]
    table = doppler_matrix(pulses, 8)
    s0, local, matrix, *sent = spectra_first(flat, replica, table, pulses, mark)
    beside0 = [partner(value, (1, 1)) for value in sent]
    sums = cross([s0], bins)
    sums = cross(beside0, bins, sums)
    s1, beside1 = [], []
    for part, halo in enumerate(halos):
        value, send = spectra_last(part, local, halo, matrix, table, pulses, sums)
        s1.append(value)
        beside1.append(partner(send, (1, 1)))
    sums = cross(s1, bins, sums)
    sums = cross(beside1, bins, sums)
    own, packed = bin_sums(sums)
    total = gates * devices
    steer = steering(chans)
    left = from_bin(own, -1)
    right = from_bin(packed, 1)
    inverse, t = solve_middle(packed, steer, total)
    mine = solve_outer(own, left, right, steer, inverse, t, total, bins)
    groups = [list(range(first, first + bins)) for first in range(0, devices, bins)]
    weight = lax.all_to_all(
        mine, "range", split_axis=0, concat_axis=0, tiled=True,
        axis_index_groups=groups if len(groups) > 1 else None,
    )
    outgoing = beam_rows(
        det_bin, det_block, det_beam, det_owner[:, 0],
        s0.reshape(bins, 2 * chans, BLOCK), s1, weight, devices,
    )
    incoming = lax.all_to_all(
        outgoing.reshape(devices, CAP, 2 * BLOCK), "range", split_axis=0, concat_axis=0, tiled=True
    )
    return incoming.astype(F32).reshape(devices * CAP, 2 * BLOCK)


def solution(mesh):
    in_specs = (
        P(None, None, None, "range"),
        P(),
        P("range"),
        P("range"),
        P("range"),
        P("range", None),
    )
    out_specs = P("range", None)
    return jax.shard_map(
        on_device, mesh=mesh, in_specs=in_specs, out_specs=out_specs, check_vma=False
    )
```

profile of v0, /device:TPU:0, one launch (start us, length us, event | category | flops | bytes accessed | tf_op | source)
XLA Modules:
  0.0 95.4 jit_solution(18386360372380763121)
XLA Ops:
  0.0 2.4 %shard_map.82 = (bf16[2,1024,128]{2,1,0:T(8,128)(2,1)}, bf16[2,1024,128]{2,1,0:T(8,128)(2,1)}, f32[8,128]{1,0:T(8,128)}) custom-call(bf16[2,2048,256]{2,1,0:T(8,128)(2,1)} %bitcast.3), custom_call_target="tpu_custom_call" | custom-call | tf_op jit(solution)/shard_map/pallas_call | solution.py:78
  2.4 1.3 %collective-permute-start.3 = (bf16[2,1024,128]{2,1,0:T(8,128)(2,1)}, bf16[2,1024,128]{2,1,0:T(8,128)(2,1)S(1)}, u32[]{:S(2)}, u32[]{:S(2)}) collective-permute-start(bf16[2,1024,128]{2,1,0:T(8,128)(2,1)} %get-tuple-element.36), channel_id=1, source_target_pairs={{1,0},{2,1},{3,2},{4,3},{5,4},{6,5},{7,6},{8,7},{9,8},{10,9},{11,1... | collective-permute-start | bytes 1572872 | tf_op jit(solution)/shard_map/ppermute | solution.py:779
  3.7 1.3 %collective-permute-start = (bf16[2,1024,128]{2,1,0:T(8,128)(2,1)}, bf16[2,1024,128]{2,1,0:T(8,128)(2,1)S(1)}, u32[]{:S(2)}, u32[]{:S(2)}) collective-permute-start(bf16[2,1024,128]{2,1,0:T(8,128)(2,1)} %get-tuple-element.31), channel_id=1, source_target_pairs={{1,0},{2,1},{3,2},{4,3},{5,4},{6,5},{7,6},{8,7},{9,8},{10,9},{11,1... | collective-permute-start | bytes 1572872 | tf_op jit(solution)/shard_map/ppermute | solution.py:779
  5.0 1.6 %copy-done = bf16[2,64,32,256]{3,2,1,0:T(8,128)(2,1)S(1)} copy-done((bf16[2,64,32,256]{3,2,1,0:T(8,128)(2,1)S(1)}, bf16[2,64,32,256]{3,2,1,0:T(8,128)(2,1)}, u32[]{:S(2)}) %copy-start) | copy-done | bytes 2097176
  7.3 4.1 %shard_map.83 = (bf16[32,2,64,128]{3,2,1,0:T(8,128)(2,1)S(1)}, f32[2048,256]{1,0:T(8,128)S(1)}, bf16[2,256,256]{2,1,0:T(8,128)(2,1)S(1)}, bf16[18,2,32,128]{3,2,...) custom-call(bf16[2,2048,256]{2,1,0:T(8,128)(2,1)S(1)} %bitcast.4, bf16[2,128]{1,0:T(2,128)(2,1)S(1)} %copy-done.4, ...), custom_call_target="tpu_custom_call" | custom-call | flops 1 | bytes 1 | tf_op jit(solution)/shard_map/pallas_call | solution.py:199
  11.4 1.8 %collective-permute-start.1 = (bf16[18,2,32,128]{3,2,1,0:T(8,128)(2,1)S(1)}, bf16[18,2,32,128]{3,2,1,0:T(8,128)(2,1)S(1)}, u32[]{:S(2)}, u32[]{:S(2)}) collective-permute-start(bf16[18,2,32,128]{3,2,1,0:T(8,128)(2,1)S(1)} %get-tuple-element.33), channel_id=1, source_target_pairs={{0,1},{1,0},{2,3},{3,2},{4,5},{5,4},{6,7},{7,6},{8,9},{9,8},{10,11... | collective-permute-start | bytes 884744 | tf_op jit(solution)/shard_map/ppermute | solution.py:288
  14.9 1.1 %shard_map.85._.refs_2_ = f32[16,192,128]{2,1,0:T(8,128)S(1)} custom-call(bf16[18,2,32,128]{3,2,1,0:T(8,128)(2,1)S(1)} %collective-permute-done.1.refs_0_, bf16[18,2,32,128]{3,2,1,0:T(8,128)(2,1)S(1)} %collective-permute-done.2.refs_1_, f32[16,192,128]{2,1,0:T(8,128)S(1)} %shard_map.84.refs_2_), custom_call_target="tpu_custom_call" | custom-call | flops 1 | bytes 1 | tf_op jit(solution)/shard_map/pallas_call | solution.py:273
  17.9 3.0 %collective-permute-start.4 = (bf16[18,2,32,128]{3,2,1,0:T(8,128)(2,1)S(1)}, bf16[18,2,32,128]{3,2,1,0:T(8,128)(2,1)S(1)}, u32[]{:S(2)}, u32[]{:S(2)}) collective-permute-start(bf16[18,2,32,128]{3,2,1,0:T(8,128)(2,1)S(1)} %get-tuple-element.38), channel_id=1, source_target_pairs={{0,1},{1,0},{2,3},{3,2},{4,5},{5,4},{6,7},{7,6},{8,9},{9,8},{10,11... | collective-permute-start | bytes 884744 | tf_op jit(solution)/shard_map/ppermute | solution.py:288
  22.1 1.1 %shard_map.89.keep_ref.refs_0_ = f32[16,192,128]{2,1,0:T(8,128)S(1)} custom-call(bf16[18,2,32,128]{3,2,1,0:T(8,128)(2,1)S(1)} %collective-permute-done.4.refs_0_, bf16[18,2,32,128]{3,2,1,0:T(8,128)(2,1)S(1)} %collective-permute-done.5.refs_1_, f32[16,192,128]{2,1,0:T(8,128)S(1)} %shard_map.88.refs_2_), custom_call_target="tpu_custom_call" | custom-call | flops 1 | bytes 1 | tf_op jit(solution)/shard_map/pallas_call | solution.py:273
  23.4 2.4 %collective-permute-start.6 = (f32[8,80,128]{2,1,0:T(8,128)S(1)}, f32[8,80,128]{2,1,0:T(8,128)S(1)}, u32[]{:S(2)}, u32[]{:S(2)}) collective-permute-start(f32[8,80,128]{2,1,0:T(8,128)S(1)} %get-tuple-element.40), channel_id=1, source_target_pairs={{0,2},{1,5},{2,0},{3,7},{4,6},{5,1},{6,4},{7,3},{8,10},{9,13},{10,... | collective-permute-start | bytes 983048 | tf_op jit(solution)/shard_map/ppermute | solution.py:288
  25.8 2.4 %collective-permute-start.7 = (f32[8,80,128]{2,1,0:T(8,128)S(1)}, f32[8,80,128]{2,1,0:T(8,128)S(1)}, u32[]{:S(2)}, u32[]{:S(2)}) collective-permute-start(f32[8,80,128]{2,1,0:T(8,128)S(1)} %get-tuple-element.41), channel_id=1, source_target_pairs={{0,4},{1,3},{2,6},{3,1},{4,0},{5,7},{6,2},{7,5},{8,12},{9,11},{10,... | collective-permute-start | bytes 983048 | tf_op jit(solution)/shard_map/ppermute | solution.py:288
  28.2 4.2 %collective-permute-done.6.a1_ref.refs_1_ = f32[8,80,128]{2,1,0:T(8,128)S(1)} collective-permute-done((f32[8,80,128]{2,1,0:T(8,128)S(1)}, f32[8,80,128]{2,1,0:T(8,128)S(1)}, u32[]{:S(2)}, u32[]{:S(2)}) %collective-permute-start.6) | collective-permute-done | bytes 327712 | tf_op jit(solution)/shard_map/ppermute | solution.py:288
  33.6 3.2 %collective-permute-start.8 = (f32[4,80,128]{2,1,0:T(8,128)S(1)}, f32[4,80,128]{2,1,0:T(8,128)S(1)}, u32[]{:S(2)}, u32[]{:S(2)}) collective-permute-start(f32[4,80,128]{2,1,0:T(8,128)S(1)} %get-tuple-element.42), channel_id=1, source_target_pairs={{0,4},{1,3},{2,6},{3,1},{4,0},{5,7},{6,2},{7,5},{8,12},{9,11},{10,... | collective-permute-start | bytes 491528 | tf_op jit(solution)/shard_map/ppermute | solution.py:288
  36.8 1.7 %collective-permute-start.9 = (f32[4,80,128]{2,1,0:T(8,128)S(1)}, f32[4,80,128]{2,1,0:T(8,128)S(1)}, u32[]{:S(2)}, u32[]{:S(2)}) collective-permute-start(f32[4,80,128]{2,1,0:T(8,128)S(1)} %get-tuple-element.43), channel_id=1, source_target_pairs={{0,2},{1,5},{2,0},{3,7},{4,6},{5,1},{6,4},{7,3},{8,10},{9,13},{10,... | collective-permute-start | bytes 491528 | tf_op jit(solution)/shard_map/ppermute | solution.py:288
  38.5 2.7 %collective-permute-done.8.refs_3_ = f32[4,80,128]{2,1,0:T(8,128)S(1)} collective-permute-done((f32[4,80,128]{2,1,0:T(8,128)S(1)}, f32[4,80,128]{2,1,0:T(8,128)S(1)}, u32[]{:S(2)}, u32[]{:S(2)}) %collective-permute-start.8) | collective-permute-done | bytes 163872 | tf_op jit(solution)/shard_map/ppermute | solution.py:288
  42.3 2.7 %collective-permute-start.10 = (f32[160,128]{1,0:T(8,128)S(1)}, f32[160,128]{1,0:T(8,128)S(1)}, u32[]{:S(2)}, u32[]{:S(2)}) collective-permute-start(f32[160,128]{1,0:T(8,128)S(1)} %get-tuple-element.44), channel_id=1, source_target_pairs={{0,16},{1,17},{2,18},{3,19},{4,20},{5,21},{6,22},{7,23},{8,24},{9,... | collective-permute-start | bytes 245768 | tf_op jit(solution)/shard_map/ppermute | solution.py:288
  44.9 1.3 %collective-permute-start.11 = (f32[160,128]{1,0:T(8,128)S(1)}, f32[160,128]{1,0:T(8,128)S(1)}, u32[]{:S(2)}, u32[]{:S(2)}) collective-permute-start(f32[160,128]{1,0:T(8,128)S(1)} %get-tuple-element.45), channel_id=1, source_target_pairs={{0,24},{1,25},{2,26},{3,27},{4,28},{5,29},{6,30},{7,31},{8,16},{9,... | collective-permute-start | bytes 245768 | tf_op jit(solution)/shard_map/ppermute | solution.py:288
  46.4 5.5 %collective-permute-done.10.refs_5_ = f32[160,128]{1,0:T(8,128)S(1)} collective-permute-done((f32[160,128]{1,0:T(8,128)S(1)}, f32[160,128]{1,0:T(8,128)S(1)}, u32[]{:S(2)}, u32[]{:S(2)}) %collective-permute-start.10) | collective-permute-done | bytes 81952 | tf_op jit(solution)/shard_map/ppermute | solution.py:288
  52.6 1.1 %collective-permute-start.13 = (f32[160,128]{1,0:T(8,128)S(1)}, f32[160,128]{1,0:T(8,128)S(1)}, u32[]{:S(2)}, u32[]{:S(2)}) collective-permute-start(f32[160,128]{1,0:T(8,128)S(1)} %get-tuple-element.47.own_ref), channel_id=1, source_target_pairs={{0,2},{1,0},{2,6},{3,1},{4,12},{5,7},{6,4},{7,3},{8,16},{9,11},{10... | collective-permute-start | bytes 245768 | tf_op jit(solution)/shard_map/ppermute | solution.py:427
  53.8 5.0 %shard_map.94 = (f32[64,128]{1,0:T(8,128)S(1)}, f32[8,128]{1,0:T(8,128)S(1)}) custom-call(f32[32,128]{1,0:T(8,128)S(1)} %get-tuple-element.48.packed_ref, f32[8,128]{1,0:T(8,128)S(1)} %copy-done.2), custom_call_target="tpu_custom_call" | custom-call | tf_op jit(solution)/shard_map/pallas_call | solution.py:685
  58.7 10.8 %shard_map.95 = bf16[32,8,384]{2,1,0:T(8,128)(2,1)S(1)} custom-call(f32[160,128]{1,0:T(8,128)S(1)} %get-tuple-element.47.own_ref, f32[160,128]{1,0:T(8,128)S(1)} %collective-permute-done.13.left_ref, f32[32,128]{1,0:T(8,128)S(1)} %collective-permute-done.14.right_ref, f32[8,128]{1,0:T(8,128)S(1)} %copy-done.2, f32[64,128]{1,0:T(8,128)S(1)} %get-tuple-element.49.inv_ref, ...), custom_call_target="tpu_custom_call" | custom-call | tf_op jit(solution)/shard_map/pallas_call | solution.py:700
  69.6 13.4 %all_to_all.10.w_ref = bf16[32,8,384]{2,1,0:T(8,128)(2,1)S(1)} all-to-all(bf16[32,8,384]{2,1,0:T(8,128)(2,1)S(1)} %shard_map.95), channel_id=1, replica_groups=mesh['range'=32] {'range'}, dimensions={0} | all-to-all | bytes 393216 | tf_op jit(solution)/shard_map/all_to_all | solution.py:800
  83.0 2.0 %shard_map.96 = bf16[64,256]{1,0:T(8,128)(2,1)S(1)} custom-call(s32[32]{0:T(128)S(1)} %copy-done.5, s32[32]{0:T(128)S(1)} %copy-done.6, s32[32]{0:T(128)S(1)} %copy-done.7, s32[32]{0:T(128)S(1)} %bitcast.6, bf16[32,128,128]{2,1,0:T(8,128)(2,1)S(1)} %bitcast.5, bf16[32,2,32,128]{3,2,1,0:T(8,128)(2,1)S(1)} %get-tuple-element.35.refs_0_.upper_ref, ...), custom_call_target="tpu_custom_call" | custom-call | tf_op jit(solution)/shard_map/pallas_call | solution.py:758
  85.0 9.8 %all_to_all.11 = bf16[32,2,256]{2,1,0:T(2,128)(2,1)S(1)} all-to-all(bf16[32,2,256]{2,1,0:T(2,128)(2,1)S(1)} %reshape.17), channel_id=1, replica_groups=mesh['range'=32] {'range'}, dimensions={0} | all-to-all | bytes 65536 | tf_op jit(solution)/shard_map/all_to_all | solution.py:808
  (43 shorter events, 9.3 us)
Async XLA Ops:
  0.0 5.0 %copy-start.1 = (bf16[512,512]{1,0:T(8,128)(2,1)S(1)}, bf16[512,512]{1,0:T(8,128)(2,1)}, u32[]{:S(2)}) copy-start(bf16[512,512]{1,0:T(8,128)(2,1)} %constant.4.clone.dft_ref) | copy-start | bytes 1572868
  0.0 5.0 %copy-start.4 = (bf16[2,128]{1,0:T(2,128)(2,1)S(1)}, bf16[2,128]{1,0:T(2,128)(2,1)}, u32[]{:S(2)}) copy-start(bf16[2,128]{1,0:T(2,128)(2,1)} %rep_ref.1) | copy-start | bytes 1540
  2.4 13.6 %collective-permute-start.3 = (bf16[2,1024,128]{2,1,0:T(8,128)(2,1)}, bf16[2,1024,128]{2,1,0:T(8,128)(2,1)S(1)}, u32[]{:S(2)}, u32[]{:S(2)}) collective-permute-start(bf16[2,1024,128]{2,1,0:T(8,128)(2,1)} %get-tuple-element.36), channel_id=1, source_target_pairs={{1,0},{2,1},{3,2},{4,3},{5,4},{6,5},{7,6},{8,7},{9,8},{10,9},{11,1... | collective-permute-start | bytes 1572872 | tf_op jit(solution)/shard_map/ppermute | solution.py:779
  3.7 13.4 %collective-permute-start = (bf16[2,1024,128]{2,1,0:T(8,128)(2,1)}, bf16[2,1024,128]{2,1,0:T(8,128)(2,1)S(1)}, u32[]{:S(2)}, u32[]{:S(2)}) collective-permute-start(bf16[2,1024,128]{2,1,0:T(8,128)(2,1)} %get-tuple-element.31), channel_id=1, source_target_pairs={{1,0},{2,1},{3,2},{4,3},{5,4},{6,5},{7,6},{8,7},{9,8},{10,9},{11,1... | collective-permute-start | bytes 1572872 | tf_op jit(solution)/shard_map/ppermute | solution.py:779
  5.0 1.6 %copy-start = (bf16[2,64,32,256]{3,2,1,0:T(8,128)(2,1)S(1)}, bf16[2,64,32,256]{3,2,1,0:T(8,128)(2,1)}, u32[]{:S(2)}) copy-start(bf16[2,64,32,256]{3,2,1,0:T(8,128)(2,1)} %param.8) | copy-start | bytes 6291460
  6.6 0.7 copy-start.3
  11.4 3.0 %collective-permute-start.1 = (bf16[18,2,32,128]{3,2,1,0:T(8,128)(2,1)S(1)}, bf16[18,2,32,128]{3,2,1,0:T(8,128)(2,1)S(1)}, u32[]{:S(2)}, u32[]{:S(2)}) collective-permute-start(bf16[18,2,32,128]{3,2,1,0:T(8,128)(2,1)S(1)} %get-tuple-element.33), channel_id=1, source_target_pairs={{0,1},{1,0},{2,3},{3,2},{4,5},{5,4},{6,7},{7,6},{8,9},{9,8},{10,11... | collective-permute-start | bytes 884744 | tf_op jit(solution)/shard_map/ppermute | solution.py:288
  13.3 1.6 %collective-permute-start.2 = (bf16[18,2,32,128]{3,2,1,0:T(8,128)(2,1)S(1)}, bf16[18,2,32,128]{3,2,1,0:T(8,128)(2,1)S(1)}, u32[]{:S(2)}, u32[]{:S(2)}) collective-permute-start(bf16[18,2,32,128]{3,2,1,0:T(8,128)(2,1)S(1)} %get-tuple-element.34), channel_id=1, source_target_pairs={{0,1},{1,0},{2,3},{3,2},{4,5},{5,4},{6,7},{7,6},{8,9},{9,8},{10,11... | collective-permute-start | bytes 884744 | tf_op jit(solution)/shard_map/ppermute | solution.py:288
  16.7 5.2 %collective-permute-start.5 = (bf16[18,2,32,128]{3,2,1,0:T(8,128)(2,1)S(1)}, bf16[18,2,32,128]{3,2,1,0:T(8,128)(2,1)S(1)}, u32[]{:S(2)}, u32[]{:S(2)}) collective-permute-start(bf16[18,2,32,128]{3,2,1,0:T(8,128)(2,1)S(1)} %get-tuple-element.39), channel_id=1, source_target_pairs={{0,1},{1,0},{2,3},{3,2},{4,5},{5,4},{6,7},{7,6},{8,9},{9,8},{10,11... | collective-permute-start | bytes 884744 | tf_op jit(solution)/shard_map/ppermute | solution.py:288
  17.9 4.2 %collective-permute-start.4 = (bf16[18,2,32,128]{3,2,1,0:T(8,128)(2,1)S(1)}, bf16[18,2,32,128]{3,2,1,0:T(8,128)(2,1)S(1)}, u32[]{:S(2)}, u32[]{:S(2)}) collective-permute-start(bf16[18,2,32,128]{3,2,1,0:T(8,128)(2,1)S(1)} %get-tuple-element.38), channel_id=1, source_target_pairs={{0,1},{1,0},{2,3},{3,2},{4,5},{5,4},{6,7},{7,6},{8,9},{9,8},{10,11... | collective-permute-start | bytes 884744 | tf_op jit(solution)/shard_map/ppermute | solution.py:288
  23.4 9.1 %collective-permute-start.6 = (f32[8,80,128]{2,1,0:T(8,128)S(1)}, f32[8,80,128]{2,1,0:T(8,128)S(1)}, u32[]{:S(2)}, u32[]{:S(2)}) collective-permute-start(f32[8,80,128]{2,1,0:T(8,128)S(1)} %get-tuple-element.40), channel_id=1, source_target_pairs={{0,2},{1,5},{2,0},{3,7},{4,6},{5,1},{6,4},{7,3},{8,10},{9,13},{10,... | collective-permute-start | bytes 983048 | tf_op jit(solution)/shard_map/ppermute | solution.py:288
  25.8 7.7 %collective-permute-start.7 = (f32[8,80,128]{2,1,0:T(8,128)S(1)}, f32[8,80,128]{2,1,0:T(8,128)S(1)}, u32[]{:S(2)}, u32[]{:S(2)}) collective-permute-start(f32[8,80,128]{2,1,0:T(8,128)S(1)} %get-tuple-element.41), channel_id=1, source_target_pairs={{0,4},{1,3},{2,6},{3,1},{4,0},{5,7},{6,2},{7,5},{8,12},{9,11},{10,... | collective-permute-start | bytes 983048 | tf_op jit(solution)/shard_map/ppermute | solution.py:288
  33.6 7.6 %collective-permute-start.8 = (f32[4,80,128]{2,1,0:T(8,128)S(1)}, f32[4,80,128]{2,1,0:T(8,128)S(1)}, u32[]{:S(2)}, u32[]{:S(2)}) collective-permute-start(f32[4,80,128]{2,1,0:T(8,128)S(1)} %get-tuple-element.42), channel_id=1, source_target_pairs={{0,4},{1,3},{2,6},{3,1},{4,0},{5,7},{6,2},{7,5},{8,12},{9,11},{10,... | collective-permute-start | bytes 491528 | tf_op jit(solution)/shard_map/ppermute | solution.py:288
  36.8 5.3 %collective-permute-start.9 = (f32[4,80,128]{2,1,0:T(8,128)S(1)}, f32[4,80,128]{2,1,0:T(8,128)S(1)}, u32[]{:S(2)}, u32[]{:S(2)}) collective-permute-start(f32[4,80,128]{2,1,0:T(8,128)S(1)} %get-tuple-element.43), channel_id=1, source_target_pairs={{0,2},{1,5},{2,0},{3,7},{4,6},{5,1},{6,4},{7,3},{8,10},{9,13},{10,... | collective-permute-start | bytes 491528 | tf_op jit(solution)/shard_map/ppermute | solution.py:288
  42.3 11.5 %copy-start.2 = (f32[8,128]{1,0:T(8,128)S(1)}, f32[8,128]{1,0:T(8,128)}, u32[]{:S(2)}) copy-start(f32[8,128]{1,0:T(8,128)} %constant.5.clone.steer_ref) | copy-start | bytes 12292
  42.3 9.6 %collective-permute-start.10 = (f32[160,128]{1,0:T(8,128)S(1)}, f32[160,128]{1,0:T(8,128)S(1)}, u32[]{:S(2)}, u32[]{:S(2)}) collective-permute-start(f32[160,128]{1,0:T(8,128)S(1)} %get-tuple-element.44), channel_id=1, source_target_pairs={{0,16},{1,17},{2,18},{3,19},{4,20},{5,21},{6,22},{7,23},{8,24},{9,... | collective-permute-start | bytes 245768 | tf_op jit(solution)/shard_map/ppermute | solution.py:288
  44.9 7.0 %collective-permute-start.11 = (f32[160,128]{1,0:T(8,128)S(1)}, f32[160,128]{1,0:T(8,128)S(1)}, u32[]{:S(2)}, u32[]{:S(2)}) collective-permute-start(f32[160,128]{1,0:T(8,128)S(1)} %get-tuple-element.45), channel_id=1, source_target_pairs={{0,24},{1,25},{2,26},{3,27},{4,28},{5,29},{6,30},{7,31},{8,16},{9,... | collective-permute-start | bytes 245768 | tf_op jit(solution)/shard_map/ppermute | solution.py:288
  46.3 36.7 %copy-start.5 = (s32[32]{0:T(128)S(1)}, s32[32]{0:T(128)}, u32[]{:S(2)}) copy-start(s32[32]{0:T(128)} %bin_ref.1) | copy-start | bytes 388
  46.3 36.7 %copy-start.6 = (s32[32]{0:T(128)S(1)}, s32[32]{0:T(128)}, u32[]{:S(2)}) copy-start(s32[32]{0:T(128)} %block_ref.1) | copy-start | bytes 388
  46.3 36.7 %copy-start.7 = (s32[32]{0:T(128)S(1)}, s32[32]{0:T(128)}, u32[]{:S(2)}) copy-start(s32[32]{0:T(128)} %beam_ref.1) | copy-start | bytes 388
  46.3 36.7 %copy-start.8 = (s32[32,1]{0,1:T(1,128)S(1)}, s32[32,1]{0,1:T(1,128)}, u32[]{:S(2)}) copy-start(s32[32,1]{0,1:T(1,128)} %param.13) | copy-start | bytes 388
  46.3 6.2 %collective-permute-start.12 = (f32[160,128]{1,0:T(8,128)S(1)}, f32[160,128]{1,0:T(8,128)S(1)}, u32[]{:S(2)}, u32[]{:S(2)}) collective-permute-start(f32[160,128]{1,0:T(8,128)S(1)} %get-tuple-element.46), channel_id=1, source_target_pairs={{0,8},{1,9},{2,10},{3,11},{4,12},{5,13},{6,14},{7,15},{8,0},{9,1},... | collective-permute-start | bytes 245768 | tf_op jit(solution)/shard_map/ppermute | solution.py:288
  52.6 6.1 %collective-permute-start.13 = (f32[160,128]{1,0:T(8,128)S(1)}, f32[160,128]{1,0:T(8,128)S(1)}, u32[]{:S(2)}, u32[]{:S(2)}) collective-permute-start(f32[160,128]{1,0:T(8,128)S(1)} %get-tuple-element.47.own_ref), channel_id=1, source_target_pairs={{0,2},{1,0},{2,6},{3,1},{4,12},{5,7},{6,4},{7,3},{8,16},{9,11},{10... | collective-permute-start | bytes 245768 | tf_op jit(solution)/shard_map/ppermute | solution.py:427
  53.8 5.0 %collective-permute-start.14 = (f32[32,128]{1,0:T(8,128)S(1)}, f32[32,128]{1,0:T(8,128)S(1)}, u32[]{:S(2)}, u32[]{:S(2)}) collective-permute-start(f32[32,128]{1,0:T(8,128)S(1)} %get-tuple-element.48.packed_ref), channel_id=1, source_target_pairs={{0,1},{1,3},{2,0},{3,7},{4,6},{5,13},{6,2},{7,5},{8,10},{9,17},{10... | collective-permute-start | bytes 49160 | tf_op jit(solution)/shard_map/ppermute | solution.py:427
where the time goes:
time: 95.7 us; the launch traced here: 95.4 us
  Pallas kernels  30.7 us (32%)
  blocking collectives  23.2 us (24%)
  starting transfers between devices  22.9 us (24%)
  waiting for transfers between devices  15.5 us (16%)
  local copies, waits for them, and re-layouts  2.96 us (3%)
    ppermute x11, starting transfers between devices, partner(): lax.ppermute(value, 'range', [(i, i ^ bits[i & 1]) for i in range(count)])  19.1 us
    ppermute x11, waiting for transfers between devices, partner(): lax.ppermute(value, 'range', [(i, i ^ bits[i & 1]) for i in range(count)])  15.5 us
    all_to_all x1, blocking collectives, on_device(): lax.all_to_all(mine, 'range', split_axis=0, concat_axis=0, tiled=True, ax...  13.4 us
    pallas_call x1, Pallas kernels, solve_outer(): pl.pallas_call(functools.partial(outer_kernel, total), out_shape=jax.Shap...  10.8 us
    all_to_all x1, blocking collectives, on_device(): lax.all_to_all(outgoing.reshape(devices, CAP, 2 * BLOCK), 'range', split_...  9.77 us
    pallas_call x1, Pallas kernels, solve_middle(): pl.pallas_call(functools.partial(middle_kernel, total), out_shape=[jax.Sh...  4.96 us
    pallas_call x4, Pallas kernels, cross(): pl.pallas_call(functools.partial(cross_kernel, len(spectra)), out_shape=j...  4.26 us
    pallas_call x1, Pallas kernels, spectra_first(): pl.pallas_call(spectra_first_kernel, out_shape=[jax.ShapeDtypeStruct((pul...  4.12 us
  transfers between devices with their start and end apart: 15, of which 9 were waited for; matrix products, arithmetic and copies ran while one was open for 0% of the time, Pallas kernels for 14%

commit v1 on v0

--- a/solution.py
+++ b/solution.py
@@ -449,15 +449,6 @@
     return jnp.concatenate([both[:rows], both[rows:]], axis=1)
 
 
-def conj_mul(a, b):
-    half = a.shape[1] // 2
-    both = lax.dot_general(
-        a, b, (((0,), (0,)), ((), ())),
-        precision=lax.Precision.HIGHEST, preferred_element_type=F32,
-    )
-    return both[:half] - turn(both[half:])
-
-
 def reciprocal(x):
     value = pl.reciprocal(x, approx=True)
     for _ in range(2):
@@ -528,12 +519,12 @@
     return out
 
 
-def invert(matrix, w_ref, l_ref):
+def invert(matrix):
     chans, width = matrix.shape
     sub = 8
     tiles = [matrix[t * sub : (t + 1) * sub, :] for t in range(chans // sub)]
     lane = iota((sub, width), 1)
-    low = jnp.bitwise_and(lane, chans - 1)
+    row = iota((sub, width), 0)
     first_half = lane < chans
 
     def spin(value):
@@ -559,6 +550,7 @@
             pivot[i][i] = column(lines[i], k + i)
             for j in range(i + 1, 4):
                 pivot[i][j] = column(lines[i], k + j), column(lines[i], chans + k + j)
+        low = jnp.bitwise_and(lane, chans - 1)
         cleared = (low >= k) & (low < k + 4)
         unit = [
             jnp.where(cleared, jnp.where(lane == k + i, 1.0, 0.0), lines[i]) for i in range(4)
@@ -577,18 +569,19 @@
                     other.append(-(im * unit[j]))
             fresh_lines.append(combine(terms))
             fresh_spun.append(combine(other))
-            w_ref[k + i : k + i + 1, :] = fresh_lines[i][:1]
-            l_ref[k + i : k + i + 1, :] = unit[i][:1]
-        for s in range(t if r == 0 else t + 1, len(tiles)):
-            tile = tiles[s]
+        fresh = []
+        for s, tile in enumerate(tiles):
             terms = []
             for i in range(4):
                 terms.append(column(tile, k + i) * fresh_lines[i])
                 terms.append(column(tile, chans + k + i) * fresh_spun[i])
-            tiles[s] = jnp.where(cleared, 0.0, tile) - combine(terms)
-    shape = (chans, width)
-    done = jnp.bitwise_and(iota(shape, 1), chans - 1) < (iota(shape, 0) // 4 + 1) * 4
-    return conj_mul(jnp.where(done, w_ref[...], 0.0), jnp.where(done, l_ref[...], 0.0))
+            value = jnp.where(cleared, 0.0, tile) - combine(terms)
+            if s == t:
+                for i in range(4):
+                    value = jnp.where(row == r + i, fresh_lines[i], value)
+            fresh.append(value)
+        tiles = fresh
+    return jnp.concatenate(tiles, axis=0)
 
 
 def unpacked(ref, scale):
@@ -605,18 +598,18 @@
     return jnp.concatenate([real_part, imag_part], axis=1)
 
 
-def middle_kernel(total, packed_ref, steer_ref, inv_ref, t_ref, w_ref, l_ref):
+def middle_kernel(total, packed_ref, steer_ref, inv_ref, t_ref):
     chans = inv_ref.shape[0]
     mixed = unpacked(packed_ref, F32(1.0 / total))
     twice = jnp.concatenate([mixed, mixed], axis=1)
     across = jnp.concatenate([twice, twice], axis=0).T[:chans, :chans]
-    inverse = invert(hermitian(mixed, across), w_ref, l_ref)
+    inverse = invert(hermitian(mixed, across))
     inv_ref[...] = inverse
     t_ref[...] = mul(steer_ref[...], inverse)
 
 
 def outer_kernel(total, own_ref, left_ref, right_ref, steer_ref, inv_ref, t_ref, out_ref,
-                 work, keep, w_ref, l_ref):
+                 work, keep, small):
     chans = inv_ref.shape[0]
     scale = F32(1.0 / total)
     half = chans // 2
@@ -625,46 +618,47 @@
     ml = left_ref[half : half + chans] * scale
     rl = left_ref[half + chans :] * scale
     rm = own_ref[half : half + chans] * scale
-    pair = jnp.concatenate([m_left, m_right], axis=1)
-    square = jnp.concatenate([pair, pair], axis=0).T
-    inv_mid = inv_ref[...]
+    across = jnp.concatenate([jnp.concatenate([m_left, m_right], axis=1), ml], axis=0).T
+    lm = jnp.concatenate([across[:chans, chans:], -across[chans:, chans:]], axis=1)
     t = t_ref[...]
-    h = mul(inv_mid, ml)
-    g = mul(rm, inv_mid)
-    work[...] = hermitian(m_left, square[:chans, :chans]) - conj_mul(ml, h)
-    s_rl = rl - mul(rm, h)
-    s_rr = hermitian(m_right, square[chans:, :chans]) - mul_conj(g, rm)
-    rhs_left = -mul(t, ml)
-    rhs_right = -mul_conj(t, rm)
-    keep[0] = s_rl
-    keep[1] = s_rr
-    keep[2] = h
-    keep[3] = g
-    keep[4, 0:BEAMS] = rhs_left
-    keep[4, BEAMS : 2 * BEAMS] = rhs_right
+    both = mul(jnp.concatenate([rm, lm], axis=0), inv_ref[...])
+    g_right, g_left = both[:chans], both[chans:]
+    by_left = mul(jnp.concatenate([g_left, g_right, t], axis=0), ml)
+    by_right = mul_conj(jnp.concatenate([g_right, t], axis=0), rm)
+    work[...] = hermitian(m_left, across[:chans, :chans]) - by_left[:chans]
+    keep[0] = rl - by_left[chans : 2 * chans]
+    keep[1] = hermitian(m_right, across[chans:, :chans]) - by_right[:chans]
+    keep[2] = g_left
+    keep[3] = g_right
+    small[0] = -by_left[2 * chans :]
+    small[1] = -by_right[chans:]
 
     @pl.loop(0, 2)
     def _(stage):
-        work[...] = invert(work[...], w_ref, l_ref)
+        work[...] = invert(work[...])
 
         @pl.when(stage == 0)
         def _():
-            inverse = work[...]
             s_rl = keep[0]
-            both = mul(jnp.concatenate([s_rl, keep[4, 0:BEAMS]], axis=0), inverse)
-            k, y_left = both[:chans], both[chans:]
-            work[...] = keep[1] - mul_conj(k, s_rl)
-            keep[0] = k
-            keep[4, BEAMS : 2 * BEAMS] = keep[4, BEAMS : 2 * BEAMS] - mul_conj(y_left, s_rl)
-            keep[4, 0:BEAMS] = y_left
-            keep[4, 2 * BEAMS : 3 * BEAMS] = t_ref[...] - mul_conj(y_left, keep[2])
-            keep[3] = keep[3] - mul_conj(k, keep[2])
+            both = mul(jnp.concatenate([s_rl, small[0]], axis=0), work[...])
+            back = mul_conj(both, s_rl)
+            work[...] = keep[1] - back[:chans]
+            small[1] = small[1] - back[chans:]
+            middle = mul(both, keep[2])
+            keep[0] = both[:chans]
+            small[0] = both[chans:]
+            keep[3] = keep[3] - middle[:chans]
+            small[2] = t_ref[...] - middle[chans:]
 
         @pl.when(stage == 1)
         def _():
-            y_right = mul(keep[4, BEAMS : 2 * BEAMS], work[...])
-            y_left = keep[4, 0:BEAMS] - mul(y_right, keep[0])
-            y_mid = keep[4, 2 * BEAMS : 3 * BEAMS] - mul(y_right, keep[3])
+            y_right = mul(small[1], work[...])
+            factors = jnp.concatenate([embed(keep[0]), embed(keep[3])], axis=1)
+            both = jnp.dot(
+                y_right, factors, precision=lax.Precision.HIGHEST, preferred_element_type=F32
+            )
+            y_left = small[0] - both[:, : 2 * chans]
+            y_mid = small[2] - both[:, 2 * chans :]
             quad = jnp.sum(steer_ref[...] * y_mid, axis=1, keepdims=True)
             y = jnp.concatenate([y_left, y_mid, y_right], axis=1) / jnp.sqrt(quad)
             real_lane = lax.rem(iota(y.shape, 1), 2 * chans) < chans
@@ -690,7 +684,6 @@
         ],
         in_specs=[vmem_spec()] * 2,
         out_specs=[vmem_spec()] * 2,
-        scratch_shapes=[pltpu.VMEM((2 * half, wide), F32)] * 2,
         compiler_params=params(),
     )(packed, steer)
 
@@ -703,8 +696,9 @@
         in_specs=[vmem_spec()] * 6,
         out_specs=vmem_spec(),
         scratch_shapes=[
-            pltpu.VMEM((chans, wide), F32), pltpu.VMEM((5, chans, wide), F32),
-            pltpu.VMEM((chans, wide), F32), pltpu.VMEM((chans, wide), F32),
+            pltpu.VMEM((chans, wide), F32),
+            pltpu.VMEM((4, chans, wide), F32),
+            pltpu.VMEM((3, BEAMS, wide), F32),
         ],
         compiler_params=params(),
     )(own, left, right, steer, inverse, t)

time: 95.7 us -> 92.5 us (0.967)
  Pallas kernels: 30.7 us -> 27.4 us
    pallas_call x1, Pallas kernels: 10.8 us -> 8.54 us  [solve_outer(): pl.pallas_call(functools.partial(outer_kernel, total), out_shape=jax.Shap...]
where the time goes in v1:
time: 92.5 us; the launch traced here: 92.2 us
  Pallas kernels  27.4 us (30%)
  blocking collectives  23.2 us (25%)
  starting transfers between devices  22.8 us (25%)
  waiting for transfers between devices  15.5 us (17%)
  local copies, waits for them, and re-layouts  2.96 us (3%)
    ppermute x11, starting transfers between devices, partner(): lax.ppermute(value, 'range', [(i, i ^ bits[i & 1]) for i in range(count)])  19.1 us
    ppermute x11, waiting for transfers between devices, partner(): lax.ppermute(value, 'range', [(i, i ^ bits[i & 1]) for i in range(count)])  15.5 us
    all_to_all x1, blocking collectives, on_device(): lax.all_to_all(mine, 'range', split_axis=0, concat_axis=0, tiled=True, ax...  13.5 us
    all_to_all x1, blocking collectives, on_device(): lax.all_to_all(outgoing.reshape(devices, CAP, 2 * BLOCK), 'range', split_...  9.77 us
    pallas_call x1, Pallas kernels, solve_outer(): pl.pallas_call(functools.partial(outer_kernel, total), out_shape=jax.Shap...  8.54 us
    pallas_call x4, Pallas kernels, cross(): pl.pallas_call(functools.partial(cross_kernel, len(spectra)), out_shape=j...  4.26 us
    pallas_call x1, Pallas kernels, spectra_first(): pl.pallas_call(spectra_first_kernel, out_shape=[jax.ShapeDtypeStruct((pul...  4.12 us
    pallas_call x1, Pallas kernels, solve_middle(): pl.pallas_call(functools.partial(middle_kernel, total), out_shape=[jax.Sh...  4 us
  transfers between devices with their start and end apart: 15, of which 9 were waited for; matrix products, arithmetic and copies ran while one was open for 0% of the time, Pallas kernels for 14%

profile of v1, /device:TPU:0, one launch (start us, length us, event | category | flops | bytes accessed | tf_op | source)
XLA Modules:
  0.0 92.2 jit_solution(11533648714337291428)
XLA Ops:
  0.0 2.4 %shard_map.82 = (bf16[2,1024,128]{2,1,0:T(8,128)(2,1)}, bf16[2,1024,128]{2,1,0:T(8,128)(2,1)}, f32[8,128]{1,0:T(8,128)}) custom-call(bf16[2,2048,256]{2,1,0:T(8,128)(2,1)} %bitcast.3), custom_call_target="tpu_custom_call" | custom-call | tf_op jit(solution)/shard_map/pallas_call | solution.py:78
  2.4 1.3 %collective-permute-start.3 = (bf16[2,1024,128]{2,1,0:T(8,128)(2,1)}, bf16[2,1024,128]{2,1,0:T(8,128)(2,1)S(1)}, u32[]{:S(2)}, u32[]{:S(2)}) collective-permute-start(bf16[2,1024,128]{2,1,0:T(8,128)(2,1)} %get-tuple-element.36), channel_id=1, source_target_pairs={{1,0},{2,1},{3,2},{4,3},{5,4},{6,5},{7,6},{8,7},{9,8},{10,9},{11,1... | collective-permute-start | bytes 1572872 | tf_op jit(solution)/shard_map/ppermute | solution.py:773
  3.7 1.3 %collective-permute-start = (bf16[2,1024,128]{2,1,0:T(8,128)(2,1)}, bf16[2,1024,128]{2,1,0:T(8,128)(2,1)S(1)}, u32[]{:S(2)}, u32[]{:S(2)}) collective-permute-start(bf16[2,1024,128]{2,1,0:T(8,128)(2,1)} %get-tuple-element.31), channel_id=1, source_target_pairs={{1,0},{2,1},{3,2},{4,3},{5,4},{6,5},{7,6},{8,7},{9,8},{10,9},{11,1... | collective-permute-start | bytes 1572872 | tf_op jit(solution)/shard_map/ppermute | solution.py:773
  5.0 1.6 %copy-done = bf16[2,64,32,256]{3,2,1,0:T(8,128)(2,1)S(1)} copy-done((bf16[2,64,32,256]{3,2,1,0:T(8,128)(2,1)S(1)}, bf16[2,64,32,256]{3,2,1,0:T(8,128)(2,1)}, u32[]{:S(2)}) %copy-start) | copy-done | bytes 2097176
  7.3 4.1 %shard_map.83 = (bf16[32,2,64,128]{3,2,1,0:T(8,128)(2,1)S(1)}, f32[2048,256]{1,0:T(8,128)S(1)}, bf16[2,256,256]{2,1,0:T(8,128)(2,1)S(1)}, bf16[18,2,32,128]{3,2,...) custom-call(bf16[2,2048,256]{2,1,0:T(8,128)(2,1)S(1)} %bitcast.4, bf16[2,128]{1,0:T(2,128)(2,1)S(1)} %copy-done.4, ...), custom_call_target="tpu_custom_call" | custom-call | flops 1 | bytes 1 | tf_op jit(solution)/shard_map/pallas_call | solution.py:199
  11.4 1.8 %collective-permute-start.1 = (bf16[18,2,32,128]{3,2,1,0:T(8,128)(2,1)S(1)}, bf16[18,2,32,128]{3,2,1,0:T(8,128)(2,1)S(1)}, u32[]{:S(2)}, u32[]{:S(2)}) collective-permute-start(bf16[18,2,32,128]{3,2,1,0:T(8,128)(2,1)S(1)} %get-tuple-element.33), channel_id=1, source_target_pairs={{0,1},{1,0},{2,3},{3,2},{4,5},{5,4},{6,7},{7,6},{8,9},{9,8},{10,11... | collective-permute-start | bytes 884744 | tf_op jit(solution)/shard_map/ppermute | solution.py:288
  14.9 1.1 %shard_map.85._.refs_2_ = f32[16,192,128]{2,1,0:T(8,128)S(1)} custom-call(bf16[18,2,32,128]{3,2,1,0:T(8,128)(2,1)S(1)} %collective-permute-done.1.refs_0_, bf16[18,2,32,128]{3,2,1,0:T(8,128)(2,1)S(1)} %collective-permute-done.2.refs_1_, f32[16,192,128]{2,1,0:T(8,128)S(1)} %shard_map.84.refs_2_), custom_call_target="tpu_custom_call" | custom-call | flops 1 | bytes 1 | tf_op jit(solution)/shard_map/pallas_call | solution.py:273
  17.9 3.0 %collective-permute-start.4 = (bf16[18,2,32,128]{3,2,1,0:T(8,128)(2,1)S(1)}, bf16[18,2,32,128]{3,2,1,0:T(8,128)(2,1)S(1)}, u32[]{:S(2)}, u32[]{:S(2)}) collective-permute-start(bf16[18,2,32,128]{3,2,1,0:T(8,128)(2,1)S(1)} %get-tuple-element.38), channel_id=1, source_target_pairs={{0,1},{1,0},{2,3},{3,2},{4,5},{5,4},{6,7},{7,6},{8,9},{9,8},{10,11... | collective-permute-start | bytes 884744 | tf_op jit(solution)/shard_map/ppermute | solution.py:288
  22.1 1.1 %shard_map.89.keep_ref.refs_0_ = f32[16,192,128]{2,1,0:T(8,128)S(1)} custom-call(bf16[18,2,32,128]{3,2,1,0:T(8,128)(2,1)S(1)} %collective-permute-done.4.refs_0_, bf16[18,2,32,128]{3,2,1,0:T(8,128)(2,1)S(1)} %collective-permute-done.5.refs_1_, f32[16,192,128]{2,1,0:T(8,128)S(1)} %shard_map.88.refs_2_), custom_call_target="tpu_custom_call" | custom-call | flops 1 | bytes 1 | tf_op jit(solution)/shard_map/pallas_call | solution.py:273
  23.4 2.4 %collective-permute-start.6 = (f32[8,80,128]{2,1,0:T(8,128)S(1)}, f32[8,80,128]{2,1,0:T(8,128)S(1)}, u32[]{:S(2)}, u32[]{:S(2)}) collective-permute-start(f32[8,80,128]{2,1,0:T(8,128)S(1)} %get-tuple-element.40), channel_id=1, source_target_pairs={{0,2},{1,5},{2,0},{3,7},{4,6},{5,1},{6,4},{7,3},{8,10},{9,13},{10,... | collective-permute-start | bytes 983048 | tf_op jit(solution)/shard_map/ppermute | solution.py:288
  25.8 2.4 %collective-permute-start.7 = (f32[8,80,128]{2,1,0:T(8,128)S(1)}, f32[8,80,128]{2,1,0:T(8,128)S(1)}, u32[]{:S(2)}, u32[]{:S(2)}) collective-permute-start(f32[8,80,128]{2,1,0:T(8,128)S(1)} %get-tuple-element.41), channel_id=1, source_target_pairs={{0,4},{1,3},{2,6},{3,1},{4,0},{5,7},{6,2},{7,5},{8,12},{9,11},{10,... | collective-permute-start | bytes 983048 | tf_op jit(solution)/shard_map/ppermute | solution.py:288
  28.2 4.3 %collective-permute-done.6.a1_ref.refs_1_ = f32[8,80,128]{2,1,0:T(8,128)S(1)} collective-permute-done((f32[8,80,128]{2,1,0:T(8,128)S(1)}, f32[8,80,128]{2,1,0:T(8,128)S(1)}, u32[]{:S(2)}, u32[]{:S(2)}) %collective-permute-start.6) | collective-permute-done | bytes 327712 | tf_op jit(solution)/shard_map/ppermute | solution.py:288
  33.6 3.2 %collective-permute-start.8 = (f32[4,80,128]{2,1,0:T(8,128)S(1)}, f32[4,80,128]{2,1,0:T(8,128)S(1)}, u32[]{:S(2)}, u32[]{:S(2)}) collective-permute-start(f32[4,80,128]{2,1,0:T(8,128)S(1)} %get-tuple-element.42), channel_id=1, source_target_pairs={{0,4},{1,3},{2,6},{3,1},{4,0},{5,7},{6,2},{7,5},{8,12},{9,11},{10,... | collective-permute-start | bytes 491528 | tf_op jit(solution)/shard_map/ppermute | solution.py:288
  36.8 1.7 %collective-permute-start.9 = (f32[4,80,128]{2,1,0:T(8,128)S(1)}, f32[4,80,128]{2,1,0:T(8,128)S(1)}, u32[]{:S(2)}, u32[]{:S(2)}) collective-permute-start(f32[4,80,128]{2,1,0:T(8,128)S(1)} %get-tuple-element.43), channel_id=1, source_target_pairs={{0,2},{1,5},{2,0},{3,7},{4,6},{5,1},{6,4},{7,3},{8,10},{9,13},{10,... | collective-permute-start | bytes 491528 | tf_op jit(solution)/shard_map/ppermute | solution.py:288
  38.5 2.7 %collective-permute-done.8.refs_3_ = f32[4,80,128]{2,1,0:T(8,128)S(1)} collective-permute-done((f32[4,80,128]{2,1,0:T(8,128)S(1)}, f32[4,80,128]{2,1,0:T(8,128)S(1)}, u32[]{:S(2)}, u32[]{:S(2)}) %collective-permute-start.8) | collective-permute-done | bytes 163872 | tf_op jit(solution)/shard_map/ppermute | solution.py:288
  42.3 2.7 %collective-permute-start.10 = (f32[160,128]{1,0:T(8,128)S(1)}, f32[160,128]{1,0:T(8,128)S(1)}, u32[]{:S(2)}, u32[]{:S(2)}) collective-permute-start(f32[160,128]{1,0:T(8,128)S(1)} %get-tuple-element.44), channel_id=1, source_target_pairs={{0,16},{1,17},{2,18},{3,19},{4,20},{5,21},{6,22},{7,23},{8,24},{9,... | collective-permute-start | bytes 245768 | tf_op jit(solution)/shard_map/ppermute | solution.py:288
  44.9 1.3 %collective-permute-start.11 = (f32[160,128]{1,0:T(8,128)S(1)}, f32[160,128]{1,0:T(8,128)S(1)}, u32[]{:S(2)}, u32[]{:S(2)}) collective-permute-start(f32[160,128]{1,0:T(8,128)S(1)} %get-tuple-element.45), channel_id=1, source_target_pairs={{0,24},{1,25},{2,26},{3,27},{4,28},{5,29},{6,30},{7,31},{8,16},{9,... | collective-permute-start | bytes 245768 | tf_op jit(solution)/shard_map/ppermute | solution.py:288
  46.4 5.5 %collective-permute-done.10.refs_5_ = f32[160,128]{1,0:T(8,128)S(1)} collective-permute-done((f32[160,128]{1,0:T(8,128)S(1)}, f32[160,128]{1,0:T(8,128)S(1)}, u32[]{:S(2)}, u32[]{:S(2)}) %collective-permute-start.10) | collective-permute-done | bytes 81952 | tf_op jit(solution)/shard_map/ppermute | solution.py:288
  52.6 1.1 %collective-permute-start.13 = (f32[160,128]{1,0:T(8,128)S(1)}, f32[160,128]{1,0:T(8,128)S(1)}, u32[]{:S(2)}, u32[]{:S(2)}) collective-permute-start(f32[160,128]{1,0:T(8,128)S(1)} %get-tuple-element.47.own_ref), channel_id=1, source_target_pairs={{0,2},{1,0},{2,6},{3,1},{4,12},{5,7},{6,4},{7,3},{8,16},{9,11},{10... | collective-permute-start | bytes 245768 | tf_op jit(solution)/shard_map/ppermute | solution.py:427
  53.7 4.0 %shard_map.94 = (f32[64,128]{1,0:T(8,128)S(1)}, f32[8,128]{1,0:T(8,128)S(1)}) custom-call(f32[32,128]{1,0:T(8,128)S(1)} %get-tuple-element.48.packed_ref, f32[8,128]{1,0:T(8,128)S(1)} %copy-done.2), custom_call_target="tpu_custom_call" | custom-call | tf_op jit(solution)/shard_map/pallas_call | solution.py:679
  57.8 8.5 %shard_map.95 = bf16[32,8,384]{2,1,0:T(8,128)(2,1)S(1)} custom-call(f32[160,128]{1,0:T(8,128)S(1)} %get-tuple-element.47.own_ref, f32[160,128]{1,0:T(8,128)S(1)} %collective-permute-done.13.left_ref, f32[32,128]{1,0:T(8,128)S(1)} %collective-permute-done.14.right_ref, f32[8,128]{1,0:T(8,128)S(1)} %copy-done.2, f32[64,128]{1,0:T(8,128)S(1)} %get-tuple-element.49.inv_ref, ...), custom_call_target="tpu_custom_call" | custom-call | tf_op jit(solution)/shard_map/pallas_call | solution.py:693
  66.3 13.5 %all_to_all.10.w_ref = bf16[32,8,384]{2,1,0:T(8,128)(2,1)S(1)} all-to-all(bf16[32,8,384]{2,1,0:T(8,128)(2,1)S(1)} %shard_map.95), channel_id=1, replica_groups=mesh['range'=32] {'range'}, dimensions={0} | all-to-all | bytes 393216 | tf_op jit(solution)/shard_map/all_to_all | solution.py:794
  79.8 2.0 %shard_map.96 = bf16[64,256]{1,0:T(8,128)(2,1)S(1)} custom-call(s32[32]{0:T(128)S(1)} %copy-done.5, s32[32]{0:T(128)S(1)} %copy-done.6, s32[32]{0:T(128)S(1)} %copy-done.7, s32[32]{0:T(128)S(1)} %bitcast.6, bf16[32,128,128]{2,1,0:T(8,128)(2,1)S(1)} %bitcast.5, bf16[32,2,32,128]{3,2,1,0:T(8,128)(2,1)S(1)} %get-tuple-element.35.refs_0_.upper_ref, ...), custom_call_target="tpu_custom_call" | custom-call | tf_op jit(solution)/shard_map/pallas_call | solution.py:752
  81.8 9.8 %all_to_all.11 = bf16[32,2,256]{2,1,0:T(2,128)(2,1)S(1)} all-to-all(bf16[32,2,256]{2,1,0:T(2,128)(2,1)S(1)} %reshape.17), channel_id=1, replica_groups=mesh['range'=32] {'range'}, dimensions={0} | all-to-all | bytes 65536 | tf_op jit(solution)/shard_map/all_to_all | solution.py:802
  (43 shorter events, 9.3 us)
Async XLA Ops:
  0.0 5.0 %copy-start.1 = (bf16[512,512]{1,0:T(8,128)(2,1)S(1)}, bf16[512,512]{1,0:T(8,128)(2,1)}, u32[]{:S(2)}) copy-start(bf16[512,512]{1,0:T(8,128)(2,1)} %constant.4.clone.dft_ref) | copy-start | bytes 1572868
  0.0 5.0 %copy-start.4 = (bf16[2,128]{1,0:T(2,128)(2,1)S(1)}, bf16[2,128]{1,0:T(2,128)(2,1)}, u32[]{:S(2)}) copy-start(bf16[2,128]{1,0:T(2,128)(2,1)} %rep_ref.1) | copy-start | bytes 1540
  2.4 13.6 %collective-permute-start.3 = (bf16[2,1024,128]{2,1,0:T(8,128)(2,1)}, bf16[2,1024,128]{2,1,0:T(8,128)(2,1)S(1)}, u32[]{:S(2)}, u32[]{:S(2)}) collective-permute-start(bf16[2,1024,128]{2,1,0:T(8,128)(2,1)} %get-tuple-element.36), channel_id=1, source_target_pairs={{1,0},{2,1},{3,2},{4,3},{5,4},{6,5},{7,6},{8,7},{9,8},{10,9},{11,1... | collective-permute-start | bytes 1572872 | tf_op jit(solution)/shard_map/ppermute | solution.py:773
  3.7 13.4 %collective-permute-start = (bf16[2,1024,128]{2,1,0:T(8,128)(2,1)}, bf16[2,1024,128]{2,1,0:T(8,128)(2,1)S(1)}, u32[]{:S(2)}, u32[]{:S(2)}) collective-permute-start(bf16[2,1024,128]{2,1,0:T(8,128)(2,1)} %get-tuple-element.31), channel_id=1, source_target_pairs={{1,0},{2,1},{3,2},{4,3},{5,4},{6,5},{7,6},{8,7},{9,8},{10,9},{11,1... | collective-permute-start | bytes 1572872 | tf_op jit(solution)/shard_map/ppermute | solution.py:773
  5.0 1.6 %copy-start = (bf16[2,64,32,256]{3,2,1,0:T(8,128)(2,1)S(1)}, bf16[2,64,32,256]{3,2,1,0:T(8,128)(2,1)}, u32[]{:S(2)}) copy-start(bf16[2,64,32,256]{3,2,1,0:T(8,128)(2,1)} %param.8) | copy-start | bytes 6291460
  6.6 0.7 copy-start.3
  11.4 3.0 %collective-permute-start.1 = (bf16[18,2,32,128]{3,2,1,0:T(8,128)(2,1)S(1)}, bf16[18,2,32,128]{3,2,1,0:T(8,128)(2,1)S(1)}, u32[]{:S(2)}, u32[]{:S(2)}) collective-permute-start(bf16[18,2,32,128]{3,2,1,0:T(8,128)(2,1)S(1)} %get-tuple-element.33), channel_id=1, source_target_pairs={{0,1},{1,0},{2,3},{3,2},{4,5},{5,4},{6,7},{7,6},{8,9},{9,8},{10,11... | collective-permute-start | bytes 884744 | tf_op jit(solution)/shard_map/ppermute | solution.py:288
  13.3 1.6 %collective-permute-start.2 = (bf16[18,2,32,128]{3,2,1,0:T(8,128)(2,1)S(1)}, bf16[18,2,32,128]{3,2,1,0:T(8,128)(2,1)S(1)}, u32[]{:S(2)}, u32[]{:S(2)}) collective-permute-start(bf16[18,2,32,128]{3,2,1,0:T(8,128)(2,1)S(1)} %get-tuple-element.34), channel_id=1, source_target_pairs={{0,1},{1,0},{2,3},{3,2},{4,5},{5,4},{6,7},{7,6},{8,9},{9,8},{10,11... | collective-permute-start | bytes 884744 | tf_op jit(solution)/shard_map/ppermute | solution.py:288
  16.7 5.2 %collective-permute-start.5 = (bf16[18,2,32,128]{3,2,1,0:T(8,128)(2,1)S(1)}, bf16[18,2,32,128]{3,2,1,0:T(8,128)(2,1)S(1)}, u32[]{:S(2)}, u32[]{:S(2)}) collective-permute-start(bf16[18,2,32,128]{3,2,1,0:T(8,128)(2,1)S(1)} %get-tuple-element.39), channel_id=1, source_target_pairs={{0,1},{1,0},{2,3},{3,2},{4,5},{5,4},{6,7},{7,6},{8,9},{9,8},{10,11... | collective-permute-start | bytes 884744 | tf_op jit(solution)/shard_map/ppermute | solution.py:288
  17.9 4.2 %collective-permute-start.4 = (bf16[18,2,32,128]{3,2,1,0:T(8,128)(2,1)S(1)}, bf16[18,2,32,128]{3,2,1,0:T(8,128)(2,1)S(1)}, u32[]{:S(2)}, u32[]{:S(2)}) collective-permute-start(bf16[18,2,32,128]{3,2,1,0:T(8,128)(2,1)S(1)} %get-tuple-element.38), channel_id=1, source_target_pairs={{0,1},{1,0},{2,3},{3,2},{4,5},{5,4},{6,7},{7,6},{8,9},{9,8},{10,11... | collective-permute-start | bytes 884744 | tf_op jit(solution)/shard_map/ppermute | solution.py:288
  23.4 9.1 %collective-permute-start.6 = (f32[8,80,128]{2,1,0:T(8,128)S(1)}, f32[8,80,128]{2,1,0:T(8,128)S(1)}, u32[]{:S(2)}, u32[]{:S(2)}) collective-permute-start(f32[8,80,128]{2,1,0:T(8,128)S(1)} %get-tuple-element.40), channel_id=1, source_target_pairs={{0,2},{1,5},{2,0},{3,7},{4,6},{5,1},{6,4},{7,3},{8,10},{9,13},{10,... | collective-permute-start | bytes 983048 | tf_op jit(solution)/shard_map/ppermute | solution.py:288
  25.8 7.6 %collective-permute-start.7 = (f32[8,80,128]{2,1,0:T(8,128)S(1)}, f32[8,80,128]{2,1,0:T(8,128)S(1)}, u32[]{:S(2)}, u32[]{:S(2)}) collective-permute-start(f32[8,80,128]{2,1,0:T(8,128)S(1)} %get-tuple-element.41), channel_id=1, source_target_pairs={{0,4},{1,3},{2,6},{3,1},{4,0},{5,7},{6,2},{7,5},{8,12},{9,11},{10,... | collective-permute-start | bytes 983048 | tf_op jit(solution)/shard_map/ppermute | solution.py:288
  33.6 7.6 %collective-permute-start.8 = (f32[4,80,128]{2,1,0:T(8,128)S(1)}, f32[4,80,128]{2,1,0:T(8,128)S(1)}, u32[]{:S(2)}, u32[]{:S(2)}) collective-permute-start(f32[4,80,128]{2,1,0:T(8,128)S(1)} %get-tuple-element.42), channel_id=1, source_target_pairs={{0,4},{1,3},{2,6},{3,1},{4,0},{5,7},{6,2},{7,5},{8,12},{9,11},{10,... | collective-permute-start | bytes 491528 | tf_op jit(solution)/shard_map/ppermute | solution.py:288
  36.8 5.3 %collective-permute-start.9 = (f32[4,80,128]{2,1,0:T(8,128)S(1)}, f32[4,80,128]{2,1,0:T(8,128)S(1)}, u32[]{:S(2)}, u32[]{:S(2)}) collective-permute-start(f32[4,80,128]{2,1,0:T(8,128)S(1)} %get-tuple-element.43), channel_id=1, source_target_pairs={{0,2},{1,5},{2,0},{3,7},{4,6},{5,1},{6,4},{7,3},{8,10},{9,13},{10,... | collective-permute-start | bytes 491528 | tf_op jit(solution)/shard_map/ppermute | solution.py:288
  42.3 11.5 %copy-start.2 = (f32[8,128]{1,0:T(8,128)S(1)}, f32[8,128]{1,0:T(8,128)}, u32[]{:S(2)}) copy-start(f32[8,128]{1,0:T(8,128)} %constant.5.clone.steer_ref) | copy-start | bytes 12292
  42.3 9.6 %collective-permute-start.10 = (f32[160,128]{1,0:T(8,128)S(1)}, f32[160,128]{1,0:T(8,128)S(1)}, u32[]{:S(2)}, u32[]{:S(2)}) collective-permute-start(f32[160,128]{1,0:T(8,128)S(1)} %get-tuple-element.44), channel_id=1, source_target_pairs={{0,16},{1,17},{2,18},{3,19},{4,20},{5,21},{6,22},{7,23},{8,24},{9,... | collective-permute-start | bytes 245768 | tf_op jit(solution)/shard_map/ppermute | solution.py:288
  44.9 7.0 %collective-permute-start.11 = (f32[160,128]{1,0:T(8,128)S(1)}, f32[160,128]{1,0:T(8,128)S(1)}, u32[]{:S(2)}, u32[]{:S(2)}) collective-permute-start(f32[160,128]{1,0:T(8,128)S(1)} %get-tuple-element.45), channel_id=1, source_target_pairs={{0,24},{1,25},{2,26},{3,27},{4,28},{5,29},{6,30},{7,31},{8,16},{9,... | collective-permute-start | bytes 245768 | tf_op jit(solution)/shard_map/ppermute | solution.py:288
  46.3 33.5 %copy-start.5 = (s32[32]{0:T(128)S(1)}, s32[32]{0:T(128)}, u32[]{:S(2)}) copy-start(s32[32]{0:T(128)} %bin_ref.1) | copy-start | bytes 388
  46.3 33.5 %copy-start.6 = (s32[32]{0:T(128)S(1)}, s32[32]{0:T(128)}, u32[]{:S(2)}) copy-start(s32[32]{0:T(128)} %block_ref.1) | copy-start | bytes 388
  46.3 33.5 %copy-start.7 = (s32[32]{0:T(128)S(1)}, s32[32]{0:T(128)}, u32[]{:S(2)}) copy-start(s32[32]{0:T(128)} %beam_ref.1) | copy-start | bytes 388
  46.3 33.5 %copy-start.8 = (s32[32,1]{0,1:T(1,128)S(1)}, s32[32,1]{0,1:T(1,128)}, u32[]{:S(2)}) copy-start(s32[32,1]{0,1:T(1,128)} %param.13) | copy-start | bytes 388
  46.3 6.2 %collective-permute-start.12 = (f32[160,128]{1,0:T(8,128)S(1)}, f32[160,128]{1,0:T(8,128)S(1)}, u32[]{:S(2)}, u32[]{:S(2)}) collective-permute-start(f32[160,128]{1,0:T(8,128)S(1)} %get-tuple-element.46), channel_id=1, source_target_pairs={{0,8},{1,9},{2,10},{3,11},{4,12},{5,13},{6,14},{7,15},{8,0},{9,1},... | collective-permute-start | bytes 245768 | tf_op jit(solution)/shard_map/ppermute | solution.py:288
  52.6 5.1 %collective-permute-start.13 = (f32[160,128]{1,0:T(8,128)S(1)}, f32[160,128]{1,0:T(8,128)S(1)}, u32[]{:S(2)}, u32[]{:S(2)}) collective-permute-start(f32[160,128]{1,0:T(8,128)S(1)} %get-tuple-element.47.own_ref), channel_id=1, source_target_pairs={{0,2},{1,0},{2,6},{3,1},{4,12},{5,7},{6,4},{7,3},{8,16},{9,11},{10... | collective-permute-start | bytes 245768 | tf_op jit(solution)/shard_map/ppermute | solution.py:427
  53.7 4.0 %collective-permute-start.14 = (f32[32,128]{1,0:T(8,128)S(1)}, f32[32,128]{1,0:T(8,128)S(1)}, u32[]{:S(2)}, u32[]{:S(2)}) collective-permute-start(f32[32,128]{1,0:T(8,128)S(1)} %get-tuple-element.48.packed_ref), channel_id=1, source_target_pairs={{0,1},{1,3},{2,0},{3,7},{4,6},{5,13},{6,2},{7,5},{8,10},{9,17},{10... | collective-permute-start | bytes 49160 | tf_op jit(solution)/shard_map/ppermute | solution.py:427

commit v2 on v1

--- a/solution.py
+++ b/solution.py
@@ -722,28 +722,35 @@
         both_ref[:, 0:BEAMS, lanes] = part.reshape(bins, BEAMS, wide)
         both_ref[:, BEAMS:, lanes] = turn(part).reshape(bins, BEAMS, wide)
 
-    def detection(j, carry):
+    def window(j):
         bin_id = bin_ref[j]
-        beam_id = beam_ref[j]
+        first = block_ref[j] == 0
+        pieces = []
+        for k in range(3):
+            band = lax.rem(bin_id + bins - 1 + k, bins)
+            later = [upper_ref[band, 0], lower_ref[band, 0], upper_ref[band, 1], lower_ref[band, 1]]
+            pieces.append(jnp.where(first, s0_ref[band], jnp.concatenate(later, axis=0)))
+        return jnp.concatenate(pieces, axis=0)
+
+    def store(j, block):
         owner = owner_ref[j]
         rank = seen_ref[owner]
         seen_ref[owner] = rank + 1
-        left = both_ref[index_of(bin_id)].astype(BF16)
-        bands = [lax.rem(bin_id + bins - 1 + k, bins) for k in range(3)]
-        first = block_ref[j] == 0
-        pieces = []
-        for b in bands:
-            later = [upper_ref[b, 0], lower_ref[b, 0], upper_ref[b, 1], lower_ref[b, 1]]
-            pieces.append(jnp.where(first, s0_ref[b], jnp.concatenate(later, axis=0)))
-        window = jnp.concatenate(pieces, axis=0)
-        both = dot(left, window)
-        line = jnp.concatenate([both[:BEAMS], both[BEAMS:]], axis=1)
-        chosen = jnp.where(iota(line.shape, 0) == beam_id, line, 0.0)
-        row = owner * CAP + rank
-        rows_ref[pl.ds(row, 1), :] = jnp.sum(chosen, axis=0, keepdims=True)
+        line = jnp.concatenate([block[:BEAMS], block[BEAMS:]], axis=1)
+        chosen = jnp.where(iota(line.shape, 0) == beam_ref[j], line, 0.0)
+        rows_ref[pl.ds(owner * CAP + rank, 1), :] = jnp.sum(chosen, axis=0, keepdims=True)
+
+    def detections(step, carry):
+        pair = [step * 2 + k for k in range(2)]
+        left = jnp.concatenate([both_ref[index_of(bin_ref[j])] for j in pair], axis=0)
+        both = dot(left.astype(BF16), jnp.concatenate([window(j) for j in pair], axis=1))
+        for k, j in enumerate(pair):
+            rows = slice(k * 2 * BEAMS, (k + 1) * 2 * BEAMS)
+            store(j, both[rows, k * gates : (k + 1) * gates])
         return carry
 
-    lax.fori_loop(0, count, detection, 0, unroll=32)
+    assert count % 2 == 0
+    lax.fori_loop(0, count // 2, detections, 0, unroll=16)
     out_ref[...] = rows_ref[...].astype(BF16)
 
 

time: 92.5 us -> 92.5 us (level)
  no operation moved by 1% of the time
where the time goes in v2:
time: 92.5 us; the launch traced here: 92.2 us
  Pallas kernels  27.5 us (30%)
  blocking collectives  23.2 us (25%)
  starting transfers between devices  22.8 us (25%)
  waiting for transfers between devices  15.5 us (17%)
  local copies, waits for them, and re-layouts  2.96 us (3%)
    ppermute x11, starting transfers between devices, partner(): lax.ppermute(value, 'range', [(i, i ^ bits[i & 1]) for i in range(count)])  19.1 us
    ppermute x11, waiting for transfers between devices, partner(): lax.ppermute(value, 'range', [(i, i ^ bits[i & 1]) for i in range(count)])  15.5 us
    all_to_all x1, blocking collectives, on_device(): lax.all_to_all(mine, 'range', split_axis=0, concat_axis=0, tiled=True, ax...  13.5 us
    all_to_all x1, blocking collectives, on_device(): lax.all_to_all(outgoing.reshape(devices, CAP, 2 * BLOCK), 'range', split_...  9.77 us
    pallas_call x1, Pallas kernels, solve_outer(): pl.pallas_call(functools.partial(outer_kernel, total), out_shape=jax.Shap...  8.54 us
    pallas_call x4, Pallas kernels, cross(): pl.pallas_call(functools.partial(cross_kernel, len(spectra)), out_shape=j...  4.26 us
    pallas_call x1, Pallas kernels, spectra_first(): pl.pallas_call(spectra_first_kernel, out_shape=[jax.ShapeDtypeStruct((pul...  4.12 us
    pallas_call x1, Pallas kernels, solve_middle(): pl.pallas_call(functools.partial(middle_kernel, total), out_shape=[jax.Sh...  4 us
  transfers between devices with their start and end apart: 15, of which 9 were waited for; matrix products, arithmetic and copies ran while one was open for 0% of the time, Pallas kernels for 14%

profile of v2, /device:TPU:0, one launch (start us, length us, event | category | flops | bytes accessed | tf_op | source)
XLA Modules:
  0.0 92.2 jit_solution(16395484578231081100)
XLA Ops:
  0.0 2.4 %shard_map.82 = (bf16[2,1024,128]{2,1,0:T(8,128)(2,1)}, bf16[2,1024,128]{2,1,0:T(8,128)(2,1)}, f32[8,128]{1,0:T(8,128)}) custom-call(bf16[2,2048,256]{2,1,0:T(8,128)(2,1)} %bitcast.3), custom_call_target="tpu_custom_call" | custom-call | tf_op jit(solution)/shard_map/pallas_call | solution.py:78
  2.4 1.3 %collective-permute-start.3 = (bf16[2,1024,128]{2,1,0:T(8,128)(2,1)}, bf16[2,1024,128]{2,1,0:T(8,128)(2,1)S(1)}, u32[]{:S(2)}, u32[]{:S(2)}) collective-permute-start(bf16[2,1024,128]{2,1,0:T(8,128)(2,1)} %get-tuple-element.36), channel_id=1, source_target_pairs={{1,0},{2,1},{3,2},{4,3},{5,4},{6,5},{7,6},{8,7},{9,8},{10,9},{11,1... | collective-permute-start | bytes 1572872 | tf_op jit(solution)/shard_map/ppermute | solution.py:780
  3.7 1.3 %collective-permute-start = (bf16[2,1024,128]{2,1,0:T(8,128)(2,1)}, bf16[2,1024,128]{2,1,0:T(8,128)(2,1)S(1)}, u32[]{:S(2)}, u32[]{:S(2)}) collective-permute-start(bf16[2,1024,128]{2,1,0:T(8,128)(2,1)} %get-tuple-element.31), channel_id=1, source_target_pairs={{1,0},{2,1},{3,2},{4,3},{5,4},{6,5},{7,6},{8,7},{9,8},{10,9},{11,1... | collective-permute-start | bytes 1572872 | tf_op jit(solution)/shard_map/ppermute | solution.py:780
  5.0 1.6 %copy-done = bf16[2,64,32,256]{3,2,1,0:T(8,128)(2,1)S(1)} copy-done((bf16[2,64,32,256]{3,2,1,0:T(8,128)(2,1)S(1)}, bf16[2,64,32,256]{3,2,1,0:T(8,128)(2,1)}, u32[]{:S(2)}) %copy-start) | copy-done | bytes 2097176
  7.3 4.1 %shard_map.83 = (bf16[32,2,64,128]{3,2,1,0:T(8,128)(2,1)S(1)}, f32[2048,256]{1,0:T(8,128)S(1)}, bf16[2,256,256]{2,1,0:T(8,128)(2,1)S(1)}, bf16[18,2,32,128]{3,2,...) custom-call(bf16[2,2048,256]{2,1,0:T(8,128)(2,1)S(1)} %bitcast.4, bf16[2,128]{1,0:T(2,128)(2,1)S(1)} %copy-done.4, ...), custom_call_target="tpu_custom_call" | custom-call | flops 1 | bytes 1 | tf_op jit(solution)/shard_map/pallas_call | solution.py:199
  11.4 1.8 %collective-permute-start.1 = (bf16[18,2,32,128]{3,2,1,0:T(8,128)(2,1)S(1)}, bf16[18,2,32,128]{3,2,1,0:T(8,128)(2,1)S(1)}, u32[]{:S(2)}, u32[]{:S(2)}) collective-permute-start(bf16[18,2,32,128]{3,2,1,0:T(8,128)(2,1)S(1)} %get-tuple-element.33), channel_id=1, source_target_pairs={{0,1},{1,0},{2,3},{3,2},{4,5},{5,4},{6,7},{7,6},{8,9},{9,8},{10,11... | collective-permute-start | bytes 884744 | tf_op jit(solution)/shard_map/ppermute | solution.py:288
  14.9 1.1 %shard_map.85._.refs_2_ = f32[16,192,128]{2,1,0:T(8,128)S(1)} custom-call(bf16[18,2,32,128]{3,2,1,0:T(8,128)(2,1)S(1)} %collective-permute-done.1.refs_0_, bf16[18,2,32,128]{3,2,1,0:T(8,128)(2,1)S(1)} %collective-permute-done.2.refs_1_, f32[16,192,128]{2,1,0:T(8,128)S(1)} %shard_map.84.refs_2_), custom_call_target="tpu_custom_call" | custom-call | flops 1 | bytes 1 | tf_op jit(solution)/shard_map/pallas_call | solution.py:273
  17.9 3.0 %collective-permute-start.4 = (bf16[18,2,32,128]{3,2,1,0:T(8,128)(2,1)S(1)}, bf16[18,2,32,128]{3,2,1,0:T(8,128)(2,1)S(1)}, u32[]{:S(2)}, u32[]{:S(2)}) collective-permute-start(bf16[18,2,32,128]{3,2,1,0:T(8,128)(2,1)S(1)} %get-tuple-element.38), channel_id=1, source_target_pairs={{0,1},{1,0},{2,3},{3,2},{4,5},{5,4},{6,7},{7,6},{8,9},{9,8},{10,11... | collective-permute-start | bytes 884744 | tf_op jit(solution)/shard_map/ppermute | solution.py:288
  22.1 1.1 %shard_map.89.keep_ref.refs_0_ = f32[16,192,128]{2,1,0:T(8,128)S(1)} custom-call(bf16[18,2,32,128]{3,2,1,0:T(8,128)(2,1)S(1)} %collective-permute-done.4.refs_0_, bf16[18,2,32,128]{3,2,1,0:T(8,128)(2,1)S(1)} %collective-permute-done.5.refs_1_, f32[16,192,128]{2,1,0:T(8,128)S(1)} %shard_map.88.refs_2_), custom_call_target="tpu_custom_call" | custom-call | flops 1 | bytes 1 | tf_op jit(solution)/shard_map/pallas_call | solution.py:273
  23.4 2.4 %collective-permute-start.6 = (f32[8,80,128]{2,1,0:T(8,128)S(1)}, f32[8,80,128]{2,1,0:T(8,128)S(1)}, u32[]{:S(2)}, u32[]{:S(2)}) collective-permute-start(f32[8,80,128]{2,1,0:T(8,128)S(1)} %get-tuple-element.40), channel_id=1, source_target_pairs={{0,2},{1,5},{2,0},{3,7},{4,6},{5,1},{6,4},{7,3},{8,10},{9,13},{10,... | collective-permute-start | bytes 983048 | tf_op jit(solution)/shard_map/ppermute | solution.py:288
  25.8 2.4 %collective-permute-start.7 = (f32[8,80,128]{2,1,0:T(8,128)S(1)}, f32[8,80,128]{2,1,0:T(8,128)S(1)}, u32[]{:S(2)}, u32[]{:S(2)}) collective-permute-start(f32[8,80,128]{2,1,0:T(8,128)S(1)} %get-tuple-element.41), channel_id=1, source_target_pairs={{0,4},{1,3},{2,6},{3,1},{4,0},{5,7},{6,2},{7,5},{8,12},{9,11},{10,... | collective-permute-start | bytes 983048 | tf_op jit(solution)/shard_map/ppermute | solution.py:288
  28.2 4.3 %collective-permute-done.6.a1_ref.refs_1_ = f32[8,80,128]{2,1,0:T(8,128)S(1)} collective-permute-done((f32[8,80,128]{2,1,0:T(8,128)S(1)}, f32[8,80,128]{2,1,0:T(8,128)S(1)}, u32[]{:S(2)}, u32[]{:S(2)}) %collective-permute-start.6) | collective-permute-done | bytes 327712 | tf_op jit(solution)/shard_map/ppermute | solution.py:288
  33.6 3.2 %collective-permute-start.8 = (f32[4,80,128]{2,1,0:T(8,128)S(1)}, f32[4,80,128]{2,1,0:T(8,128)S(1)}, u32[]{:S(2)}, u32[]{:S(2)}) collective-permute-start(f32[4,80,128]{2,1,0:T(8,128)S(1)} %get-tuple-element.42), channel_id=1, source_target_pairs={{0,4},{1,3},{2,6},{3,1},{4,0},{5,7},{6,2},{7,5},{8,12},{9,11},{10,... | collective-permute-start | bytes 491528 | tf_op jit(solution)/shard_map/ppermute | solution.py:288
  36.8 1.7 %collective-permute-start.9 = (f32[4,80,128]{2,1,0:T(8,128)S(1)}, f32[4,80,128]{2,1,0:T(8,128)S(1)}, u32[]{:S(2)}, u32[]{:S(2)}) collective-permute-start(f32[4,80,128]{2,1,0:T(8,128)S(1)} %get-tuple-element.43), channel_id=1, source_target_pairs={{0,2},{1,5},{2,0},{3,7},{4,6},{5,1},{6,4},{7,3},{8,10},{9,13},{10,... | collective-permute-start | bytes 491528 | tf_op jit(solution)/shard_map/ppermute | solution.py:288
  38.5 2.7 %collective-permute-done.8.refs_3_ = f32[4,80,128]{2,1,0:T(8,128)S(1)} collective-permute-done((f32[4,80,128]{2,1,0:T(8,128)S(1)}, f32[4,80,128]{2,1,0:T(8,128)S(1)}, u32[]{:S(2)}, u32[]{:S(2)}) %collective-permute-start.8) | collective-permute-done | bytes 163872 | tf_op jit(solution)/shard_map/ppermute | solution.py:288
  42.3 2.7 %collective-permute-start.10 = (f32[160,128]{1,0:T(8,128)S(1)}, f32[160,128]{1,0:T(8,128)S(1)}, u32[]{:S(2)}, u32[]{:S(2)}) collective-permute-start(f32[160,128]{1,0:T(8,128)S(1)} %get-tuple-element.44), channel_id=1, source_target_pairs={{0,16},{1,17},{2,18},{3,19},{4,20},{5,21},{6,22},{7,23},{8,24},{9,... | collective-permute-start | bytes 245768 | tf_op jit(solution)/shard_map/ppermute | solution.py:288
  44.9 1.3 %collective-permute-start.11 = (f32[160,128]{1,0:T(8,128)S(1)}, f32[160,128]{1,0:T(8,128)S(1)}, u32[]{:S(2)}, u32[]{:S(2)}) collective-permute-start(f32[160,128]{1,0:T(8,128)S(1)} %get-tuple-element.45), channel_id=1, source_target_pairs={{0,24},{1,25},{2,26},{3,27},{4,28},{5,29},{6,30},{7,31},{8,16},{9,... | collective-permute-start | bytes 245768 | tf_op jit(solution)/shard_map/ppermute | solution.py:288
  46.4 5.5 %collective-permute-done.10.refs_5_ = f32[160,128]{1,0:T(8,128)S(1)} collective-permute-done((f32[160,128]{1,0:T(8,128)S(1)}, f32[160,128]{1,0:T(8,128)S(1)}, u32[]{:S(2)}, u32[]{:S(2)}) %collective-permute-start.10) | collective-permute-done | bytes 81952 | tf_op jit(solution)/shard_map/ppermute | solution.py:288
  52.6 1.1 %collective-permute-start.13 = (f32[160,128]{1,0:T(8,128)S(1)}, f32[160,128]{1,0:T(8,128)S(1)}, u32[]{:S(2)}, u32[]{:S(2)}) collective-permute-start(f32[160,128]{1,0:T(8,128)S(1)} %get-tuple-element.47.own_ref), channel_id=1, source_target_pairs={{0,2},{1,0},{2,6},{3,1},{4,12},{5,7},{6,4},{7,3},{8,16},{9,11},{10... | collective-permute-start | bytes 245768 | tf_op jit(solution)/shard_map/ppermute | solution.py:427
  53.7 4.0 %shard_map.94 = (f32[64,128]{1,0:T(8,128)S(1)}, f32[8,128]{1,0:T(8,128)S(1)}) custom-call(f32[32,128]{1,0:T(8,128)S(1)} %get-tuple-element.48.packed_ref, f32[8,128]{1,0:T(8,128)S(1)} %copy-done.2), custom_call_target="tpu_custom_call" | custom-call | tf_op jit(solution)/shard_map/pallas_call | solution.py:679
  57.8 8.5 %shard_map.95 = bf16[32,8,384]{2,1,0:T(8,128)(2,1)S(1)} custom-call(f32[160,128]{1,0:T(8,128)S(1)} %get-tuple-element.47.own_ref, f32[160,128]{1,0:T(8,128)S(1)} %collective-permute-done.13.left_ref, f32[32,128]{1,0:T(8,128)S(1)} %collective-permute-done.14.right_ref, f32[8,128]{1,0:T(8,128)S(1)} %copy-done.2, f32[64,128]{1,0:T(8,128)S(1)} %get-tuple-element.49.inv_ref, ...), custom_call_target="tpu_custom_call" | custom-call | tf_op jit(solution)/shard_map/pallas_call | solution.py:693
  66.3 13.5 %all_to_all.10.w_ref = bf16[32,8,384]{2,1,0:T(8,128)(2,1)S(1)} all-to-all(bf16[32,8,384]{2,1,0:T(8,128)(2,1)S(1)} %shard_map.95), channel_id=1, replica_groups=mesh['range'=32] {'range'}, dimensions={0} | all-to-all | bytes 393216 | tf_op jit(solution)/shard_map/all_to_all | solution.py:801
  79.8 2.0 %shard_map.96 = bf16[64,256]{1,0:T(8,128)(2,1)S(1)} custom-call(s32[32]{0:T(128)S(1)} %copy-done.5, s32[32]{0:T(128)S(1)} %copy-done.6, s32[32]{0:T(128)S(1)} %copy-done.7, s32[32]{0:T(128)S(1)} %bitcast.6, bf16[32,128,128]{2,1,0:T(8,128)(2,1)S(1)} %bitcast.5, bf16[32,2,32,128]{3,2,1,0:T(8,128)(2,1)S(1)} %get-tuple-element.35.refs_0_.upper_ref, ...), custom_call_target="tpu_custom_call" | custom-call | tf_op jit(solution)/shard_map/pallas_call | solution.py:759
  81.8 9.8 %all_to_all.11 = bf16[32,2,256]{2,1,0:T(2,128)(2,1)S(1)} all-to-all(bf16[32,2,256]{2,1,0:T(2,128)(2,1)S(1)} %reshape.17), channel_id=1, replica_groups=mesh['range'=32] {'range'}, dimensions={0} | all-to-all | bytes 65536 | tf_op jit(solution)/shard_map/all_to_all | solution.py:809
  (43 shorter events, 9.3 us)
Async XLA Ops:
  0.0 5.0 %copy-start.1 = (bf16[512,512]{1,0:T(8,128)(2,1)S(1)}, bf16[512,512]{1,0:T(8,128)(2,1)}, u32[]{:S(2)}) copy-start(bf16[512,512]{1,0:T(8,128)(2,1)} %constant.4.clone.dft_ref) | copy-start | bytes 1572868
  0.0 5.0 %copy-start.4 = (bf16[2,128]{1,0:T(2,128)(2,1)S(1)}, bf16[2,128]{1,0:T(2,128)(2,1)}, u32[]{:S(2)}) copy-start(bf16[2,128]{1,0:T(2,128)(2,1)} %rep_ref.1) | copy-start | bytes 1540
  2.4 13.6 %collective-permute-start.3 = (bf16[2,1024,128]{2,1,0:T(8,128)(2,1)}, bf16[2,1024,128]{2,1,0:T(8,128)(2,1)S(1)}, u32[]{:S(2)}, u32[]{:S(2)}) collective-permute-start(bf16[2,1024,128]{2,1,0:T(8,128)(2,1)} %get-tuple-element.36), channel_id=1, source_target_pairs={{1,0},{2,1},{3,2},{4,3},{5,4},{6,5},{7,6},{8,7},{9,8},{10,9},{11,1... | collective-permute-start | bytes 1572872 | tf_op jit(solution)/shard_map/ppermute | solution.py:780
  3.7 13.4 %collective-permute-start = (bf16[2,1024,128]{2,1,0:T(8,128)(2,1)}, bf16[2,1024,128]{2,1,0:T(8,128)(2,1)S(1)}, u32[]{:S(2)}, u32[]{:S(2)}) collective-permute-start(bf16[2,1024,128]{2,1,0:T(8,128)(2,1)} %get-tuple-element.31), channel_id=1, source_target_pairs={{1,0},{2,1},{3,2},{4,3},{5,4},{6,5},{7,6},{8,7},{9,8},{10,9},{11,1... | collective-permute-start | bytes 1572872 | tf_op jit(solution)/shard_map/ppermute | solution.py:780
  5.0 1.6 %copy-start = (bf16[2,64,32,256]{3,2,1,0:T(8,128)(2,1)S(1)}, bf16[2,64,32,256]{3,2,1,0:T(8,128)(2,1)}, u32[]{:S(2)}) copy-start(bf16[2,64,32,256]{3,2,1,0:T(8,128)(2,1)} %param.8) | copy-start | bytes 6291460
  6.6 0.7 copy-start.3
  11.4 3.0 %collective-permute-start.1 = (bf16[18,2,32,128]{3,2,1,0:T(8,128)(2,1)S(1)}, bf16[18,2,32,128]{3,2,1,0:T(8,128)(2,1)S(1)}, u32[]{:S(2)}, u32[]{:S(2)}) collective-permute-start(bf16[18,2,32,128]{3,2,1,0:T(8,128)(2,1)S(1)} %get-tuple-element.33), channel_id=1, source_target_pairs={{0,1},{1,0},{2,3},{3,2},{4,5},{5,4},{6,7},{7,6},{8,9},{9,8},{10,11... | collective-permute-start | bytes 884744 | tf_op jit(solution)/shard_map/ppermute | solution.py:288
  13.3 1.6 %collective-permute-start.2 = (bf16[18,2,32,128]{3,2,1,0:T(8,128)(2,1)S(1)}, bf16[18,2,32,128]{3,2,1,0:T(8,128)(2,1)S(1)}, u32[]{:S(2)}, u32[]{:S(2)}) collective-permute-start(bf16[18,2,32,128]{3,2,1,0:T(8,128)(2,1)S(1)} %get-tuple-element.34), channel_id=1, source_target_pairs={{0,1},{1,0},{2,3},{3,2},{4,5},{5,4},{6,7},{7,6},{8,9},{9,8},{10,11... | collective-permute-start | bytes 884744 | tf_op jit(solution)/shard_map/ppermute | solution.py:288
  16.7 5.2 %collective-permute-start.5 = (bf16[18,2,32,128]{3,2,1,0:T(8,128)(2,1)S(1)}, bf16[18,2,32,128]{3,2,1,0:T(8,128)(2,1)S(1)}, u32[]{:S(2)}, u32[]{:S(2)}) collective-permute-start(bf16[18,2,32,128]{3,2,1,0:T(8,128)(2,1)S(1)} %get-tuple-element.39), channel_id=1, source_target_pairs={{0,1},{1,0},{2,3},{3,2},{4,5},{5,4},{6,7},{7,6},{8,9},{9,8},{10,11... | collective-permute-start | bytes 884744 | tf_op jit(solution)/shard_map/ppermute | solution.py:288
  17.9 4.2 %collective-permute-start.4 = (bf16[18,2,32,128]{3,2,1,0:T(8,128)(2,1)S(1)}, bf16[18,2,32,128]{3,2,1,0:T(8,128)(2,1)S(1)}, u32[]{:S(2)}, u32[]{:S(2)}) collective-permute-start(bf16[18,2,32,128]{3,2,1,0:T(8,128)(2,1)S(1)} %get-tuple-element.38), channel_id=1, source_target_pairs={{0,1},{1,0},{2,3},{3,2},{4,5},{5,4},{6,7},{7,6},{8,9},{9,8},{10,11... | collective-permute-start | bytes 884744 | tf_op jit(solution)/shard_map/ppermute | solution.py:288
  23.4 9.1 %collective-permute-start.6 = (f32[8,80,128]{2,1,0:T(8,128)S(1)}, f32[8,80,128]{2,1,0:T(8,128)S(1)}, u32[]{:S(2)}, u32[]{:S(2)}) collective-permute-start(f32[8,80,128]{2,1,0:T(8,128)S(1)} %get-tuple-element.40), channel_id=1, source_target_pairs={{0,2},{1,5},{2,0},{3,7},{4,6},{5,1},{6,4},{7,3},{8,10},{9,13},{10,... | collective-permute-start | bytes 983048 | tf_op jit(solution)/shard_map/ppermute | solution.py:288
  25.8 7.6 %collective-permute-start.7 = (f32[8,80,128]{2,1,0:T(8,128)S(1)}, f32[8,80,128]{2,1,0:T(8,128)S(1)}, u32[]{:S(2)}, u32[]{:S(2)}) collective-permute-start(f32[8,80,128]{2,1,0:T(8,128)S(1)} %get-tuple-element.41), channel_id=1, source_target_pairs={{0,4},{1,3},{2,6},{3,1},{4,0},{5,7},{6,2},{7,5},{8,12},{9,11},{10,... | collective-permute-start | bytes 983048 | tf_op jit(solution)/shard_map/ppermute | solution.py:288
  33.6 7.6 %collective-permute-start.8 = (f32[4,80,128]{2,1,0:T(8,128)S(1)}, f32[4,80,128]{2,1,0:T(8,128)S(1)}, u32[]{:S(2)}, u32[]{:S(2)}) collective-permute-start(f32[4,80,128]{2,1,0:T(8,128)S(1)} %get-tuple-element.42), channel_id=1, source_target_pairs={{0,4},{1,3},{2,6},{3,1},{4,0},{5,7},{6,2},{7,5},{8,12},{9,11},{10,... | collective-permute-start | bytes 491528 | tf_op jit(solution)/shard_map/ppermute | solution.py:288
  36.8 5.3 %collective-permute-start.9 = (f32[4,80,128]{2,1,0:T(8,128)S(1)}, f32[4,80,128]{2,1,0:T(8,128)S(1)}, u32[]{:S(2)}, u32[]{:S(2)}) collective-permute-start(f32[4,80,128]{2,1,0:T(8,128)S(1)} %get-tuple-element.43), channel_id=1, source_target_pairs={{0,2},{1,5},{2,0},{3,7},{4,6},{5,1},{6,4},{7,3},{8,10},{9,13},{10,... | collective-permute-start | bytes 491528 | tf_op jit(solution)/shard_map/ppermute | solution.py:288
  42.3 11.5 %copy-start.2 = (f32[8,128]{1,0:T(8,128)S(1)}, f32[8,128]{1,0:T(8,128)}, u32[]{:S(2)}) copy-start(f32[8,128]{1,0:T(8,128)} %constant.5.clone.steer_ref) | copy-start | bytes 12292
  42.3 9.6 %collective-permute-start.10 = (f32[160,128]{1,0:T(8,128)S(1)}, f32[160,128]{1,0:T(8,128)S(1)}, u32[]{:S(2)}, u32[]{:S(2)}) collective-permute-start(f32[160,128]{1,0:T(8,128)S(1)} %get-tuple-element.44), channel_id=1, source_target_pairs={{0,16},{1,17},{2,18},{3,19},{4,20},{5,21},{6,22},{7,23},{8,24},{9,... | collective-permute-start | bytes 245768 | tf_op jit(solution)/shard_map/ppermute | solution.py:288
  44.9 7.0 %collective-permute-start.11 = (f32[160,128]{1,0:T(8,128)S(1)}, f32[160,128]{1,0:T(8,128)S(1)}, u32[]{:S(2)}, u32[]{:S(2)}) collective-permute-start(f32[160,128]{1,0:T(8,128)S(1)} %get-tuple-element.45), channel_id=1, source_target_pairs={{0,24},{1,25},{2,26},{3,27},{4,28},{5,29},{6,30},{7,31},{8,16},{9,... | collective-permute-start | bytes 245768 | tf_op jit(solution)/shard_map/ppermute | solution.py:288
  46.3 33.5 %copy-start.5 = (s32[32]{0:T(128)S(1)}, s32[32]{0:T(128)}, u32[]{:S(2)}) copy-start(s32[32]{0:T(128)} %bin_ref.1) | copy-start | bytes 388
  46.3 33.5 %copy-start.6 = (s32[32]{0:T(128)S(1)}, s32[32]{0:T(128)}, u32[]{:S(2)}) copy-start(s32[32]{0:T(128)} %block_ref.1) | copy-start | bytes 388
  46.3 33.5 %copy-start.7 = (s32[32]{0:T(128)S(1)}, s32[32]{0:T(128)}, u32[]{:S(2)}) copy-start(s32[32]{0:T(128)} %beam_ref.1) | copy-start | bytes 388
  46.3 33.5 %copy-start.8 = (s32[32,1]{0,1:T(1,128)S(1)}, s32[32,1]{0,1:T(1,128)}, u32[]{:S(2)}) copy-start(s32[32,1]{0,1:T(1,128)} %param.13) | copy-start | bytes 388
  46.3 6.2 %collective-permute-start.12 = (f32[160,128]{1,0:T(8,128)S(1)}, f32[160,128]{1,0:T(8,128)S(1)}, u32[]{:S(2)}, u32[]{:S(2)}) collective-permute-start(f32[160,128]{1,0:T(8,128)S(1)} %get-tuple-element.46), channel_id=1, source_target_pairs={{0,8},{1,9},{2,10},{3,11},{4,12},{5,13},{6,14},{7,15},{8,0},{9,1},... | collective-permute-start | bytes 245768 | tf_op jit(solution)/shard_map/ppermute | solution.py:288
  52.6 5.1 %collective-permute-start.13 = (f32[160,128]{1,0:T(8,128)S(1)}, f32[160,128]{1,0:T(8,128)S(1)}, u32[]{:S(2)}, u32[]{:S(2)}) collective-permute-start(f32[160,128]{1,0:T(8,128)S(1)} %get-tuple-element.47.own_ref), channel_id=1, source_target_pairs={{0,2},{1,0},{2,6},{3,1},{4,12},{5,7},{6,4},{7,3},{8,16},{9,11},{10... | collective-permute-start | bytes 245768 | tf_op jit(solution)/shard_map/ppermute | solution.py:427
  53.7 4.0 %collective-permute-start.14 = (f32[32,128]{1,0:T(8,128)S(1)}, f32[32,128]{1,0:T(8,128)S(1)}, u32[]{:S(2)}, u32[]{:S(2)}) collective-permute-start(f32[32,128]{1,0:T(8,128)S(1)} %get-tuple-element.48.packed_ref), channel_id=1, source_target_pairs={{0,1},{1,3},{2,0},{3,7},{4,6},{5,13},{6,2},{7,5},{8,10},{9,17},{10... | collective-permute-start | bytes 49160 | tf_op jit(solution)/shard_map/ppermute | solution.py:427

commit v3 on v1

--- a/solution.py
+++ b/solution.py
@@ -81,7 +81,7 @@
         in_specs=[hbm_spec()],
         out_specs=[vmem_spec()] * 3,
         scratch_shapes=[pltpu.SemaphoreType.DMA((8,))],
-        compiler_params=params(63),
+        compiler_params=params(61.5),
     )(raw)
 
 

time: 92.5 us -> 92.3 us (level)
    unnamed x18 -> x20, local copies, waits for them, and re-layouts: 2.3 us -> 1.76 us
  transfers between devices with their start and end apart: 15 -> 15, of which waited for: 9 -> 8; matrix products, arithmetic and copies ran while one was open for 0% -> 0% of each run, Pallas kernels for 14% -> 14%
where the time goes in v3:
time: 92.3 us; the launch traced here: 92.1 us
  Pallas kernels  27.5 us (30%)
  starting transfers between devices  23.4 us (25%)
  blocking collectives  23.1 us (25%)
  waiting for transfers between devices  15.4 us (17%)
  local copies, waits for them, and re-layouts  2.42 us (3%)
    ppermute x11, starting transfers between devices, partner(): lax.ppermute(value, 'range', [(i, i ^ bits[i & 1]) for i in range(count)])  19.7 us
    ppermute x11, waiting for transfers between devices, partner(): lax.ppermute(value, 'range', [(i, i ^ bits[i & 1]) for i in range(count)])  15.4 us
    all_to_all x1, blocking collectives, on_device(): lax.all_to_all(mine, 'range', split_axis=0, concat_axis=0, tiled=True, ax...  13.4 us
    all_to_all x1, blocking collectives, on_device(): lax.all_to_all(outgoing.reshape(devices, CAP, 2 * BLOCK), 'range', split_...  9.77 us
    pallas_call x1, Pallas kernels, solve_outer(): pl.pallas_call(functools.partial(outer_kernel, total), out_shape=jax.Shap...  8.54 us
    pallas_call x4, Pallas kernels, cross(): pl.pallas_call(functools.partial(cross_kernel, len(spectra)), out_shape=j...  4.26 us
    pallas_call x1, Pallas kernels, spectra_first(): pl.pallas_call(spectra_first_kernel, out_shape=[jax.ShapeDtypeStruct((pul...  4.12 us
    pallas_call x1, Pallas kernels, solve_middle(): pl.pallas_call(functools.partial(middle_kernel, total), out_shape=[jax.Sh...  4 us
  transfers between devices with their start and end apart: 15, of which 8 were waited for; matrix products, arithmetic and copies ran while one was open for 0% of the time, Pallas kernels for 14%

profile of v3, /device:TPU:0, one launch (start us, length us, event | category | flops | bytes accessed | tf_op | source)
XLA Modules:
  0.0 92.1 jit_solution(9349646913444543933)
XLA Ops:
  0.0 2.5 %shard_map.82 = (bf16[2,1024,128]{2,1,0:T(8,128)(2,1)}, bf16[2,1024,128]{2,1,0:T(8,128)(2,1)}, f32[8,128]{1,0:T(8,128)}) custom-call(bf16[2,2048,256]{2,1,0:T(8,128)(2,1)} %bitcast.3), custom_call_target="tpu_custom_call" | custom-call | tf_op jit(solution)/shard_map/pallas_call | solution.py:78
  2.5 1.3 %collective-permute-start.3 = (bf16[2,1024,128]{2,1,0:T(8,128)(2,1)}, bf16[2,1024,128]{2,1,0:T(8,128)(2,1)S(1)}, u32[]{:S(2)}, u32[]{:S(2)}) collective-permute-start(bf16[2,1024,128]{2,1,0:T(8,128)(2,1)} %get-tuple-element.36), channel_id=1, source_target_pairs={{1,0},{2,1},{3,2},{4,3},{5,4},{6,5},{7,6},{8,7},{9,8},{10,9},{11,1... | collective-permute-start | bytes 1572872 | tf_op jit(solution)/shard_map/ppermute | solution.py:773
  3.8 1.3 %collective-permute-start = (bf16[2,1024,128]{2,1,0:T(8,128)(2,1)}, bf16[2,1024,128]{2,1,0:T(8,128)(2,1)S(1)}, u32[]{:S(2)}, u32[]{:S(2)}) collective-permute-start(bf16[2,1024,128]{2,1,0:T(8,128)(2,1)} %get-tuple-element.31), channel_id=1, source_target_pairs={{1,0},{2,1},{3,2},{4,3},{5,4},{6,5},{7,6},{8,7},{9,8},{10,9},{11,1... | collective-permute-start | bytes 1572872 | tf_op jit(solution)/shard_map/ppermute | solution.py:773
  6.9 4.1 %shard_map.83 = (bf16[32,2,64,128]{3,2,1,0:T(8,128)(2,1)S(1)}, f32[2048,256]{1,0:T(8,128)S(1)}, bf16[2,256,256]{2,1,0:T(8,128)(2,1)S(1)}, bf16[18,2,32,128]{3,2,...) custom-call(bf16[2,2048,256]{2,1,0:T(8,128)(2,1)S(1)} %bitcast.4, bf16[2,128]{1,0:T(2,128)(2,1)S(1)} %copy-done.5, ...), custom_call_target="tpu_custom_call" | custom-call | flops 1 | bytes 1 | tf_op jit(solution)/shard_map/pallas_call | solution.py:199
  11.0 1.8 %collective-permute-start.1 = (bf16[18,2,32,128]{3,2,1,0:T(8,128)(2,1)S(1)}, bf16[18,2,32,128]{3,2,1,0:T(8,128)(2,1)S(1)}, u32[]{:S(2)}, u32[]{:S(2)}) collective-permute-start(bf16[18,2,32,128]{3,2,1,0:T(8,128)(2,1)S(1)} %get-tuple-element.33), channel_id=1, source_target_pairs={{0,1},{1,0},{2,3},{3,2},{4,5},{5,4},{6,7},{7,6},{8,9},{9,8},{10,11... | collective-permute-start | bytes 884744 | tf_op jit(solution)/shard_map/ppermute | solution.py:288
  14.4 1.1 %shard_map.85._.refs_2_ = f32[16,192,128]{2,1,0:T(8,128)S(1)} custom-call(bf16[18,2,32,128]{3,2,1,0:T(8,128)(2,1)S(1)} %collective-permute-done.1.refs_0_, bf16[18,2,32,128]{3,2,1,0:T(8,128)(2,1)S(1)} %collective-permute-done.2.refs_1_, f32[16,192,128]{2,1,0:T(8,128)S(1)} %shard_map.84.refs_2_), custom_call_target="tpu_custom_call" | custom-call | flops 1 | bytes 1 | tf_op jit(solution)/shard_map/pallas_call | solution.py:273
  17.4 3.5 %collective-permute-start.4 = (bf16[18,2,32,128]{3,2,1,0:T(8,128)(2,1)S(1)}, bf16[18,2,32,128]{3,2,1,0:T(8,128)(2,1)S(1)}, u32[]{:S(2)}, u32[]{:S(2)}) collective-permute-start(bf16[18,2,32,128]{3,2,1,0:T(8,128)(2,1)S(1)} %get-tuple-element.38), channel_id=1, source_target_pairs={{0,1},{1,0},{2,3},{3,2},{4,5},{5,4},{6,7},{7,6},{8,9},{9,8},{10,11... | collective-permute-start | bytes 884744 | tf_op jit(solution)/shard_map/ppermute | solution.py:288
  20.9 1.1 %shard_map.88.refs_2_ = f32[16,192,128]{2,1,0:T(8,128)S(1)} custom-call(bf16[32,2,32,128]{3,2,1,0:T(8,128)(2,1)S(1)} %get-tuple-element.35.refs_0_.upper_ref, bf16[32,2,32,128]{3,2,1,0:T(8,128)(2,1)S(1)} %get-tuple-element.37.refs_1_.lower_ref, f32[16,192,128]{2,1,0:T(8,128)S(1)} %shard_map.85._.refs_2_), custom_call_target="tpu_custom_call" | custom-call | flops 1 | bytes 1 | tf_op jit(solution)/shard_map/pallas_call | solution.py:273
  22.1 1.1 %shard_map.89.keep_ref.refs_0_ = f32[16,192,128]{2,1,0:T(8,128)S(1)} custom-call(bf16[18,2,32,128]{3,2,1,0:T(8,128)(2,1)S(1)} %collective-permute-done.4.refs_0_, bf16[18,2,32,128]{3,2,1,0:T(8,128)(2,1)S(1)} %collective-permute-done.5.refs_1_, f32[16,192,128]{2,1,0:T(8,128)S(1)} %shard_map.88.refs_2_), custom_call_target="tpu_custom_call" | custom-call | flops 1 | bytes 1 | tf_op jit(solution)/shard_map/pallas_call | solution.py:273
  23.5 2.4 %collective-permute-start.6 = (f32[8,80,128]{2,1,0:T(8,128)S(1)}, f32[8,80,128]{2,1,0:T(8,128)S(1)}, u32[]{:S(2)}, u32[]{:S(2)}) collective-permute-start(f32[8,80,128]{2,1,0:T(8,128)S(1)} %get-tuple-element.40), channel_id=1, source_target_pairs={{0,2},{1,5},{2,0},{3,7},{4,6},{5,1},{6,4},{7,3},{8,10},{9,13},{10,... | collective-permute-start | bytes 983048 | tf_op jit(solution)/shard_map/ppermute | solution.py:288
  25.9 2.4 %collective-permute-start.7 = (f32[8,80,128]{2,1,0:T(8,128)S(1)}, f32[8,80,128]{2,1,0:T(8,128)S(1)}, u32[]{:S(2)}, u32[]{:S(2)}) collective-permute-start(f32[8,80,128]{2,1,0:T(8,128)S(1)} %get-tuple-element.41), channel_id=1, source_target_pairs={{0,4},{1,3},{2,6},{3,1},{4,0},{5,7},{6,2},{7,5},{8,12},{9,11},{10,... | collective-permute-start | bytes 983048 | tf_op jit(solution)/shard_map/ppermute | solution.py:288
  28.3 4.3 %collective-permute-done.6.a1_ref.refs_1_ = f32[8,80,128]{2,1,0:T(8,128)S(1)} collective-permute-done((f32[8,80,128]{2,1,0:T(8,128)S(1)}, f32[8,80,128]{2,1,0:T(8,128)S(1)}, u32[]{:S(2)}, u32[]{:S(2)}) %collective-permute-start.6) | collective-permute-done | bytes 327712 | tf_op jit(solution)/shard_map/ppermute | solution.py:288
  33.7 3.2 %collective-permute-start.8 = (f32[4,80,128]{2,1,0:T(8,128)S(1)}, f32[4,80,128]{2,1,0:T(8,128)S(1)}, u32[]{:S(2)}, u32[]{:S(2)}) collective-permute-start(f32[4,80,128]{2,1,0:T(8,128)S(1)} %get-tuple-element.42), channel_id=1, source_target_pairs={{0,4},{1,3},{2,6},{3,1},{4,0},{5,7},{6,2},{7,5},{8,12},{9,11},{10,... | collective-permute-start | bytes 491528 | tf_op jit(solution)/shard_map/ppermute | solution.py:288
  36.9 1.7 %collective-permute-start.9 = (f32[4,80,128]{2,1,0:T(8,128)S(1)}, f32[4,80,128]{2,1,0:T(8,128)S(1)}, u32[]{:S(2)}, u32[]{:S(2)}) collective-permute-start(f32[4,80,128]{2,1,0:T(8,128)S(1)} %get-tuple-element.43), channel_id=1, source_target_pairs={{0,2},{1,5},{2,0},{3,7},{4,6},{5,1},{6,4},{7,3},{8,10},{9,13},{10,... | collective-permute-start | bytes 491528 | tf_op jit(solution)/shard_map/ppermute | solution.py:288
  38.6 2.7 %collective-permute-done.8.refs_3_ = f32[4,80,128]{2,1,0:T(8,128)S(1)} collective-permute-done((f32[4,80,128]{2,1,0:T(8,128)S(1)}, f32[4,80,128]{2,1,0:T(8,128)S(1)}, u32[]{:S(2)}, u32[]{:S(2)}) %collective-permute-start.8) | collective-permute-done | bytes 163872 | tf_op jit(solution)/shard_map/ppermute | solution.py:288
  42.4 2.6 %collective-permute-start.10 = (f32[160,128]{1,0:T(8,128)S(1)}, f32[160,128]{1,0:T(8,128)S(1)}, u32[]{:S(2)}, u32[]{:S(2)}) collective-permute-start(f32[160,128]{1,0:T(8,128)S(1)} %get-tuple-element.44), channel_id=1, source_target_pairs={{0,16},{1,17},{2,18},{3,19},{4,20},{5,21},{6,22},{7,23},{8,24},{9,... | collective-permute-start | bytes 245768 | tf_op jit(solution)/shard_map/ppermute | solution.py:288
  45.0 1.4 %collective-permute-start.11 = (f32[160,128]{1,0:T(8,128)S(1)}, f32[160,128]{1,0:T(8,128)S(1)}, u32[]{:S(2)}, u32[]{:S(2)}) collective-permute-start(f32[160,128]{1,0:T(8,128)S(1)} %get-tuple-element.45), channel_id=1, source_target_pairs={{0,24},{1,25},{2,26},{3,27},{4,28},{5,29},{6,30},{7,31},{8,16},{9,... | collective-permute-start | bytes 245768 | tf_op jit(solution)/shard_map/ppermute | solution.py:288
  46.5 5.4 %collective-permute-done.10.refs_5_ = f32[160,128]{1,0:T(8,128)S(1)} collective-permute-done((f32[160,128]{1,0:T(8,128)S(1)}, f32[160,128]{1,0:T(8,128)S(1)}, u32[]{:S(2)}, u32[]{:S(2)}) %collective-permute-start.10) | collective-permute-done | bytes 81952 | tf_op jit(solution)/shard_map/ppermute | solution.py:288
  52.6 1.1 %collective-permute-start.13 = (f32[160,128]{1,0:T(8,128)S(1)}, f32[160,128]{1,0:T(8,128)S(1)}, u32[]{:S(2)}, u32[]{:S(2)}) collective-permute-start(f32[160,128]{1,0:T(8,128)S(1)} %get-tuple-element.47.own_ref), channel_id=1, source_target_pairs={{0,2},{1,0},{2,6},{3,1},{4,12},{5,7},{6,4},{7,3},{8,16},{9,11},{10... | collective-permute-start | bytes 245768 | tf_op jit(solution)/shard_map/ppermute | solution.py:427
  53.7 4.0 %shard_map.94 = (f32[64,128]{1,0:T(8,128)S(1)}, f32[8,128]{1,0:T(8,128)S(1)}) custom-call(f32[32,128]{1,0:T(8,128)S(1)} %get-tuple-element.48.packed_ref, f32[8,128]{1,0:T(8,128)S(1)} %copy-done.3), custom_call_target="tpu_custom_call" | custom-call | tf_op jit(solution)/shard_map/pallas_call | solution.py:679
  57.7 8.5 %shard_map.95 = bf16[32,8,384]{2,1,0:T(8,128)(2,1)S(1)} custom-call(f32[160,128]{1,0:T(8,128)S(1)} %get-tuple-element.47.own_ref, f32[160,128]{1,0:T(8,128)S(1)} %collective-permute-done.13.left_ref, f32[32,128]{1,0:T(8,128)S(1)} %collective-permute-done.14.right_ref, f32[8,128]{1,0:T(8,128)S(1)} %copy-done.3, f32[64,128]{1,0:T(8,128)S(1)} %get-tuple-element.49.inv_ref, ...), custom_call_target="tpu_custom_call" | custom-call | tf_op jit(solution)/shard_map/pallas_call | solution.py:693
  66.3 13.4 %all_to_all.10.w_ref = bf16[32,8,384]{2,1,0:T(8,128)(2,1)S(1)} all-to-all(bf16[32,8,384]{2,1,0:T(8,128)(2,1)S(1)} %shard_map.95), channel_id=1, replica_groups=mesh['range'=32] {'range'}, dimensions={0} | all-to-all | bytes 393216 | tf_op jit(solution)/shard_map/all_to_all | solution.py:794
  79.7 2.0 %shard_map.96 = bf16[64,256]{1,0:T(8,128)(2,1)S(1)} custom-call(s32[32]{0:T(128)S(1)} %copy-done.6, s32[32]{0:T(128)S(1)} %copy-done.7, s32[32]{0:T(128)S(1)} %copy-done.8, s32[32]{0:T(128)S(1)} %bitcast.6, bf16[32,128,128]{2,1,0:T(8,128)(2,1)S(1)} %bitcast.5, bf16[32,2,32,128]{3,2,1,0:T(8,128)(2,1)S(1)} %get-tuple-element.35.refs_0_.upper_ref, ...), custom_call_target="tpu_custom_call" | custom-call | tf_op jit(solution)/shard_map/pallas_call | solution.py:752
  81.6 9.8 %all_to_all.11 = bf16[32,2,256]{2,1,0:T(2,128)(2,1)S(1)} all-to-all(bf16[32,2,256]{2,1,0:T(2,128)(2,1)S(1)} %reshape.17), channel_id=1, replica_groups=mesh['range'=32] {'range'}, dimensions={0} | all-to-all | bytes 65536 | tf_op jit(solution)/shard_map/all_to_all | solution.py:802
  (45 shorter events, 9.3 us)
Async XLA Ops:
  0.0 5.1 %copy-start = (bf16[2,64,32,256]{3,2,1,0:T(8,128)(2,1)S(1)}, bf16[2,64,32,256]{3,2,1,0:T(8,128)(2,1)}, u32[]{:S(2)}) copy-start(bf16[2,64,32,256]{3,2,1,0:T(8,128)(2,1)} %param.8) | copy-start | bytes 6291460
  0.0 5.1 %copy-start.5 = (bf16[2,128]{1,0:T(2,128)(2,1)S(1)}, bf16[2,128]{1,0:T(2,128)(2,1)}, u32[]{:S(2)}) copy-start(bf16[2,128]{1,0:T(2,128)(2,1)} %rep_ref.1) | copy-start | bytes 1540
  2.5 13.0 %collective-permute-start.3 = (bf16[2,1024,128]{2,1,0:T(8,128)(2,1)}, bf16[2,1024,128]{2,1,0:T(8,128)(2,1)S(1)}, u32[]{:S(2)}, u32[]{:S(2)}) collective-permute-start(bf16[2,1024,128]{2,1,0:T(8,128)(2,1)} %get-tuple-element.36), channel_id=1, source_target_pairs={{1,0},{2,1},{3,2},{4,3},{5,4},{6,5},{7,6},{8,7},{9,8},{10,9},{11,1... | collective-permute-start | bytes 1572872 | tf_op jit(solution)/shard_map/ppermute | solution.py:773
  3.8 12.9 %collective-permute-start = (bf16[2,1024,128]{2,1,0:T(8,128)(2,1)}, bf16[2,1024,128]{2,1,0:T(8,128)(2,1)S(1)}, u32[]{:S(2)}, u32[]{:S(2)}) collective-permute-start(bf16[2,1024,128]{2,1,0:T(8,128)(2,1)} %get-tuple-element.31), channel_id=1, source_target_pairs={{1,0},{2,1},{3,2},{4,3},{5,4},{6,5},{7,6},{8,7},{9,8},{10,9},{11,1... | collective-permute-start | bytes 1572872 | tf_op jit(solution)/shard_map/ppermute | solution.py:773
  5.1 1.0 %copy-start.1 = (bf16[512,512]{1,0:T(8,128)(2,1)S(1)}, bf16[512,512]{1,0:T(8,128)(2,1)}, u32[]{:S(2)}) copy-start(bf16[512,512]{1,0:T(8,128)(2,1)} %constant.4.clone.dft_ref) | copy-start | bytes 1572868
  11.0 3.0 %collective-permute-start.1 = (bf16[18,2,32,128]{3,2,1,0:T(8,128)(2,1)S(1)}, bf16[18,2,32,128]{3,2,1,0:T(8,128)(2,1)S(1)}, u32[]{:S(2)}, u32[]{:S(2)}) collective-permute-start(bf16[18,2,32,128]{3,2,1,0:T(8,128)(2,1)S(1)} %get-tuple-element.33), channel_id=1, source_target_pairs={{0,1},{1,0},{2,3},{3,2},{4,5},{5,4},{6,7},{7,6},{8,9},{9,8},{10,11... | collective-permute-start | bytes 884744 | tf_op jit(solution)/shard_map/ppermute | solution.py:288
  12.8 1.6 %collective-permute-start.2 = (bf16[18,2,32,128]{3,2,1,0:T(8,128)(2,1)S(1)}, bf16[18,2,32,128]{3,2,1,0:T(8,128)(2,1)S(1)}, u32[]{:S(2)}, u32[]{:S(2)}) collective-permute-start(bf16[18,2,32,128]{3,2,1,0:T(8,128)(2,1)S(1)} %get-tuple-element.34), channel_id=1, source_target_pairs={{0,1},{1,0},{2,3},{3,2},{4,5},{5,4},{6,7},{7,6},{8,9},{9,8},{10,11... | collective-permute-start | bytes 884744 | tf_op jit(solution)/shard_map/ppermute | solution.py:288
  13.9 1.6 %copy-start.2 = (bf16[512,512]{1,0:T(8,128)(2,1)S(1)}, bf16[512,512]{1,0:T(8,128)(2,1)}, u32[]{:S(2)}) copy-start(bf16[512,512]{1,0:T(8,128)(2,1)} %constant.4.clone.dft_ref) | copy-start | bytes 1572868
  16.3 5.8 %collective-permute-start.5 = (bf16[18,2,32,128]{3,2,1,0:T(8,128)(2,1)S(1)}, bf16[18,2,32,128]{3,2,1,0:T(8,128)(2,1)S(1)}, u32[]{:S(2)}, u32[]{:S(2)}) collective-permute-start(bf16[18,2,32,128]{3,2,1,0:T(8,128)(2,1)S(1)} %get-tuple-element.39), channel_id=1, source_target_pairs={{0,1},{1,0},{2,3},{3,2},{4,5},{5,4},{6,7},{7,6},{8,9},{9,8},{10,11... | collective-permute-start | bytes 884744 | tf_op jit(solution)/shard_map/ppermute | solution.py:288
  17.4 4.7 %collective-permute-start.4 = (bf16[18,2,32,128]{3,2,1,0:T(8,128)(2,1)S(1)}, bf16[18,2,32,128]{3,2,1,0:T(8,128)(2,1)S(1)}, u32[]{:S(2)}, u32[]{:S(2)}) collective-permute-start(bf16[18,2,32,128]{3,2,1,0:T(8,128)(2,1)S(1)} %get-tuple-element.38), channel_id=1, source_target_pairs={{0,1},{1,0},{2,3},{3,2},{4,5},{5,4},{6,7},{7,6},{8,9},{9,8},{10,11... | collective-permute-start | bytes 884744 | tf_op jit(solution)/shard_map/ppermute | solution.py:288
  23.5 9.1 %collective-permute-start.6 = (f32[8,80,128]{2,1,0:T(8,128)S(1)}, f32[8,80,128]{2,1,0:T(8,128)S(1)}, u32[]{:S(2)}, u32[]{:S(2)}) collective-permute-start(f32[8,80,128]{2,1,0:T(8,128)S(1)} %get-tuple-element.40), channel_id=1, source_target_pairs={{0,2},{1,5},{2,0},{3,7},{4,6},{5,1},{6,4},{7,3},{8,10},{9,13},{10,... | collective-permute-start | bytes 983048 | tf_op jit(solution)/shard_map/ppermute | solution.py:288
  25.9 7.6 %collective-permute-start.7 = (f32[8,80,128]{2,1,0:T(8,128)S(1)}, f32[8,80,128]{2,1,0:T(8,128)S(1)}, u32[]{:S(2)}, u32[]{:S(2)}) collective-permute-start(f32[8,80,128]{2,1,0:T(8,128)S(1)} %get-tuple-element.41), channel_id=1, source_target_pairs={{0,4},{1,3},{2,6},{3,1},{4,0},{5,7},{6,2},{7,5},{8,12},{9,11},{10,... | collective-permute-start | bytes 983048 | tf_op jit(solution)/shard_map/ppermute | solution.py:288
  33.7 7.6 %collective-permute-start.8 = (f32[4,80,128]{2,1,0:T(8,128)S(1)}, f32[4,80,128]{2,1,0:T(8,128)S(1)}, u32[]{:S(2)}, u32[]{:S(2)}) collective-permute-start(f32[4,80,128]{2,1,0:T(8,128)S(1)} %get-tuple-element.42), channel_id=1, source_target_pairs={{0,4},{1,3},{2,6},{3,1},{4,0},{5,7},{6,2},{7,5},{8,12},{9,11},{10,... | collective-permute-start | bytes 491528 | tf_op jit(solution)/shard_map/ppermute | solution.py:288
  36.9 5.3 %collective-permute-start.9 = (f32[4,80,128]{2,1,0:T(8,128)S(1)}, f32[4,80,128]{2,1,0:T(8,128)S(1)}, u32[]{:S(2)}, u32[]{:S(2)}) collective-permute-start(f32[4,80,128]{2,1,0:T(8,128)S(1)} %get-tuple-element.43), channel_id=1, source_target_pairs={{0,2},{1,5},{2,0},{3,7},{4,6},{5,1},{6,4},{7,3},{8,10},{9,13},{10,... | collective-permute-start | bytes 491528 | tf_op jit(solution)/shard_map/ppermute | solution.py:288
  42.3 11.4 %copy-start.3 = (f32[8,128]{1,0:T(8,128)S(1)}, f32[8,128]{1,0:T(8,128)}, u32[]{:S(2)}) copy-start(f32[8,128]{1,0:T(8,128)} %constant.5.clone.steer_ref) | copy-start | bytes 12292
  42.4 9.5 %collective-permute-start.10 = (f32[160,128]{1,0:T(8,128)S(1)}, f32[160,128]{1,0:T(8,128)S(1)}, u32[]{:S(2)}, u32[]{:S(2)}) collective-permute-start(f32[160,128]{1,0:T(8,128)S(1)} %get-tuple-element.44), channel_id=1, source_target_pairs={{0,16},{1,17},{2,18},{3,19},{4,20},{5,21},{6,22},{7,23},{8,24},{9,... | collective-permute-start | bytes 245768 | tf_op jit(solution)/shard_map/ppermute | solution.py:288
  45.0 6.8 %collective-permute-start.11 = (f32[160,128]{1,0:T(8,128)S(1)}, f32[160,128]{1,0:T(8,128)S(1)}, u32[]{:S(2)}, u32[]{:S(2)}) collective-permute-start(f32[160,128]{1,0:T(8,128)S(1)} %get-tuple-element.45), channel_id=1, source_target_pairs={{0,24},{1,25},{2,26},{3,27},{4,28},{5,29},{6,30},{7,31},{8,16},{9,... | collective-permute-start | bytes 245768 | tf_op jit(solution)/shard_map/ppermute | solution.py:288
  46.4 33.3 %copy-start.6 = (s32[32]{0:T(128)S(1)}, s32[32]{0:T(128)}, u32[]{:S(2)}) copy-start(s32[32]{0:T(128)} %bin_ref.1) | copy-start | bytes 388
  46.4 33.3 %copy-start.7 = (s32[32]{0:T(128)S(1)}, s32[32]{0:T(128)}, u32[]{:S(2)}) copy-start(s32[32]{0:T(128)} %block_ref.1) | copy-start | bytes 388
  46.4 33.3 %copy-start.8 = (s32[32]{0:T(128)S(1)}, s32[32]{0:T(128)}, u32[]{:S(2)}) copy-start(s32[32]{0:T(128)} %beam_ref.1) | copy-start | bytes 388
  46.4 33.3 %copy-start.9 = (s32[32,1]{0,1:T(1,128)S(1)}, s32[32,1]{0,1:T(1,128)}, u32[]{:S(2)}) copy-start(s32[32,1]{0,1:T(1,128)} %param.13) | copy-start | bytes 388
  46.4 6.1 %collective-permute-start.12 = (f32[160,128]{1,0:T(8,128)S(1)}, f32[160,128]{1,0:T(8,128)S(1)}, u32[]{:S(2)}, u32[]{:S(2)}) collective-permute-start(f32[160,128]{1,0:T(8,128)S(1)} %get-tuple-element.46), channel_id=1, source_target_pairs={{0,8},{1,9},{2,10},{3,11},{4,12},{5,13},{6,14},{7,15},{8,0},{9,1},... | collective-permute-start | bytes 245768 | tf_op jit(solution)/shard_map/ppermute | solution.py:288
  52.6 5.1 %collective-permute-start.13 = (f32[160,128]{1,0:T(8,128)S(1)}, f32[160,128]{1,0:T(8,128)S(1)}, u32[]{:S(2)}, u32[]{:S(2)}) collective-permute-start(f32[160,128]{1,0:T(8,128)S(1)} %get-tuple-element.47.own_ref), channel_id=1, source_target_pairs={{0,2},{1,0},{2,6},{3,1},{4,12},{5,7},{6,4},{7,3},{8,16},{9,11},{10... | collective-permute-start | bytes 245768 | tf_op jit(solution)/shard_map/ppermute | solution.py:427
  53.7 4.0 %collective-permute-start.14 = (f32[32,128]{1,0:T(8,128)S(1)}, f32[32,128]{1,0:T(8,128)S(1)}, u32[]{:S(2)}, u32[]{:S(2)}) collective-permute-start(f32[32,128]{1,0:T(8,128)S(1)} %get-tuple-element.48.packed_ref), channel_id=1, source_target_pairs={{0,1},{1,3},{2,0},{3,7},{4,6},{5,13},{6,2},{7,5},{8,10},{9,17},{10... | collective-permute-start | bytes 49160 | tf_op jit(solution)/shard_map/ppermute | solution.py:427
  (1 other events, 0.7 us)

commit v4 on v3

--- a/solution.py
+++ b/solution.py
@@ -242,7 +242,7 @@
     def write(e, block):
         out_ref[e] = block if before_ref is None else block + before_ref[e]
 
-    @pl.loop(0, count // 2, unroll=2)
+    @pl.loop(0, count // 2, unroll=8)
     def _(step):
         e = step * 2
         each = []
@@ -608,8 +608,7 @@
     t_ref[...] = mul(steer_ref[...], inverse)
 
 
-def outer_kernel(total, own_ref, left_ref, right_ref, steer_ref, inv_ref, t_ref, out_ref,
-                 work, keep, small):
+def outer_kernel(total, own_ref, left_ref, right_ref, steer_ref, inv_ref, t_ref, out_ref):
     chans = inv_ref.shape[0]
     scale = F32(1.0 / total)
     half = chans // 2
@@ -625,46 +624,29 @@
     g_right, g_left = both[:chans], both[chans:]
     by_left = mul(jnp.concatenate([g_left, g_right, t], axis=0), ml)
     by_right = mul_conj(jnp.concatenate([g_right, t], axis=0), rm)
-    work[...] = hermitian(m_left, across[:chans, :chans]) - by_left[:chans]
-    keep[0] = rl - by_left[chans : 2 * chans]
-    keep[1] = hermitian(m_right, across[chans:, :chans]) - by_right[:chans]
-    keep[2] = g_left
-    keep[3] = g_right
-    small[0] = -by_left[2 * chans :]
-    small[1] = -by_right[chans:]
-
-    @pl.loop(0, 2)
-    def _(stage):
-        work[...] = invert(work[...])
-
-        @pl.when(stage == 0)
-        def _():
-            s_rl = keep[0]
-            both = mul(jnp.concatenate([s_rl, small[0]], axis=0), work[...])
-            back = mul_conj(both, s_rl)
-            work[...] = keep[1] - back[:chans]
-            small[1] = small[1] - back[chans:]
-            middle = mul(both, keep[2])
-            keep[0] = both[:chans]
-            small[0] = both[chans:]
-            keep[3] = keep[3] - middle[:chans]
-            small[2] = t_ref[...] - middle[chans:]
-
-        @pl.when(stage == 1)
-        def _():
-            y_right = mul(small[1], work[...])
-            factors = jnp.concatenate([embed(keep[0]), embed(keep[3])], axis=1)
-            both = jnp.dot(
-                y_right, factors, precision=lax.Precision.HIGHEST, preferred_element_type=F32
-            )
-            y_left = small[0] - both[:, : 2 * chans]
-            y_mid = small[2] - both[:, 2 * chans :]
-            quad = jnp.sum(steer_ref[...] * y_mid, axis=1, keepdims=True)
-            y = jnp.concatenate([y_left, y_mid, y_right], axis=1) / jnp.sqrt(quad)
-            real_lane = lax.rem(iota(y.shape, 1), 2 * chans) < chans
-            mine = jnp.where(real_lane, y, -y).astype(BF16)
-            for c in range(out_ref.shape[0]):
-                out_ref[c] = mine
+    s_ll = hermitian(m_left, across[:chans, :chans]) - by_left[:chans]
+    s_rl = rl - by_left[chans : 2 * chans]
+    s_rr = hermitian(m_right, across[chans:, :chans]) - by_right[:chans]
+
+    both = mul(jnp.concatenate([s_rl, -by_left[2 * chans :]], axis=0), invert(s_ll))
+    back = mul_conj(both, s_rl)
+    middle = mul(both, g_left)
+    k, y_left = both[:chans], both[chans:]
+    q = g_right - middle[:chans]
+
+    y_right = mul(-by_right[chans:] - back[chans:], invert(s_rr - back[:chans]))
+    both = jnp.dot(
+        y_right, jnp.concatenate([embed(k), embed(q)], axis=1),
+        precision=lax.Precision.HIGHEST, preferred_element_type=F32,
+    )
+    y_left = y_left - both[:, : 2 * chans]
+    y_mid = t - middle[chans:] - both[:, 2 * chans :]
+    quad = jnp.sum(steer_ref[...] * y_mid, axis=1, keepdims=True)
+    y = jnp.concatenate([y_left, y_mid, y_right], axis=1) / jnp.sqrt(quad)
+    real_lane = lax.rem(iota(y.shape, 1), 2 * chans) < chans
+    mine = jnp.where(real_lane, y, -y).astype(BF16)
+    for c in range(out_ref.shape[0]):
+        out_ref[c] = mine
 
 
 def steering(chans):
@@ -695,11 +677,6 @@
         out_shape=jax.ShapeDtypeStruct((copies, BEAMS, 3 * wide), BF16),
         in_specs=[vmem_spec()] * 6,
         out_specs=vmem_spec(),
-        scratch_shapes=[
-            pltpu.VMEM((chans, wide), F32),
-            pltpu.VMEM((4, chans, wide), F32),
-            pltpu.VMEM((3, BEAMS, wide), F32),
-        ],
         compiler_params=params(),
     )(own, left, right, steer, inverse, t)
 

time: 92.3 us -> 94.2 us (1.021)
  waiting for transfers between devices: 15.4 us -> 16.6 us
    pallas_call x1, Pallas kernels: 8.54 us -> 11 us  [solve_outer(): pl.pallas_call(functools.partial(outer_kernel, total), out_shape=jax.Shap...]
    pallas_call x4, Pallas kernels: 4.26 us -> 1.88 us  [cross(): pl.pallas_call(functools.partial(cross_kernel, len(spectra)), out_shape=j...]
    ppermute x11, waiting for transfers between devices: 15.4 us -> 16.6 us  [partner(): lax.ppermute(value, 'range', [(i, i ^ bits[i & 1]) for i in range(count)])]
  transfers between devices with their start and end apart: 15 -> 15, of which waited for: 8 -> 9; matrix products, arithmetic and copies ran while one was open for 0% -> 0% of each run, Pallas kernels for 14% -> 12%
where the time goes in v4:
time: 94.2 us; the launch traced here: 94 us
  Pallas kernels  27.6 us (29%)
  starting transfers between devices  23.9 us (25%)
  blocking collectives  23.1 us (25%)
  waiting for transfers between devices  16.6 us (18%)
  local copies, waits for them, and re-layouts  2.42 us (3%)
    ppermute x11, starting transfers between devices, partner(): lax.ppermute(value, 'range', [(i, i ^ bits[i & 1]) for i in range(count)])  20.3 us
    ppermute x11, waiting for transfers between devices, partner(): lax.ppermute(value, 'range', [(i, i ^ bits[i & 1]) for i in range(count)])  16.6 us
    all_to_all x1, blocking collectives, on_device(): lax.all_to_all(mine, 'range', split_axis=0, concat_axis=0, tiled=True, ax...  13.4 us
    pallas_call x1, Pallas kernels, solve_outer(): pl.pallas_call(functools.partial(outer_kernel, total), out_shape=jax.Shap...  11 us
    all_to_all x1, blocking collectives, on_device(): lax.all_to_all(outgoing.reshape(devices, CAP, 2 * BLOCK), 'range', split_...  9.77 us
    pallas_call x1, Pallas kernels, spectra_first(): pl.pallas_call(spectra_first_kernel, out_shape=[jax.ShapeDtypeStruct((pul...  4.12 us
    pallas_call x1, Pallas kernels, solve_middle(): pl.pallas_call(functools.partial(middle_kernel, total), out_shape=[jax.Sh...  4 us
    ppermute x2, starting transfers between devices, on_device(): halos = [lax.ppermute(value, 'range', before) for value in slices]  2.58 us
  transfers between devices with their start and end apart: 15, of which 9 were waited for; matrix products, arithmetic and copies ran while one was open for 0% of the time, Pallas kernels for 12%

profile of v4, /device:TPU:0, one launch (start us, length us, event | category | flops | bytes accessed | tf_op | source)
XLA Modules:
  0.0 94.0 jit_solution(2331976822105091480)
XLA Ops:
  0.0 2.5 %shard_map.82 = (bf16[2,1024,128]{2,1,0:T(8,128)(2,1)}, bf16[2,1024,128]{2,1,0:T(8,128)(2,1)}, f32[8,128]{1,0:T(8,128)}) custom-call(bf16[2,2048,256]{2,1,0:T(8,128)(2,1)} %bitcast.3), custom_call_target="tpu_custom_call" | custom-call | tf_op jit(solution)/shard_map/pallas_call | solution.py:78
  2.5 1.3 %collective-permute-start.3 = (bf16[2,1024,128]{2,1,0:T(8,128)(2,1)}, bf16[2,1024,128]{2,1,0:T(8,128)(2,1)S(1)}, u32[]{:S(2)}, u32[]{:S(2)}) collective-permute-start(bf16[2,1024,128]{2,1,0:T(8,128)(2,1)} %get-tuple-element.36), channel_id=1, source_target_pairs={{1,0},{2,1},{3,2},{4,3},{5,4},{6,5},{7,6},{8,7},{9,8},{10,9},{11,1... | collective-permute-start | bytes 1572872 | tf_op jit(solution)/shard_map/ppermute | solution.py:750
  3.8 1.3 %collective-permute-start = (bf16[2,1024,128]{2,1,0:T(8,128)(2,1)}, bf16[2,1024,128]{2,1,0:T(8,128)(2,1)S(1)}, u32[]{:S(2)}, u32[]{:S(2)}) collective-permute-start(bf16[2,1024,128]{2,1,0:T(8,128)(2,1)} %get-tuple-element.31), channel_id=1, source_target_pairs={{1,0},{2,1},{3,2},{4,3},{5,4},{6,5},{7,6},{8,7},{9,8},{10,9},{11,1... | collective-permute-start | bytes 1572872 | tf_op jit(solution)/shard_map/ppermute | solution.py:750
  5.1 1.0 %copy-done.1 = bf16[512,512]{1,0:T(8,128)(2,1)S(1)} copy-done((bf16[512,512]{1,0:T(8,128)(2,1)S(1)}, bf16[512,512]{1,0:T(8,128)(2,1)}, u32[]{:S(2)}) %copy-start.1) | copy-done | bytes 524312
  6.9 4.1 %shard_map.83 = (bf16[32,2,64,128]{3,2,1,0:T(8,128)(2,1)S(1)}, f32[2048,256]{1,0:T(8,128)S(1)}, bf16[2,256,256]{2,1,0:T(8,128)(2,1)S(1)}, bf16[18,2,32,128]{3,2,...) custom-call(bf16[2,2048,256]{2,1,0:T(8,128)(2,1)S(1)} %bitcast.4, bf16[2,128]{1,0:T(2,128)(2,1)S(1)} %copy-done.5, ...), custom_call_target="tpu_custom_call" | custom-call | flops 1 | bytes 1 | tf_op jit(solution)/shard_map/pallas_call | solution.py:199
  11.0 1.8 %collective-permute-start.1 = (bf16[18,2,32,128]{3,2,1,0:T(8,128)(2,1)S(1)}, bf16[18,2,32,128]{3,2,1,0:T(8,128)(2,1)S(1)}, u32[]{:S(2)}, u32[]{:S(2)}) collective-permute-start(bf16[18,2,32,128]{3,2,1,0:T(8,128)(2,1)S(1)} %get-tuple-element.33), channel_id=1, source_target_pairs={{0,1},{1,0},{2,3},{3,2},{4,5},{5,4},{6,7},{7,6},{8,9},{9,8},{10,11... | collective-permute-start | bytes 884744 | tf_op jit(solution)/shard_map/ppermute | solution.py:288
  16.8 4.1 %collective-permute-start.4 = (bf16[18,2,32,128]{3,2,1,0:T(8,128)(2,1)S(1)}, bf16[18,2,32,128]{3,2,1,0:T(8,128)(2,1)S(1)}, u32[]{:S(2)}, u32[]{:S(2)}) collective-permute-start(bf16[18,2,32,128]{3,2,1,0:T(8,128)(2,1)S(1)} %get-tuple-element.38), channel_id=1, source_target_pairs={{0,1},{1,0},{2,3},{3,2},{4,5},{5,4},{6,7},{7,6},{8,9},{9,8},{10,11... | collective-permute-start | bytes 884744 | tf_op jit(solution)/shard_map/ppermute | solution.py:288
  22.9 2.4 %collective-permute-start.6 = (f32[8,80,128]{2,1,0:T(8,128)S(1)}, f32[8,80,128]{2,1,0:T(8,128)S(1)}, u32[]{:S(2)}, u32[]{:S(2)}) collective-permute-start(f32[8,80,128]{2,1,0:T(8,128)S(1)} %get-tuple-element.40), channel_id=1, source_target_pairs={{0,2},{1,5},{2,0},{3,7},{4,6},{5,1},{6,4},{7,3},{8,10},{9,13},{10,... | collective-permute-start | bytes 983048 | tf_op jit(solution)/shard_map/ppermute | solution.py:288
  25.3 2.4 %collective-permute-start.7 = (f32[8,80,128]{2,1,0:T(8,128)S(1)}, f32[8,80,128]{2,1,0:T(8,128)S(1)}, u32[]{:S(2)}, u32[]{:S(2)}) collective-permute-start(f32[8,80,128]{2,1,0:T(8,128)S(1)} %get-tuple-element.41), channel_id=1, source_target_pairs={{0,4},{1,3},{2,6},{3,1},{4,0},{5,7},{6,2},{7,5},{8,12},{9,11},{10,... | collective-permute-start | bytes 983048 | tf_op jit(solution)/shard_map/ppermute | solution.py:288
  27.7 4.3 %collective-permute-done.6.a1_ref.refs_1_ = f32[8,80,128]{2,1,0:T(8,128)S(1)} collective-permute-done((f32[8,80,128]{2,1,0:T(8,128)S(1)}, f32[8,80,128]{2,1,0:T(8,128)S(1)}, u32[]{:S(2)}, u32[]{:S(2)}) %collective-permute-start.6) | collective-permute-done | bytes 327712 | tf_op jit(solution)/shard_map/ppermute | solution.py:288
  32.0 0.9 %collective-permute-done.7.b1_ref.refs_2_ = f32[8,80,128]{2,1,0:T(8,128)S(1)} collective-permute-done((f32[8,80,128]{2,1,0:T(8,128)S(1)}, f32[8,80,128]{2,1,0:T(8,128)S(1)}, u32[]{:S(2)}, u32[]{:S(2)}) %collective-permute-start.7) | collective-permute-done | bytes 327712 | tf_op jit(solution)/shard_map/ppermute | solution.py:288
  33.1 3.2 %collective-permute-start.8 = (f32[4,80,128]{2,1,0:T(8,128)S(1)}, f32[4,80,128]{2,1,0:T(8,128)S(1)}, u32[]{:S(2)}, u32[]{:S(2)}) collective-permute-start(f32[4,80,128]{2,1,0:T(8,128)S(1)} %get-tuple-element.42), channel_id=1, source_target_pairs={{0,4},{1,3},{2,6},{3,1},{4,0},{5,7},{6,2},{7,5},{8,12},{9,11},{10,... | collective-permute-start | bytes 491528 | tf_op jit(solution)/shard_map/ppermute | solution.py:288
  36.3 1.7 %collective-permute-start.9 = (f32[4,80,128]{2,1,0:T(8,128)S(1)}, f32[4,80,128]{2,1,0:T(8,128)S(1)}, u32[]{:S(2)}, u32[]{:S(2)}) collective-permute-start(f32[4,80,128]{2,1,0:T(8,128)S(1)} %get-tuple-element.43), channel_id=1, source_target_pairs={{0,2},{1,5},{2,0},{3,7},{4,6},{5,1},{6,4},{7,3},{8,10},{9,13},{10,... | collective-permute-start | bytes 491528 | tf_op jit(solution)/shard_map/ppermute | solution.py:288
  38.0 2.7 %collective-permute-done.8.refs_3_ = f32[4,80,128]{2,1,0:T(8,128)S(1)} collective-permute-done((f32[4,80,128]{2,1,0:T(8,128)S(1)}, f32[4,80,128]{2,1,0:T(8,128)S(1)}, u32[]{:S(2)}, u32[]{:S(2)}) %collective-permute-start.8) | collective-permute-done | bytes 163872 | tf_op jit(solution)/shard_map/ppermute | solution.py:288
  40.7 0.9 collective-permute-done.9.refs_4_
  41.8 2.6 %collective-permute-start.10 = (f32[160,128]{1,0:T(8,128)S(1)}, f32[160,128]{1,0:T(8,128)S(1)}, u32[]{:S(2)}, u32[]{:S(2)}) collective-permute-start(f32[160,128]{1,0:T(8,128)S(1)} %get-tuple-element.44), channel_id=1, source_target_pairs={{0,16},{1,17},{2,18},{3,19},{4,20},{5,21},{6,22},{7,23},{8,24},{9,... | collective-permute-start | bytes 245768 | tf_op jit(solution)/shard_map/ppermute | solution.py:288
  44.4 1.3 %collective-permute-start.11 = (f32[160,128]{1,0:T(8,128)S(1)}, f32[160,128]{1,0:T(8,128)S(1)}, u32[]{:S(2)}, u32[]{:S(2)}) collective-permute-start(f32[160,128]{1,0:T(8,128)S(1)} %get-tuple-element.45), channel_id=1, source_target_pairs={{0,24},{1,25},{2,26},{3,27},{4,28},{5,29},{6,30},{7,31},{8,16},{9,... | collective-permute-start | bytes 245768 | tf_op jit(solution)/shard_map/ppermute | solution.py:288
  45.8 5.4 %collective-permute-done.10.refs_5_ = f32[160,128]{1,0:T(8,128)S(1)} collective-permute-done((f32[160,128]{1,0:T(8,128)S(1)}, f32[160,128]{1,0:T(8,128)S(1)}, u32[]{:S(2)}, u32[]{:S(2)}) %collective-permute-start.10) | collective-permute-done | bytes 81952 | tf_op jit(solution)/shard_map/ppermute | solution.py:288
  52.0 1.1 %collective-permute-start.13 = (f32[160,128]{1,0:T(8,128)S(1)}, f32[160,128]{1,0:T(8,128)S(1)}, u32[]{:S(2)}, u32[]{:S(2)}) collective-permute-start(f32[160,128]{1,0:T(8,128)S(1)} %get-tuple-element.47.own_ref), channel_id=1, source_target_pairs={{0,2},{1,0},{2,6},{3,1},{4,12},{5,7},{6,4},{7,3},{8,16},{9,11},{10... | collective-permute-start | bytes 245768 | tf_op jit(solution)/shard_map/ppermute | solution.py:427
  53.1 4.0 %shard_map.94 = (f32[64,128]{1,0:T(8,128)S(1)}, f32[8,128]{1,0:T(8,128)S(1)}) custom-call(f32[32,128]{1,0:T(8,128)S(1)} %get-tuple-element.48.packed_ref, f32[8,128]{1,0:T(8,128)S(1)} %copy-done.3), custom_call_target="tpu_custom_call" | custom-call | tf_op jit(solution)/shard_map/pallas_call | solution.py:661
  57.1 11.0 %shard_map.95 = bf16[32,8,384]{2,1,0:T(8,128)(2,1)S(1)} custom-call(f32[160,128]{1,0:T(8,128)S(1)} %get-tuple-element.47.own_ref, f32[160,128]{1,0:T(8,128)S(1)} %collective-permute-done.13.left_ref, f32[32,128]{1,0:T(8,128)S(1)} %collective-permute-done.14.right_ref, f32[8,128]{1,0:T(8,128)S(1)} %copy-done.3, f32[64,128]{1,0:T(8,128)S(1)} %get-tuple-element.49.inv_ref, ...), custom_call_target="tpu_custom_call" | custom-call | tf_op jit(solution)/shard_map/pallas_call | solution.py:675
  68.2 13.4 %all_to_all.10.w_ref = bf16[32,8,384]{2,1,0:T(8,128)(2,1)S(1)} all-to-all(bf16[32,8,384]{2,1,0:T(8,128)(2,1)S(1)} %shard_map.95), channel_id=1, replica_groups=mesh['range'=32] {'range'}, dimensions={0} | all-to-all | bytes 393216 | tf_op jit(solution)/shard_map/all_to_all | solution.py:771
  81.6 2.0 %shard_map.96 = bf16[64,256]{1,0:T(8,128)(2,1)S(1)} custom-call(s32[32]{0:T(128)S(1)} %copy-done.6, s32[32]{0:T(128)S(1)} %copy-done.7, s32[32]{0:T(128)S(1)} %copy-done.8, s32[32]{0:T(128)S(1)} %bitcast.6, bf16[32,128,128]{2,1,0:T(8,128)(2,1)S(1)} %bitcast.5, bf16[32,2,32,128]{3,2,1,0:T(8,128)(2,1)S(1)} %get-tuple-element.35.refs_0_.upper_ref, ...), custom_call_target="tpu_custom_call" | custom-call | tf_op jit(solution)/shard_map/pallas_call | solution.py:729
  83.5 9.8 %all_to_all.11 = bf16[32,2,256]{2,1,0:T(2,128)(2,1)S(1)} all-to-all(bf16[32,2,256]{2,1,0:T(2,128)(2,1)S(1)} %reshape.17), channel_id=1, replica_groups=mesh['range'=32] {'range'}, dimensions={0} | all-to-all | bytes 65536 | tf_op jit(solution)/shard_map/all_to_all | solution.py:779
  (45 shorter events, 8.4 us)
Async XLA Ops:
  0.0 5.1 %copy-start = (bf16[2,64,32,256]{3,2,1,0:T(8,128)(2,1)S(1)}, bf16[2,64,32,256]{3,2,1,0:T(8,128)(2,1)}, u32[]{:S(2)}) copy-start(bf16[2,64,32,256]{3,2,1,0:T(8,128)(2,1)} %param.8) | copy-start | bytes 6291460
  0.0 5.1 %copy-start.5 = (bf16[2,128]{1,0:T(2,128)(2,1)S(1)}, bf16[2,128]{1,0:T(2,128)(2,1)}, u32[]{:S(2)}) copy-start(bf16[2,128]{1,0:T(2,128)(2,1)} %rep_ref.1) | copy-start | bytes 1540
  2.5 12.4 %collective-permute-start.3 = (bf16[2,1024,128]{2,1,0:T(8,128)(2,1)}, bf16[2,1024,128]{2,1,0:T(8,128)(2,1)S(1)}, u32[]{:S(2)}, u32[]{:S(2)}) collective-permute-start(bf16[2,1024,128]{2,1,0:T(8,128)(2,1)} %get-tuple-element.36), channel_id=1, source_target_pairs={{1,0},{2,1},{3,2},{4,3},{5,4},{6,5},{7,6},{8,7},{9,8},{10,9},{11,1... | collective-permute-start | bytes 1572872 | tf_op jit(solution)/shard_map/ppermute | solution.py:750
  3.8 12.3 %collective-permute-start = (bf16[2,1024,128]{2,1,0:T(8,128)(2,1)}, bf16[2,1024,128]{2,1,0:T(8,128)(2,1)S(1)}, u32[]{:S(2)}, u32[]{:S(2)}) collective-permute-start(bf16[2,1024,128]{2,1,0:T(8,128)(2,1)} %get-tuple-element.31), channel_id=1, source_target_pairs={{1,0},{2,1},{3,2},{4,3},{5,4},{6,5},{7,6},{8,7},{9,8},{10,9},{11,1... | collective-permute-start | bytes 1572872 | tf_op jit(solution)/shard_map/ppermute | solution.py:750
  5.1 1.0 %copy-start.1 = (bf16[512,512]{1,0:T(8,128)(2,1)S(1)}, bf16[512,512]{1,0:T(8,128)(2,1)}, u32[]{:S(2)}) copy-start(bf16[512,512]{1,0:T(8,128)(2,1)} %constant.4.clone.dft_ref) | copy-start | bytes 1572868
  11.0 3.0 %collective-permute-start.1 = (bf16[18,2,32,128]{3,2,1,0:T(8,128)(2,1)S(1)}, bf16[18,2,32,128]{3,2,1,0:T(8,128)(2,1)S(1)}, u32[]{:S(2)}, u32[]{:S(2)}) collective-permute-start(bf16[18,2,32,128]{3,2,1,0:T(8,128)(2,1)S(1)} %get-tuple-element.33), channel_id=1, source_target_pairs={{0,1},{1,0},{2,3},{3,2},{4,5},{5,4},{6,7},{7,6},{8,9},{9,8},{10,11... | collective-permute-start | bytes 884744 | tf_op jit(solution)/shard_map/ppermute | solution.py:288
  12.8 1.6 %collective-permute-start.2 = (bf16[18,2,32,128]{3,2,1,0:T(8,128)(2,1)S(1)}, bf16[18,2,32,128]{3,2,1,0:T(8,128)(2,1)S(1)}, u32[]{:S(2)}, u32[]{:S(2)}) collective-permute-start(bf16[18,2,32,128]{3,2,1,0:T(8,128)(2,1)S(1)} %get-tuple-element.34), channel_id=1, source_target_pairs={{0,1},{1,0},{2,3},{3,2},{4,5},{5,4},{6,7},{7,6},{8,9},{9,8},{10,11... | collective-permute-start | bytes 884744 | tf_op jit(solution)/shard_map/ppermute | solution.py:288
  13.4 1.6 %copy-start.2 = (bf16[512,512]{1,0:T(8,128)(2,1)S(1)}, bf16[512,512]{1,0:T(8,128)(2,1)}, u32[]{:S(2)}) copy-start(bf16[512,512]{1,0:T(8,128)(2,1)} %constant.4.clone.dft_ref) | copy-start | bytes 1572868
  15.7 5.8 %collective-permute-start.5 = (bf16[18,2,32,128]{3,2,1,0:T(8,128)(2,1)S(1)}, bf16[18,2,32,128]{3,2,1,0:T(8,128)(2,1)S(1)}, u32[]{:S(2)}, u32[]{:S(2)}) collective-permute-start(bf16[18,2,32,128]{3,2,1,0:T(8,128)(2,1)S(1)} %get-tuple-element.39), channel_id=1, source_target_pairs={{0,1},{1,0},{2,3},{3,2},{4,5},{5,4},{6,7},{7,6},{8,9},{9,8},{10,11... | collective-permute-start | bytes 884744 | tf_op jit(solution)/shard_map/ppermute | solution.py:288
  16.8 5.3 %collective-permute-start.4 = (bf16[18,2,32,128]{3,2,1,0:T(8,128)(2,1)S(1)}, bf16[18,2,32,128]{3,2,1,0:T(8,128)(2,1)S(1)}, u32[]{:S(2)}, u32[]{:S(2)}) collective-permute-start(bf16[18,2,32,128]{3,2,1,0:T(8,128)(2,1)S(1)} %get-tuple-element.38), channel_id=1, source_target_pairs={{0,1},{1,0},{2,3},{3,2},{4,5},{5,4},{6,7},{7,6},{8,9},{9,8},{10,11... | collective-permute-start | bytes 884744 | tf_op jit(solution)/shard_map/ppermute | solution.py:288
  22.9 9.1 %collective-permute-start.6 = (f32[8,80,128]{2,1,0:T(8,128)S(1)}, f32[8,80,128]{2,1,0:T(8,128)S(1)}, u32[]{:S(2)}, u32[]{:S(2)}) collective-permute-start(f32[8,80,128]{2,1,0:T(8,128)S(1)} %get-tuple-element.40), channel_id=1, source_target_pairs={{0,2},{1,5},{2,0},{3,7},{4,6},{5,1},{6,4},{7,3},{8,10},{9,13},{10,... | collective-permute-start | bytes 983048 | tf_op jit(solution)/shard_map/ppermute | solution.py:288
  25.3 7.6 %collective-permute-start.7 = (f32[8,80,128]{2,1,0:T(8,128)S(1)}, f32[8,80,128]{2,1,0:T(8,128)S(1)}, u32[]{:S(2)}, u32[]{:S(2)}) collective-permute-start(f32[8,80,128]{2,1,0:T(8,128)S(1)} %get-tuple-element.41), channel_id=1, source_target_pairs={{0,4},{1,3},{2,6},{3,1},{4,0},{5,7},{6,2},{7,5},{8,12},{9,11},{10,... | collective-permute-start | bytes 983048 | tf_op jit(solution)/shard_map/ppermute | solution.py:288
  33.1 7.6 %collective-permute-start.8 = (f32[4,80,128]{2,1,0:T(8,128)S(1)}, f32[4,80,128]{2,1,0:T(8,128)S(1)}, u32[]{:S(2)}, u32[]{:S(2)}) collective-permute-start(f32[4,80,128]{2,1,0:T(8,128)S(1)} %get-tuple-element.42), channel_id=1, source_target_pairs={{0,4},{1,3},{2,6},{3,1},{4,0},{5,7},{6,2},{7,5},{8,12},{9,11},{10,... | collective-permute-start | bytes 491528 | tf_op jit(solution)/shard_map/ppermute | solution.py:288
  36.3 5.3 %collective-permute-start.9 = (f32[4,80,128]{2,1,0:T(8,128)S(1)}, f32[4,80,128]{2,1,0:T(8,128)S(1)}, u32[]{:S(2)}, u32[]{:S(2)}) collective-permute-start(f32[4,80,128]{2,1,0:T(8,128)S(1)} %get-tuple-element.43), channel_id=1, source_target_pairs={{0,2},{1,5},{2,0},{3,7},{4,6},{5,1},{6,4},{7,3},{8,10},{9,13},{10,... | collective-permute-start | bytes 491528 | tf_op jit(solution)/shard_map/ppermute | solution.py:288
  41.7 11.4 %copy-start.3 = (f32[8,128]{1,0:T(8,128)S(1)}, f32[8,128]{1,0:T(8,128)}, u32[]{:S(2)}) copy-start(f32[8,128]{1,0:T(8,128)} %constant.5.clone.steer_ref) | copy-start | bytes 12292
  41.8 9.5 %collective-permute-start.10 = (f32[160,128]{1,0:T(8,128)S(1)}, f32[160,128]{1,0:T(8,128)S(1)}, u32[]{:S(2)}, u32[]{:S(2)}) collective-permute-start(f32[160,128]{1,0:T(8,128)S(1)} %get-tuple-element.44), channel_id=1, source_target_pairs={{0,16},{1,17},{2,18},{3,19},{4,20},{5,21},{6,22},{7,23},{8,24},{9,... | collective-permute-start | bytes 245768 | tf_op jit(solution)/shard_map/ppermute | solution.py:288
  44.4 6.8 %collective-permute-start.11 = (f32[160,128]{1,0:T(8,128)S(1)}, f32[160,128]{1,0:T(8,128)S(1)}, u32[]{:S(2)}, u32[]{:S(2)}) collective-permute-start(f32[160,128]{1,0:T(8,128)S(1)} %get-tuple-element.45), channel_id=1, source_target_pairs={{0,24},{1,25},{2,26},{3,27},{4,28},{5,29},{6,30},{7,31},{8,16},{9,... | collective-permute-start | bytes 245768 | tf_op jit(solution)/shard_map/ppermute | solution.py:288
  45.8 35.8 %copy-start.6 = (s32[32]{0:T(128)S(1)}, s32[32]{0:T(128)}, u32[]{:S(2)}) copy-start(s32[32]{0:T(128)} %bin_ref.1) | copy-start | bytes 388
  45.8 35.8 %copy-start.7 = (s32[32]{0:T(128)S(1)}, s32[32]{0:T(128)}, u32[]{:S(2)}) copy-start(s32[32]{0:T(128)} %block_ref.1) | copy-start | bytes 388
  45.8 35.8 %copy-start.8 = (s32[32]{0:T(128)S(1)}, s32[32]{0:T(128)}, u32[]{:S(2)}) copy-start(s32[32]{0:T(128)} %beam_ref.1) | copy-start | bytes 388
  45.8 35.8 %copy-start.9 = (s32[32,1]{0,1:T(1,128)S(1)}, s32[32,1]{0,1:T(1,128)}, u32[]{:S(2)}) copy-start(s32[32,1]{0,1:T(1,128)} %param.13) | copy-start | bytes 388
  45.8 6.1 %collective-permute-start.12 = (f32[160,128]{1,0:T(8,128)S(1)}, f32[160,128]{1,0:T(8,128)S(1)}, u32[]{:S(2)}, u32[]{:S(2)}) collective-permute-start(f32[160,128]{1,0:T(8,128)S(1)} %get-tuple-element.46), channel_id=1, source_target_pairs={{0,8},{1,9},{2,10},{3,11},{4,12},{5,13},{6,14},{7,15},{8,0},{9,1},... | collective-permute-start | bytes 245768 | tf_op jit(solution)/shard_map/ppermute | solution.py:288
  52.0 5.1 %collective-permute-start.13 = (f32[160,128]{1,0:T(8,128)S(1)}, f32[160,128]{1,0:T(8,128)S(1)}, u32[]{:S(2)}, u32[]{:S(2)}) collective-permute-start(f32[160,128]{1,0:T(8,128)S(1)} %get-tuple-element.47.own_ref), channel_id=1, source_target_pairs={{0,2},{1,0},{2,6},{3,1},{4,12},{5,7},{6,4},{7,3},{8,16},{9,11},{10... | collective-permute-start | bytes 245768 | tf_op jit(solution)/shard_map/ppermute | solution.py:427
  53.1 4.0 %collective-permute-start.14 = (f32[32,128]{1,0:T(8,128)S(1)}, f32[32,128]{1,0:T(8,128)S(1)}, u32[]{:S(2)}, u32[]{:S(2)}) collective-permute-start(f32[32,128]{1,0:T(8,128)S(1)} %get-tuple-element.48.packed_ref), channel_id=1, source_target_pairs={{0,1},{1,3},{2,0},{3,7},{4,6},{5,13},{6,2},{7,5},{8,10},{9,17},{10... | collective-permute-start | bytes 49160 | tf_op jit(solution)/shard_map/ppermute | solution.py:427
  (1 other events, 0.7 us)

commit v5 on v3

--- a/solution.py
+++ b/solution.py
@@ -242,7 +242,7 @@
     def write(e, block):
         out_ref[e] = block if before_ref is None else block + before_ref[e]
 
-    @pl.loop(0, count // 2, unroll=2)
+    @pl.loop(0, count // 2, unroll=8)
     def _(step):
         e = step * 2
         each = []

time: 92.3 us -> 91.7 us (level)
  Pallas kernels: 27.5 us -> 25.1 us
  waiting for transfers between devices: 15.4 us -> 16.6 us
    pallas_call x4, Pallas kernels: 4.26 us -> 1.88 us  [cross(): pl.pallas_call(functools.partial(cross_kernel, len(spectra)), out_shape=j...]
    ppermute x11, waiting for transfers between devices: 15.4 us -> 16.6 us  [partner(): lax.ppermute(value, 'range', [(i, i ^ bits[i & 1]) for i in range(count)])]
  transfers between devices with their start and end apart: 15 -> 15, of which waited for: 8 -> 9; matrix products, arithmetic and copies ran while one was open for 0% -> 0% of each run, Pallas kernels for 14% -> 12%
where the time goes in v5:
time: 91.7 us; the launch traced here: 91.5 us
  Pallas kernels  25.1 us (27%)
  starting transfers between devices  23.9 us (26%)
  blocking collectives  23.2 us (25%)
  waiting for transfers between devices  16.6 us (18%)
  local copies, waits for them, and re-layouts  2.42 us (3%)
    ppermute x11, starting transfers between devices, partner(): lax.ppermute(value, 'range', [(i, i ^ bits[i & 1]) for i in range(count)])  20.3 us
    ppermute x11, waiting for transfers between devices, partner(): lax.ppermute(value, 'range', [(i, i ^ bits[i & 1]) for i in range(count)])  16.6 us
    all_to_all x1, blocking collectives, on_device(): lax.all_to_all(mine, 'range', split_axis=0, concat_axis=0, tiled=True, ax...  13.4 us
    all_to_all x1, blocking collectives, on_device(): lax.all_to_all(outgoing.reshape(devices, CAP, 2 * BLOCK), 'range', split_...  9.77 us
    pallas_call x1, Pallas kernels, solve_outer(): pl.pallas_call(functools.partial(outer_kernel, total), out_shape=jax.Shap...  8.53 us
    pallas_call x1, Pallas kernels, spectra_first(): pl.pallas_call(spectra_first_kernel, out_shape=[jax.ShapeDtypeStruct((pul...  4.12 us
    pallas_call x1, Pallas kernels, solve_middle(): pl.pallas_call(functools.partial(middle_kernel, total), out_shape=[jax.Sh...  4 us
    ppermute x2, starting transfers between devices, on_device(): halos = [lax.ppermute(value, 'range', before) for value in slices]  2.58 us
  transfers between devices with their start and end apart: 15, of which 9 were waited for; matrix products, arithmetic and copies ran while one was open for 0% of the time, Pallas kernels for 12%

profile of v5, /device:TPU:0, one launch (start us, length us, event | category | flops | bytes accessed | tf_op | source)
XLA Modules:
  0.0 91.5 jit_solution(8360900838416982355)
XLA Ops:
  0.0 2.5 %shard_map.82 = (bf16[2,1024,128]{2,1,0:T(8,128)(2,1)}, bf16[2,1024,128]{2,1,0:T(8,128)(2,1)}, f32[8,128]{1,0:T(8,128)}) custom-call(bf16[2,2048,256]{2,1,0:T(8,128)(2,1)} %bitcast.3), custom_call_target="tpu_custom_call" | custom-call | tf_op jit(solution)/shard_map/pallas_call | solution.py:78
  2.5 1.3 %collective-permute-start.3 = (bf16[2,1024,128]{2,1,0:T(8,128)(2,1)}, bf16[2,1024,128]{2,1,0:T(8,128)(2,1)S(1)}, u32[]{:S(2)}, u32[]{:S(2)}) collective-permute-start(bf16[2,1024,128]{2,1,0:T(8,128)(2,1)} %get-tuple-element.36), channel_id=1, source_target_pairs={{1,0},{2,1},{3,2},{4,3},{5,4},{6,5},{7,6},{8,7},{9,8},{10,9},{11,1... | collective-permute-start | bytes 1572872 | tf_op jit(solution)/shard_map/ppermute | solution.py:773
  3.8 1.3 %collective-permute-start = (bf16[2,1024,128]{2,1,0:T(8,128)(2,1)}, bf16[2,1024,128]{2,1,0:T(8,128)(2,1)S(1)}, u32[]{:S(2)}, u32[]{:S(2)}) collective-permute-start(bf16[2,1024,128]{2,1,0:T(8,128)(2,1)} %get-tuple-element.31), channel_id=1, source_target_pairs={{1,0},{2,1},{3,2},{4,3},{5,4},{6,5},{7,6},{8,7},{9,8},{10,9},{11,1... | collective-permute-start | bytes 1572872 | tf_op jit(solution)/shard_map/ppermute | solution.py:773
  5.1 1.0 %copy-done.1 = bf16[512,512]{1,0:T(8,128)(2,1)S(1)} copy-done((bf16[512,512]{1,0:T(8,128)(2,1)S(1)}, bf16[512,512]{1,0:T(8,128)(2,1)}, u32[]{:S(2)}) %copy-start.1) | copy-done | bytes 524312
  6.9 4.1 %shard_map.83 = (bf16[32,2,64,128]{3,2,1,0:T(8,128)(2,1)S(1)}, f32[2048,256]{1,0:T(8,128)S(1)}, bf16[2,256,256]{2,1,0:T(8,128)(2,1)S(1)}, bf16[18,2,32,128]{3,2,...) custom-call(bf16[2,2048,256]{2,1,0:T(8,128)(2,1)S(1)} %bitcast.4, bf16[2,128]{1,0:T(2,128)(2,1)S(1)} %copy-done.5, ...), custom_call_target="tpu_custom_call" | custom-call | flops 1 | bytes 1 | tf_op jit(solution)/shard_map/pallas_call | solution.py:199
  11.0 1.8 %collective-permute-start.1 = (bf16[18,2,32,128]{3,2,1,0:T(8,128)(2,1)S(1)}, bf16[18,2,32,128]{3,2,1,0:T(8,128)(2,1)S(1)}, u32[]{:S(2)}, u32[]{:S(2)}) collective-permute-start(bf16[18,2,32,128]{3,2,1,0:T(8,128)(2,1)S(1)} %get-tuple-element.33), channel_id=1, source_target_pairs={{0,1},{1,0},{2,3},{3,2},{4,5},{5,4},{6,7},{7,6},{8,9},{9,8},{10,11... | collective-permute-start | bytes 884744 | tf_op jit(solution)/shard_map/ppermute | solution.py:288
  16.8 4.1 %collective-permute-start.4 = (bf16[18,2,32,128]{3,2,1,0:T(8,128)(2,1)S(1)}, bf16[18,2,32,128]{3,2,1,0:T(8,128)(2,1)S(1)}, u32[]{:S(2)}, u32[]{:S(2)}) collective-permute-start(bf16[18,2,32,128]{3,2,1,0:T(8,128)(2,1)S(1)} %get-tuple-element.38), channel_id=1, source_target_pairs={{0,1},{1,0},{2,3},{3,2},{4,5},{5,4},{6,7},{7,6},{8,9},{9,8},{10,11... | collective-permute-start | bytes 884744 | tf_op jit(solution)/shard_map/ppermute | solution.py:288
  22.9 2.4 %collective-permute-start.6 = (f32[8,80,128]{2,1,0:T(8,128)S(1)}, f32[8,80,128]{2,1,0:T(8,128)S(1)}, u32[]{:S(2)}, u32[]{:S(2)}) collective-permute-start(f32[8,80,128]{2,1,0:T(8,128)S(1)} %get-tuple-element.40), channel_id=1, source_target_pairs={{0,2},{1,5},{2,0},{3,7},{4,6},{5,1},{6,4},{7,3},{8,10},{9,13},{10,... | collective-permute-start | bytes 983048 | tf_op jit(solution)/shard_map/ppermute | solution.py:288
  25.3 2.4 %collective-permute-start.7 = (f32[8,80,128]{2,1,0:T(8,128)S(1)}, f32[8,80,128]{2,1,0:T(8,128)S(1)}, u32[]{:S(2)}, u32[]{:S(2)}) collective-permute-start(f32[8,80,128]{2,1,0:T(8,128)S(1)} %get-tuple-element.41), channel_id=1, source_target_pairs={{0,4},{1,3},{2,6},{3,1},{4,0},{5,7},{6,2},{7,5},{8,12},{9,11},{10,... | collective-permute-start | bytes 983048 | tf_op jit(solution)/shard_map/ppermute | solution.py:288
  27.7 4.3 %collective-permute-done.6.a1_ref.refs_1_ = f32[8,80,128]{2,1,0:T(8,128)S(1)} collective-permute-done((f32[8,80,128]{2,1,0:T(8,128)S(1)}, f32[8,80,128]{2,1,0:T(8,128)S(1)}, u32[]{:S(2)}, u32[]{:S(2)}) %collective-permute-start.6) | collective-permute-done | bytes 327712 | tf_op jit(solution)/shard_map/ppermute | solution.py:288
  32.0 0.9 %collective-permute-done.7.b1_ref.refs_2_ = f32[8,80,128]{2,1,0:T(8,128)S(1)} collective-permute-done((f32[8,80,128]{2,1,0:T(8,128)S(1)}, f32[8,80,128]{2,1,0:T(8,128)S(1)}, u32[]{:S(2)}, u32[]{:S(2)}) %collective-permute-start.7) | collective-permute-done | bytes 327712 | tf_op jit(solution)/shard_map/ppermute | solution.py:288
  33.1 3.2 %collective-permute-start.8 = (f32[4,80,128]{2,1,0:T(8,128)S(1)}, f32[4,80,128]{2,1,0:T(8,128)S(1)}, u32[]{:S(2)}, u32[]{:S(2)}) collective-permute-start(f32[4,80,128]{2,1,0:T(8,128)S(1)} %get-tuple-element.42), channel_id=1, source_target_pairs={{0,4},{1,3},{2,6},{3,1},{4,0},{5,7},{6,2},{7,5},{8,12},{9,11},{10,... | collective-permute-start | bytes 491528 | tf_op jit(solution)/shard_map/ppermute | solution.py:288
  36.3 1.7 %collective-permute-start.9 = (f32[4,80,128]{2,1,0:T(8,128)S(1)}, f32[4,80,128]{2,1,0:T(8,128)S(1)}, u32[]{:S(2)}, u32[]{:S(2)}) collective-permute-start(f32[4,80,128]{2,1,0:T(8,128)S(1)} %get-tuple-element.43), channel_id=1, source_target_pairs={{0,2},{1,5},{2,0},{3,7},{4,6},{5,1},{6,4},{7,3},{8,10},{9,13},{10,... | collective-permute-start | bytes 491528 | tf_op jit(solution)/shard_map/ppermute | solution.py:288
  38.0 2.7 %collective-permute-done.8.refs_3_ = f32[4,80,128]{2,1,0:T(8,128)S(1)} collective-permute-done((f32[4,80,128]{2,1,0:T(8,128)S(1)}, f32[4,80,128]{2,1,0:T(8,128)S(1)}, u32[]{:S(2)}, u32[]{:S(2)}) %collective-permute-start.8) | collective-permute-done | bytes 163872 | tf_op jit(solution)/shard_map/ppermute | solution.py:288
  40.7 0.9 collective-permute-done.9.refs_4_
  41.8 2.6 %collective-permute-start.10 = (f32[160,128]{1,0:T(8,128)S(1)}, f32[160,128]{1,0:T(8,128)S(1)}, u32[]{:S(2)}, u32[]{:S(2)}) collective-permute-start(f32[160,128]{1,0:T(8,128)S(1)} %get-tuple-element.44), channel_id=1, source_target_pairs={{0,16},{1,17},{2,18},{3,19},{4,20},{5,21},{6,22},{7,23},{8,24},{9,... | collective-permute-start | bytes 245768 | tf_op jit(solution)/shard_map/ppermute | solution.py:288
  44.4 1.3 %collective-permute-start.11 = (f32[160,128]{1,0:T(8,128)S(1)}, f32[160,128]{1,0:T(8,128)S(1)}, u32[]{:S(2)}, u32[]{:S(2)}) collective-permute-start(f32[160,128]{1,0:T(8,128)S(1)} %get-tuple-element.45), channel_id=1, source_target_pairs={{0,24},{1,25},{2,26},{3,27},{4,28},{5,29},{6,30},{7,31},{8,16},{9,... | collective-permute-start | bytes 245768 | tf_op jit(solution)/shard_map/ppermute | solution.py:288
  45.8 5.4 %collective-permute-done.10.refs_5_ = f32[160,128]{1,0:T(8,128)S(1)} collective-permute-done((f32[160,128]{1,0:T(8,128)S(1)}, f32[160,128]{1,0:T(8,128)S(1)}, u32[]{:S(2)}, u32[]{:S(2)}) %collective-permute-start.10) | collective-permute-done | bytes 81952 | tf_op jit(solution)/shard_map/ppermute | solution.py:288
  52.0 1.1 %collective-permute-start.13 = (f32[160,128]{1,0:T(8,128)S(1)}, f32[160,128]{1,0:T(8,128)S(1)}, u32[]{:S(2)}, u32[]{:S(2)}) collective-permute-start(f32[160,128]{1,0:T(8,128)S(1)} %get-tuple-element.47.own_ref), channel_id=1, source_target_pairs={{0,2},{1,0},{2,6},{3,1},{4,12},{5,7},{6,4},{7,3},{8,16},{9,11},{10... | collective-permute-start | bytes 245768 | tf_op jit(solution)/shard_map/ppermute | solution.py:427
  53.1 4.0 %shard_map.94 = (f32[64,128]{1,0:T(8,128)S(1)}, f32[8,128]{1,0:T(8,128)S(1)}) custom-call(f32[32,128]{1,0:T(8,128)S(1)} %get-tuple-element.48.packed_ref, f32[8,128]{1,0:T(8,128)S(1)} %copy-done.3), custom_call_target="tpu_custom_call" | custom-call | tf_op jit(solution)/shard_map/pallas_call | solution.py:679
  57.1 8.5 %shard_map.95 = bf16[32,8,384]{2,1,0:T(8,128)(2,1)S(1)} custom-call(f32[160,128]{1,0:T(8,128)S(1)} %get-tuple-element.47.own_ref, f32[160,128]{1,0:T(8,128)S(1)} %collective-permute-done.13.left_ref, f32[32,128]{1,0:T(8,128)S(1)} %collective-permute-done.14.right_ref, f32[8,128]{1,0:T(8,128)S(1)} %copy-done.3, f32[64,128]{1,0:T(8,128)S(1)} %get-tuple-element.49.inv_ref, ...), custom_call_target="tpu_custom_call" | custom-call | tf_op jit(solution)/shard_map/pallas_call | solution.py:693
  65.7 13.4 %all_to_all.10.w_ref = bf16[32,8,384]{2,1,0:T(8,128)(2,1)S(1)} all-to-all(bf16[32,8,384]{2,1,0:T(8,128)(2,1)S(1)} %shard_map.95), channel_id=1, replica_groups=mesh['range'=32] {'range'}, dimensions={0} | all-to-all | bytes 393216 | tf_op jit(solution)/shard_map/all_to_all | solution.py:794
  79.1 2.0 %shard_map.96 = bf16[64,256]{1,0:T(8,128)(2,1)S(1)} custom-call(s32[32]{0:T(128)S(1)} %copy-done.6, s32[32]{0:T(128)S(1)} %copy-done.7, s32[32]{0:T(128)S(1)} %copy-done.8, s32[32]{0:T(128)S(1)} %bitcast.6, bf16[32,128,128]{2,1,0:T(8,128)(2,1)S(1)} %bitcast.5, bf16[32,2,32,128]{3,2,1,0:T(8,128)(2,1)S(1)} %get-tuple-element.35.refs_0_.upper_ref, ...), custom_call_target="tpu_custom_call" | custom-call | tf_op jit(solution)/shard_map/pallas_call | solution.py:752
  81.0 9.8 %all_to_all.11 = bf16[32,2,256]{2,1,0:T(2,128)(2,1)S(1)} all-to-all(bf16[32,2,256]{2,1,0:T(2,128)(2,1)S(1)} %reshape.17), channel_id=1, replica_groups=mesh['range'=32] {'range'}, dimensions={0} | all-to-all | bytes 65536 | tf_op jit(solution)/shard_map/all_to_all | solution.py:802
  (45 shorter events, 8.4 us)
Async XLA Ops:
  0.0 5.1 %copy-start = (bf16[2,64,32,256]{3,2,1,0:T(8,128)(2,1)S(1)}, bf16[2,64,32,256]{3,2,1,0:T(8,128)(2,1)}, u32[]{:S(2)}) copy-start(bf16[2,64,32,256]{3,2,1,0:T(8,128)(2,1)} %param.8) | copy-start | bytes 6291460
  0.0 5.1 %copy-start.5 = (bf16[2,128]{1,0:T(2,128)(2,1)S(1)}, bf16[2,128]{1,0:T(2,128)(2,1)}, u32[]{:S(2)}) copy-start(bf16[2,128]{1,0:T(2,128)(2,1)} %rep_ref.1) | copy-start | bytes 1540
  2.5 12.4 %collective-permute-start.3 = (bf16[2,1024,128]{2,1,0:T(8,128)(2,1)}, bf16[2,1024,128]{2,1,0:T(8,128)(2,1)S(1)}, u32[]{:S(2)}, u32[]{:S(2)}) collective-permute-start(bf16[2,1024,128]{2,1,0:T(8,128)(2,1)} %get-tuple-element.36), channel_id=1, source_target_pairs={{1,0},{2,1},{3,2},{4,3},{5,4},{6,5},{7,6},{8,7},{9,8},{10,9},{11,1... | collective-permute-start | bytes 1572872 | tf_op jit(solution)/shard_map/ppermute | solution.py:773
  3.8 12.3 %collective-permute-start = (bf16[2,1024,128]{2,1,0:T(8,128)(2,1)}, bf16[2,1024,128]{2,1,0:T(8,128)(2,1)S(1)}, u32[]{:S(2)}, u32[]{:S(2)}) collective-permute-start(bf16[2,1024,128]{2,1,0:T(8,128)(2,1)} %get-tuple-element.31), channel_id=1, source_target_pairs={{1,0},{2,1},{3,2},{4,3},{5,4},{6,5},{7,6},{8,7},{9,8},{10,9},{11,1... | collective-permute-start | bytes 1572872 | tf_op jit(solution)/shard_map/ppermute | solution.py:773
  5.1 1.0 %copy-start.1 = (bf16[512,512]{1,0:T(8,128)(2,1)S(1)}, bf16[512,512]{1,0:T(8,128)(2,1)}, u32[]{:S(2)}) copy-start(bf16[512,512]{1,0:T(8,128)(2,1)} %constant.4.clone.dft_ref) | copy-start | bytes 1572868
  11.0 3.0 %collective-permute-start.1 = (bf16[18,2,32,128]{3,2,1,0:T(8,128)(2,1)S(1)}, bf16[18,2,32,128]{3,2,1,0:T(8,128)(2,1)S(1)}, u32[]{:S(2)}, u32[]{:S(2)}) collective-permute-start(bf16[18,2,32,128]{3,2,1,0:T(8,128)(2,1)S(1)} %get-tuple-element.33), channel_id=1, source_target_pairs={{0,1},{1,0},{2,3},{3,2},{4,5},{5,4},{6,7},{7,6},{8,9},{9,8},{10,11... | collective-permute-start | bytes 884744 | tf_op jit(solution)/shard_map/ppermute | solution.py:288
  12.8 1.6 %collective-permute-start.2 = (bf16[18,2,32,128]{3,2,1,0:T(8,128)(2,1)S(1)}, bf16[18,2,32,128]{3,2,1,0:T(8,128)(2,1)S(1)}, u32[]{:S(2)}, u32[]{:S(2)}) collective-permute-start(bf16[18,2,32,128]{3,2,1,0:T(8,128)(2,1)S(1)} %get-tuple-element.34), channel_id=1, source_target_pairs={{0,1},{1,0},{2,3},{3,2},{4,5},{5,4},{6,7},{7,6},{8,9},{9,8},{10,11... | collective-permute-start | bytes 884744 | tf_op jit(solution)/shard_map/ppermute | solution.py:288
  13.4 1.6 %copy-start.2 = (bf16[512,512]{1,0:T(8,128)(2,1)S(1)}, bf16[512,512]{1,0:T(8,128)(2,1)}, u32[]{:S(2)}) copy-start(bf16[512,512]{1,0:T(8,128)(2,1)} %constant.4.clone.dft_ref) | copy-start | bytes 1572868
  15.7 5.8 %collective-permute-start.5 = (bf16[18,2,32,128]{3,2,1,0:T(8,128)(2,1)S(1)}, bf16[18,2,32,128]{3,2,1,0:T(8,128)(2,1)S(1)}, u32[]{:S(2)}, u32[]{:S(2)}) collective-permute-start(bf16[18,2,32,128]{3,2,1,0:T(8,128)(2,1)S(1)} %get-tuple-element.39), channel_id=1, source_target_pairs={{0,1},{1,0},{2,3},{3,2},{4,5},{5,4},{6,7},{7,6},{8,9},{9,8},{10,11... | collective-permute-start | bytes 884744 | tf_op jit(solution)/shard_map/ppermute | solution.py:288
  16.8 5.3 %collective-permute-start.4 = (bf16[18,2,32,128]{3,2,1,0:T(8,128)(2,1)S(1)}, bf16[18,2,32,128]{3,2,1,0:T(8,128)(2,1)S(1)}, u32[]{:S(2)}, u32[]{:S(2)}) collective-permute-start(bf16[18,2,32,128]{3,2,1,0:T(8,128)(2,1)S(1)} %get-tuple-element.38), channel_id=1, source_target_pairs={{0,1},{1,0},{2,3},{3,2},{4,5},{5,4},{6,7},{7,6},{8,9},{9,8},{10,11... | collective-permute-start | bytes 884744 | tf_op jit(solution)/shard_map/ppermute | solution.py:288
  22.9 9.1 %collective-permute-start.6 = (f32[8,80,128]{2,1,0:T(8,128)S(1)}, f32[8,80,128]{2,1,0:T(8,128)S(1)}, u32[]{:S(2)}, u32[]{:S(2)}) collective-permute-start(f32[8,80,128]{2,1,0:T(8,128)S(1)} %get-tuple-element.40), channel_id=1, source_target_pairs={{0,2},{1,5},{2,0},{3,7},{4,6},{5,1},{6,4},{7,3},{8,10},{9,13},{10,... | collective-permute-start | bytes 983048 | tf_op jit(solution)/shard_map/ppermute | solution.py:288
  25.3 7.6 %collective-permute-start.7 = (f32[8,80,128]{2,1,0:T(8,128)S(1)}, f32[8,80,128]{2,1,0:T(8,128)S(1)}, u32[]{:S(2)}, u32[]{:S(2)}) collective-permute-start(f32[8,80,128]{2,1,0:T(8,128)S(1)} %get-tuple-element.41), channel_id=1, source_target_pairs={{0,4},{1,3},{2,6},{3,1},{4,0},{5,7},{6,2},{7,5},{8,12},{9,11},{10,... | collective-permute-start | bytes 983048 | tf_op jit(solution)/shard_map/ppermute | solution.py:288
  33.1 7.6 %collective-permute-start.8 = (f32[4,80,128]{2,1,0:T(8,128)S(1)}, f32[4,80,128]{2,1,0:T(8,128)S(1)}, u32[]{:S(2)}, u32[]{:S(2)}) collective-permute-start(f32[4,80,128]{2,1,0:T(8,128)S(1)} %get-tuple-element.42), channel_id=1, source_target_pairs={{0,4},{1,3},{2,6},{3,1},{4,0},{5,7},{6,2},{7,5},{8,12},{9,11},{10,... | collective-permute-start | bytes 491528 | tf_op jit(solution)/shard_map/ppermute | solution.py:288
  36.3 5.3 %collective-permute-start.9 = (f32[4,80,128]{2,1,0:T(8,128)S(1)}, f32[4,80,128]{2,1,0:T(8,128)S(1)}, u32[]{:S(2)}, u32[]{:S(2)}) collective-permute-start(f32[4,80,128]{2,1,0:T(8,128)S(1)} %get-tuple-element.43), channel_id=1, source_target_pairs={{0,2},{1,5},{2,0},{3,7},{4,6},{5,1},{6,4},{7,3},{8,10},{9,13},{10,... | collective-permute-start | bytes 491528 | tf_op jit(solution)/shard_map/ppermute | solution.py:288
  41.7 11.4 %copy-start.3 = (f32[8,128]{1,0:T(8,128)S(1)}, f32[8,128]{1,0:T(8,128)}, u32[]{:S(2)}) copy-start(f32[8,128]{1,0:T(8,128)} %constant.5.clone.steer_ref) | copy-start | bytes 12292
  41.8 9.5 %collective-permute-start.10 = (f32[160,128]{1,0:T(8,128)S(1)}, f32[160,128]{1,0:T(8,128)S(1)}, u32[]{:S(2)}, u32[]{:S(2)}) collective-permute-start(f32[160,128]{1,0:T(8,128)S(1)} %get-tuple-element.44), channel_id=1, source_target_pairs={{0,16},{1,17},{2,18},{3,19},{4,20},{5,21},{6,22},{7,23},{8,24},{9,... | collective-permute-start | bytes 245768 | tf_op jit(solution)/shard_map/ppermute | solution.py:288
  44.4 6.8 %collective-permute-start.11 = (f32[160,128]{1,0:T(8,128)S(1)}, f32[160,128]{1,0:T(8,128)S(1)}, u32[]{:S(2)}, u32[]{:S(2)}) collective-permute-start(f32[160,128]{1,0:T(8,128)S(1)} %get-tuple-element.45), channel_id=1, source_target_pairs={{0,24},{1,25},{2,26},{3,27},{4,28},{5,29},{6,30},{7,31},{8,16},{9,... | collective-permute-start | bytes 245768 | tf_op jit(solution)/shard_map/ppermute | solution.py:288
  45.8 33.3 %copy-start.6 = (s32[32]{0:T(128)S(1)}, s32[32]{0:T(128)}, u32[]{:S(2)}) copy-start(s32[32]{0:T(128)} %bin_ref.1) | copy-start | bytes 388
  45.8 33.3 %copy-start.7 = (s32[32]{0:T(128)S(1)}, s32[32]{0:T(128)}, u32[]{:S(2)}) copy-start(s32[32]{0:T(128)} %block_ref.1) | copy-start | bytes 388
  45.8 33.3 %copy-start.8 = (s32[32]{0:T(128)S(1)}, s32[32]{0:T(128)}, u32[]{:S(2)}) copy-start(s32[32]{0:T(128)} %beam_ref.1) | copy-start | bytes 388
  45.8 33.3 %copy-start.9 = (s32[32,1]{0,1:T(1,128)S(1)}, s32[32,1]{0,1:T(1,128)}, u32[]{:S(2)}) copy-start(s32[32,1]{0,1:T(1,128)} %param.13) | copy-start | bytes 388
  45.8 6.1 %collective-permute-start.12 = (f32[160,128]{1,0:T(8,128)S(1)}, f32[160,128]{1,0:T(8,128)S(1)}, u32[]{:S(2)}, u32[]{:S(2)}) collective-permute-start(f32[160,128]{1,0:T(8,128)S(1)} %get-tuple-element.46), channel_id=1, source_target_pairs={{0,8},{1,9},{2,10},{3,11},{4,12},{5,13},{6,14},{7,15},{8,0},{9,1},... | collective-permute-start | bytes 245768 | tf_op jit(solution)/shard_map/ppermute | solution.py:288
  52.0 5.1 %collective-permute-start.13 = (f32[160,128]{1,0:T(8,128)S(1)}, f32[160,128]{1,0:T(8,128)S(1)}, u32[]{:S(2)}, u32[]{:S(2)}) collective-permute-start(f32[160,128]{1,0:T(8,128)S(1)} %get-tuple-element.47.own_ref), channel_id=1, source_target_pairs={{0,2},{1,0},{2,6},{3,1},{4,12},{5,7},{6,4},{7,3},{8,16},{9,11},{10... | collective-permute-start | bytes 245768 | tf_op jit(solution)/shard_map/ppermute | solution.py:427
  53.1 4.0 %collective-permute-start.14 = (f32[32,128]{1,0:T(8,128)S(1)}, f32[32,128]{1,0:T(8,128)S(1)}, u32[]{:S(2)}, u32[]{:S(2)}) collective-permute-start(f32[32,128]{1,0:T(8,128)S(1)} %get-tuple-element.48.packed_ref), channel_id=1, source_target_pairs={{0,1},{1,3},{2,0},{3,7},{4,6},{5,13},{6,2},{7,5},{8,10},{9,17},{10... | collective-permute-start | bytes 49160 | tf_op jit(solution)/shard_map/ppermute | solution.py:427
  (1 other events, 0.7 us)

commit v6 on v5

--- a/solution.py
+++ b/solution.py
@@ -80,8 +80,8 @@
         out_shape=[half, half, jax.ShapeDtypeStruct((8, 128), F32)],
         in_specs=[hbm_spec()],
         out_specs=[vmem_spec()] * 3,
-        scratch_shapes=[pltpu.SemaphoreType.DMA((8,))],
-        compiler_params=params(61.5),
+        scratch_shapes=[pltpu.SemaphoreType.DMA((2,))],
+        compiler_params=params(63),
     )(raw)
 
 

time: 91.7 us -> 91.5 us (level)
    unnamed x20 -> x18, local copies, waits for them, and re-layouts: 1.76 us -> 2.3 us
where the time goes in v6:
time: 91.5 us; the launch traced here: 91.2 us
  Pallas kernels  24.9 us (27%)
  starting transfers between devices  23.4 us (26%)
  blocking collectives  23.2 us (25%)
  waiting for transfers between devices  16.6 us (18%)
  local copies, waits for them, and re-layouts  2.96 us (3%)
    ppermute x11, starting transfers between devices, partner(): lax.ppermute(value, 'range', [(i, i ^ bits[i & 1]) for i in range(count)])  19.8 us
    ppermute x11, waiting for transfers between devices, partner(): lax.ppermute(value, 'range', [(i, i ^ bits[i & 1]) for i in range(count)])  16.6 us
    all_to_all x1, blocking collectives, on_device(): lax.all_to_all(mine, 'range', split_axis=0, concat_axis=0, tiled=True, ax...  13.4 us
    all_to_all x1, blocking collectives, on_device(): lax.all_to_all(outgoing.reshape(devices, CAP, 2 * BLOCK), 'range', split_...  9.77 us
    pallas_call x1, Pallas kernels, solve_outer(): pl.pallas_call(functools.partial(outer_kernel, total), out_shape=jax.Shap...  8.54 us
    pallas_call x1, Pallas kernels, spectra_first(): pl.pallas_call(spectra_first_kernel, out_shape=[jax.ShapeDtypeStruct((pul...  4.12 us
    pallas_call x1, Pallas kernels, solve_middle(): pl.pallas_call(functools.partial(middle_kernel, total), out_shape=[jax.Sh...  4 us
    ppermute x2, starting transfers between devices, on_device(): halos = [lax.ppermute(value, 'range', before) for value in slices]  2.58 us
  transfers between devices with their start and end apart: 15, of which 9 were waited for; matrix products, arithmetic and copies ran while one was open for 0% of the time, Pallas kernels for 12%

profile of v6, /device:TPU:0, one launch (start us, length us, event | category | flops | bytes accessed | tf_op | source)
XLA Modules:
  0.0 91.2 jit_solution(16462437355179100242)
XLA Ops:
  0.0 2.3 %shard_map.82 = (bf16[2,1024,128]{2,1,0:T(8,128)(2,1)}, bf16[2,1024,128]{2,1,0:T(8,128)(2,1)}, f32[8,128]{1,0:T(8,128)}) custom-call(bf16[2,2048,256]{2,1,0:T(8,128)(2,1)} %bitcast.3), custom_call_target="tpu_custom_call" | custom-call | tf_op jit(solution)/shard_map/pallas_call | solution.py:78
  2.3 1.3 %collective-permute-start.3 = (bf16[2,1024,128]{2,1,0:T(8,128)(2,1)}, bf16[2,1024,128]{2,1,0:T(8,128)(2,1)S(1)}, u32[]{:S(2)}, u32[]{:S(2)}) collective-permute-start(bf16[2,1024,128]{2,1,0:T(8,128)(2,1)} %get-tuple-element.36), channel_id=1, source_target_pairs={{1,0},{2,1},{3,2},{4,3},{5,4},{6,5},{7,6},{8,7},{9,8},{10,9},{11,1... | collective-permute-start | bytes 1572872 | tf_op jit(solution)/shard_map/ppermute | solution.py:773
  3.6 1.3 %collective-permute-start = (bf16[2,1024,128]{2,1,0:T(8,128)(2,1)}, bf16[2,1024,128]{2,1,0:T(8,128)(2,1)S(1)}, u32[]{:S(2)}, u32[]{:S(2)}) collective-permute-start(bf16[2,1024,128]{2,1,0:T(8,128)(2,1)} %get-tuple-element.31), channel_id=1, source_target_pairs={{1,0},{2,1},{3,2},{4,3},{5,4},{6,5},{7,6},{8,7},{9,8},{10,9},{11,1... | collective-permute-start | bytes 1572872 | tf_op jit(solution)/shard_map/ppermute | solution.py:773
  4.9 1.6 %copy-done = bf16[2,64,32,256]{3,2,1,0:T(8,128)(2,1)S(1)} copy-done((bf16[2,64,32,256]{3,2,1,0:T(8,128)(2,1)S(1)}, bf16[2,64,32,256]{3,2,1,0:T(8,128)(2,1)}, u32[]{:S(2)}) %copy-start) | copy-done | bytes 2097176
  7.2 4.1 %shard_map.83 = (bf16[32,2,64,128]{3,2,1,0:T(8,128)(2,1)S(1)}, f32[2048,256]{1,0:T(8,128)S(1)}, bf16[2,256,256]{2,1,0:T(8,128)(2,1)S(1)}, bf16[18,2,32,128]{3,2,...) custom-call(bf16[2,2048,256]{2,1,0:T(8,128)(2,1)S(1)} %bitcast.4, bf16[2,128]{1,0:T(2,128)(2,1)S(1)} %copy-done.4, ...), custom_call_target="tpu_custom_call" | custom-call | flops 1 | bytes 1 | tf_op jit(solution)/shard_map/pallas_call | solution.py:199
  11.3 1.8 %collective-permute-start.1 = (bf16[18,2,32,128]{3,2,1,0:T(8,128)(2,1)S(1)}, bf16[18,2,32,128]{3,2,1,0:T(8,128)(2,1)S(1)}, u32[]{:S(2)}, u32[]{:S(2)}) collective-permute-start(bf16[18,2,32,128]{3,2,1,0:T(8,128)(2,1)S(1)} %get-tuple-element.33), channel_id=1, source_target_pairs={{0,1},{1,0},{2,3},{3,2},{4,5},{5,4},{6,7},{7,6},{8,9},{9,8},{10,11... | collective-permute-start | bytes 884744 | tf_op jit(solution)/shard_map/ppermute | solution.py:288
  17.2 3.6 %collective-permute-start.4 = (bf16[18,2,32,128]{3,2,1,0:T(8,128)(2,1)S(1)}, bf16[18,2,32,128]{3,2,1,0:T(8,128)(2,1)S(1)}, u32[]{:S(2)}, u32[]{:S(2)}) collective-permute-start(bf16[18,2,32,128]{3,2,1,0:T(8,128)(2,1)S(1)} %get-tuple-element.38), channel_id=1, source_target_pairs={{0,1},{1,0},{2,3},{3,2},{4,5},{5,4},{6,7},{7,6},{8,9},{9,8},{10,11... | collective-permute-start | bytes 884744 | tf_op jit(solution)/shard_map/ppermute | solution.py:288
  22.7 2.4 %collective-permute-start.6 = (f32[8,80,128]{2,1,0:T(8,128)S(1)}, f32[8,80,128]{2,1,0:T(8,128)S(1)}, u32[]{:S(2)}, u32[]{:S(2)}) collective-permute-start(f32[8,80,128]{2,1,0:T(8,128)S(1)} %get-tuple-element.40), channel_id=1, source_target_pairs={{0,2},{1,5},{2,0},{3,7},{4,6},{5,1},{6,4},{7,3},{8,10},{9,13},{10,... | collective-permute-start | bytes 983048 | tf_op jit(solution)/shard_map/ppermute | solution.py:288
  25.1 2.4 %collective-permute-start.7 = (f32[8,80,128]{2,1,0:T(8,128)S(1)}, f32[8,80,128]{2,1,0:T(8,128)S(1)}, u32[]{:S(2)}, u32[]{:S(2)}) collective-permute-start(f32[8,80,128]{2,1,0:T(8,128)S(1)} %get-tuple-element.41), channel_id=1, source_target_pairs={{0,4},{1,3},{2,6},{3,1},{4,0},{5,7},{6,2},{7,5},{8,12},{9,11},{10,... | collective-permute-start | bytes 983048 | tf_op jit(solution)/shard_map/ppermute | solution.py:288
  27.5 4.2 %collective-permute-done.6.a1_ref.refs_1_ = f32[8,80,128]{2,1,0:T(8,128)S(1)} collective-permute-done((f32[8,80,128]{2,1,0:T(8,128)S(1)}, f32[8,80,128]{2,1,0:T(8,128)S(1)}, u32[]{:S(2)}, u32[]{:S(2)}) %collective-permute-start.6) | collective-permute-done | bytes 327712 | tf_op jit(solution)/shard_map/ppermute | solution.py:288
  31.7 1.0 %collective-permute-done.7.b1_ref.refs_2_ = f32[8,80,128]{2,1,0:T(8,128)S(1)} collective-permute-done((f32[8,80,128]{2,1,0:T(8,128)S(1)}, f32[8,80,128]{2,1,0:T(8,128)S(1)}, u32[]{:S(2)}, u32[]{:S(2)}) %collective-permute-start.7) | collective-permute-done | bytes 327712 | tf_op jit(solution)/shard_map/ppermute | solution.py:288
  32.9 3.2 %collective-permute-start.8 = (f32[4,80,128]{2,1,0:T(8,128)S(1)}, f32[4,80,128]{2,1,0:T(8,128)S(1)}, u32[]{:S(2)}, u32[]{:S(2)}) collective-permute-start(f32[4,80,128]{2,1,0:T(8,128)S(1)} %get-tuple-element.42), channel_id=1, source_target_pairs={{0,4},{1,3},{2,6},{3,1},{4,0},{5,7},{6,2},{7,5},{8,12},{9,11},{10,... | collective-permute-start | bytes 491528 | tf_op jit(solution)/shard_map/ppermute | solution.py:288
  36.1 1.7 %collective-permute-start.9 = (f32[4,80,128]{2,1,0:T(8,128)S(1)}, f32[4,80,128]{2,1,0:T(8,128)S(1)}, u32[]{:S(2)}, u32[]{:S(2)}) collective-permute-start(f32[4,80,128]{2,1,0:T(8,128)S(1)} %get-tuple-element.43), channel_id=1, source_target_pairs={{0,2},{1,5},{2,0},{3,7},{4,6},{5,1},{6,4},{7,3},{8,10},{9,13},{10,... | collective-permute-start | bytes 491528 | tf_op jit(solution)/shard_map/ppermute | solution.py:288
  37.8 2.7 %collective-permute-done.8.refs_3_ = f32[4,80,128]{2,1,0:T(8,128)S(1)} collective-permute-done((f32[4,80,128]{2,1,0:T(8,128)S(1)}, f32[4,80,128]{2,1,0:T(8,128)S(1)}, u32[]{:S(2)}, u32[]{:S(2)}) %collective-permute-start.8) | collective-permute-done | bytes 163872 | tf_op jit(solution)/shard_map/ppermute | solution.py:288
  40.5 0.9 collective-permute-done.9.refs_4_
  41.5 2.7 %collective-permute-start.10 = (f32[160,128]{1,0:T(8,128)S(1)}, f32[160,128]{1,0:T(8,128)S(1)}, u32[]{:S(2)}, u32[]{:S(2)}) collective-permute-start(f32[160,128]{1,0:T(8,128)S(1)} %get-tuple-element.44), channel_id=1, source_target_pairs={{0,16},{1,17},{2,18},{3,19},{4,20},{5,21},{6,22},{7,23},{8,24},{9,... | collective-permute-start | bytes 245768 | tf_op jit(solution)/shard_map/ppermute | solution.py:288
  44.2 1.4 %collective-permute-start.11 = (f32[160,128]{1,0:T(8,128)S(1)}, f32[160,128]{1,0:T(8,128)S(1)}, u32[]{:S(2)}, u32[]{:S(2)}) collective-permute-start(f32[160,128]{1,0:T(8,128)S(1)} %get-tuple-element.45), channel_id=1, source_target_pairs={{0,24},{1,25},{2,26},{3,27},{4,28},{5,29},{6,30},{7,31},{8,16},{9,... | collective-permute-start | bytes 245768 | tf_op jit(solution)/shard_map/ppermute | solution.py:288
  45.6 5.4 %collective-permute-done.10.refs_5_ = f32[160,128]{1,0:T(8,128)S(1)} collective-permute-done((f32[160,128]{1,0:T(8,128)S(1)}, f32[160,128]{1,0:T(8,128)S(1)}, u32[]{:S(2)}, u32[]{:S(2)}) %collective-permute-start.10) | collective-permute-done | bytes 81952 | tf_op jit(solution)/shard_map/ppermute | solution.py:288
  51.8 1.0 %collective-permute-start.13 = (f32[160,128]{1,0:T(8,128)S(1)}, f32[160,128]{1,0:T(8,128)S(1)}, u32[]{:S(2)}, u32[]{:S(2)}) collective-permute-start(f32[160,128]{1,0:T(8,128)S(1)} %get-tuple-element.47.own_ref), channel_id=1, source_target_pairs={{0,2},{1,0},{2,6},{3,1},{4,12},{5,7},{6,4},{7,3},{8,16},{9,11},{10... | collective-permute-start | bytes 245768 | tf_op jit(solution)/shard_map/ppermute | solution.py:427
  52.9 4.0 %shard_map.94 = (f32[64,128]{1,0:T(8,128)S(1)}, f32[8,128]{1,0:T(8,128)S(1)}) custom-call(f32[32,128]{1,0:T(8,128)S(1)} %get-tuple-element.48.packed_ref, f32[8,128]{1,0:T(8,128)S(1)} %copy-done.2), custom_call_target="tpu_custom_call" | custom-call | tf_op jit(solution)/shard_map/pallas_call | solution.py:679
  56.9 8.5 %shard_map.95 = bf16[32,8,384]{2,1,0:T(8,128)(2,1)S(1)} custom-call(f32[160,128]{1,0:T(8,128)S(1)} %get-tuple-element.47.own_ref, f32[160,128]{1,0:T(8,128)S(1)} %collective-permute-done.13.left_ref, f32[32,128]{1,0:T(8,128)S(1)} %collective-permute-done.14.right_ref, f32[8,128]{1,0:T(8,128)S(1)} %copy-done.2, f32[64,128]{1,0:T(8,128)S(1)} %get-tuple-element.49.inv_ref, ...), custom_call_target="tpu_custom_call" | custom-call | tf_op jit(solution)/shard_map/pallas_call | solution.py:693
  65.4 13.4 %all_to_all.10.w_ref = bf16[32,8,384]{2,1,0:T(8,128)(2,1)S(1)} all-to-all(bf16[32,8,384]{2,1,0:T(8,128)(2,1)S(1)} %shard_map.95), channel_id=1, replica_groups=mesh['range'=32] {'range'}, dimensions={0} | all-to-all | bytes 393216 | tf_op jit(solution)/shard_map/all_to_all | solution.py:794
  78.8 2.0 %shard_map.96 = bf16[64,256]{1,0:T(8,128)(2,1)S(1)} custom-call(s32[32]{0:T(128)S(1)} %copy-done.5, s32[32]{0:T(128)S(1)} %copy-done.6, s32[32]{0:T(128)S(1)} %copy-done.7, s32[32]{0:T(128)S(1)} %bitcast.6, bf16[32,128,128]{2,1,0:T(8,128)(2,1)S(1)} %bitcast.5, bf16[32,2,32,128]{3,2,1,0:T(8,128)(2,1)S(1)} %get-tuple-element.35.refs_0_.upper_ref, ...), custom_call_target="tpu_custom_call" | custom-call | tf_op jit(solution)/shard_map/pallas_call | solution.py:752
  80.8 9.8 %all_to_all.11 = bf16[32,2,256]{2,1,0:T(2,128)(2,1)S(1)} all-to-all(bf16[32,2,256]{2,1,0:T(2,128)(2,1)S(1)} %reshape.17), channel_id=1, replica_groups=mesh['range'=32] {'range'}, dimensions={0} | all-to-all | bytes 65536 | tf_op jit(solution)/shard_map/all_to_all | solution.py:802
  (43 shorter events, 8.5 us)
Async XLA Ops:
  0.0 4.9 %copy-start.1 = (bf16[512,512]{1,0:T(8,128)(2,1)S(1)}, bf16[512,512]{1,0:T(8,128)(2,1)}, u32[]{:S(2)}) copy-start(bf16[512,512]{1,0:T(8,128)(2,1)} %constant.4.clone.dft_ref) | copy-start | bytes 1572868
  0.0 4.9 %copy-start.4 = (bf16[2,128]{1,0:T(2,128)(2,1)S(1)}, bf16[2,128]{1,0:T(2,128)(2,1)}, u32[]{:S(2)}) copy-start(bf16[2,128]{1,0:T(2,128)(2,1)} %rep_ref.1) | copy-start | bytes 1540
  2.3 12.9 %collective-permute-start.3 = (bf16[2,1024,128]{2,1,0:T(8,128)(2,1)}, bf16[2,1024,128]{2,1,0:T(8,128)(2,1)S(1)}, u32[]{:S(2)}, u32[]{:S(2)}) collective-permute-start(bf16[2,1024,128]{2,1,0:T(8,128)(2,1)} %get-tuple-element.36), channel_id=1, source_target_pairs={{1,0},{2,1},{3,2},{4,3},{5,4},{6,5},{7,6},{8,7},{9,8},{10,9},{11,1... | collective-permute-start | bytes 1572872 | tf_op jit(solution)/shard_map/ppermute | solution.py:773
  3.6 12.8 %collective-permute-start = (bf16[2,1024,128]{2,1,0:T(8,128)(2,1)}, bf16[2,1024,128]{2,1,0:T(8,128)(2,1)S(1)}, u32[]{:S(2)}, u32[]{:S(2)}) collective-permute-start(bf16[2,1024,128]{2,1,0:T(8,128)(2,1)} %get-tuple-element.31), channel_id=1, source_target_pairs={{1,0},{2,1},{3,2},{4,3},{5,4},{6,5},{7,6},{8,7},{9,8},{10,9},{11,1... | collective-permute-start | bytes 1572872 | tf_op jit(solution)/shard_map/ppermute | solution.py:773
  4.9 1.6 %copy-start = (bf16[2,64,32,256]{3,2,1,0:T(8,128)(2,1)S(1)}, bf16[2,64,32,256]{3,2,1,0:T(8,128)(2,1)}, u32[]{:S(2)}) copy-start(bf16[2,64,32,256]{3,2,1,0:T(8,128)(2,1)} %param.8) | copy-start | bytes 6291460
  6.5 0.7 copy-start.3
  11.3 3.0 %collective-permute-start.1 = (bf16[18,2,32,128]{3,2,1,0:T(8,128)(2,1)S(1)}, bf16[18,2,32,128]{3,2,1,0:T(8,128)(2,1)S(1)}, u32[]{:S(2)}, u32[]{:S(2)}) collective-permute-start(bf16[18,2,32,128]{3,2,1,0:T(8,128)(2,1)S(1)} %get-tuple-element.33), channel_id=1, source_target_pairs={{0,1},{1,0},{2,3},{3,2},{4,5},{5,4},{6,7},{7,6},{8,9},{9,8},{10,11... | collective-permute-start | bytes 884744 | tf_op jit(solution)/shard_map/ppermute | solution.py:288
  13.1 1.6 %collective-permute-start.2 = (bf16[18,2,32,128]{3,2,1,0:T(8,128)(2,1)S(1)}, bf16[18,2,32,128]{3,2,1,0:T(8,128)(2,1)S(1)}, u32[]{:S(2)}, u32[]{:S(2)}) collective-permute-start(bf16[18,2,32,128]{3,2,1,0:T(8,128)(2,1)S(1)} %get-tuple-element.34), channel_id=1, source_target_pairs={{0,1},{1,0},{2,3},{3,2},{4,5},{5,4},{6,7},{7,6},{8,9},{9,8},{10,11... | collective-permute-start | bytes 884744 | tf_op jit(solution)/shard_map/ppermute | solution.py:288
  16.0 5.2 %collective-permute-start.5 = (bf16[18,2,32,128]{3,2,1,0:T(8,128)(2,1)S(1)}, bf16[18,2,32,128]{3,2,1,0:T(8,128)(2,1)S(1)}, u32[]{:S(2)}, u32[]{:S(2)}) collective-permute-start(bf16[18,2,32,128]{3,2,1,0:T(8,128)(2,1)S(1)} %get-tuple-element.39), channel_id=1, source_target_pairs={{0,1},{1,0},{2,3},{3,2},{4,5},{5,4},{6,7},{7,6},{8,9},{9,8},{10,11... | collective-permute-start | bytes 884744 | tf_op jit(solution)/shard_map/ppermute | solution.py:288
  17.2 4.8 %collective-permute-start.4 = (bf16[18,2,32,128]{3,2,1,0:T(8,128)(2,1)S(1)}, bf16[18,2,32,128]{3,2,1,0:T(8,128)(2,1)S(1)}, u32[]{:S(2)}, u32[]{:S(2)}) collective-permute-start(bf16[18,2,32,128]{3,2,1,0:T(8,128)(2,1)S(1)} %get-tuple-element.38), channel_id=1, source_target_pairs={{0,1},{1,0},{2,3},{3,2},{4,5},{5,4},{6,7},{7,6},{8,9},{9,8},{10,11... | collective-permute-start | bytes 884744 | tf_op jit(solution)/shard_map/ppermute | solution.py:288
  22.7 9.1 %collective-permute-start.6 = (f32[8,80,128]{2,1,0:T(8,128)S(1)}, f32[8,80,128]{2,1,0:T(8,128)S(1)}, u32[]{:S(2)}, u32[]{:S(2)}) collective-permute-start(f32[8,80,128]{2,1,0:T(8,128)S(1)} %get-tuple-element.40), channel_id=1, source_target_pairs={{0,2},{1,5},{2,0},{3,7},{4,6},{5,1},{6,4},{7,3},{8,10},{9,13},{10,... | collective-permute-start | bytes 983048 | tf_op jit(solution)/shard_map/ppermute | solution.py:288
  25.1 7.6 %collective-permute-start.7 = (f32[8,80,128]{2,1,0:T(8,128)S(1)}, f32[8,80,128]{2,1,0:T(8,128)S(1)}, u32[]{:S(2)}, u32[]{:S(2)}) collective-permute-start(f32[8,80,128]{2,1,0:T(8,128)S(1)} %get-tuple-element.41), channel_id=1, source_target_pairs={{0,4},{1,3},{2,6},{3,1},{4,0},{5,7},{6,2},{7,5},{8,12},{9,11},{10,... | collective-permute-start | bytes 983048 | tf_op jit(solution)/shard_map/ppermute | solution.py:288
  32.9 7.6 %collective-permute-start.8 = (f32[4,80,128]{2,1,0:T(8,128)S(1)}, f32[4,80,128]{2,1,0:T(8,128)S(1)}, u32[]{:S(2)}, u32[]{:S(2)}) collective-permute-start(f32[4,80,128]{2,1,0:T(8,128)S(1)} %get-tuple-element.42), channel_id=1, source_target_pairs={{0,4},{1,3},{2,6},{3,1},{4,0},{5,7},{6,2},{7,5},{8,12},{9,11},{10,... | collective-permute-start | bytes 491528 | tf_op jit(solution)/shard_map/ppermute | solution.py:288
  36.1 5.3 %collective-permute-start.9 = (f32[4,80,128]{2,1,0:T(8,128)S(1)}, f32[4,80,128]{2,1,0:T(8,128)S(1)}, u32[]{:S(2)}, u32[]{:S(2)}) collective-permute-start(f32[4,80,128]{2,1,0:T(8,128)S(1)} %get-tuple-element.43), channel_id=1, source_target_pairs={{0,2},{1,5},{2,0},{3,7},{4,6},{5,1},{6,4},{7,3},{8,10},{9,13},{10,... | collective-permute-start | bytes 491528 | tf_op jit(solution)/shard_map/ppermute | solution.py:288
  41.5 11.3 %copy-start.2 = (f32[8,128]{1,0:T(8,128)S(1)}, f32[8,128]{1,0:T(8,128)}, u32[]{:S(2)}) copy-start(f32[8,128]{1,0:T(8,128)} %constant.5.clone.steer_ref) | copy-start | bytes 12292
  41.5 9.5 %collective-permute-start.10 = (f32[160,128]{1,0:T(8,128)S(1)}, f32[160,128]{1,0:T(8,128)S(1)}, u32[]{:S(2)}, u32[]{:S(2)}) collective-permute-start(f32[160,128]{1,0:T(8,128)S(1)} %get-tuple-element.44), channel_id=1, source_target_pairs={{0,16},{1,17},{2,18},{3,19},{4,20},{5,21},{6,22},{7,23},{8,24},{9,... | collective-permute-start | bytes 245768 | tf_op jit(solution)/shard_map/ppermute | solution.py:288
  44.2 6.8 %collective-permute-start.11 = (f32[160,128]{1,0:T(8,128)S(1)}, f32[160,128]{1,0:T(8,128)S(1)}, u32[]{:S(2)}, u32[]{:S(2)}) collective-permute-start(f32[160,128]{1,0:T(8,128)S(1)} %get-tuple-element.45), channel_id=1, source_target_pairs={{0,24},{1,25},{2,26},{3,27},{4,28},{5,29},{6,30},{7,31},{8,16},{9,... | collective-permute-start | bytes 245768 | tf_op jit(solution)/shard_map/ppermute | solution.py:288
  45.6 33.3 %copy-start.5 = (s32[32]{0:T(128)S(1)}, s32[32]{0:T(128)}, u32[]{:S(2)}) copy-start(s32[32]{0:T(128)} %bin_ref.1) | copy-start | bytes 388
  45.6 33.3 %copy-start.6 = (s32[32]{0:T(128)S(1)}, s32[32]{0:T(128)}, u32[]{:S(2)}) copy-start(s32[32]{0:T(128)} %block_ref.1) | copy-start | bytes 388
  45.6 33.3 %copy-start.7 = (s32[32]{0:T(128)S(1)}, s32[32]{0:T(128)}, u32[]{:S(2)}) copy-start(s32[32]{0:T(128)} %beam_ref.1) | copy-start | bytes 388
  45.6 33.3 %copy-start.8 = (s32[32,1]{0,1:T(1,128)S(1)}, s32[32,1]{0,1:T(1,128)}, u32[]{:S(2)}) copy-start(s32[32,1]{0,1:T(1,128)} %param.13) | copy-start | bytes 388
  45.6 6.1 %collective-permute-start.12 = (f32[160,128]{1,0:T(8,128)S(1)}, f32[160,128]{1,0:T(8,128)S(1)}, u32[]{:S(2)}, u32[]{:S(2)}) collective-permute-start(f32[160,128]{1,0:T(8,128)S(1)} %get-tuple-element.46), channel_id=1, source_target_pairs={{0,8},{1,9},{2,10},{3,11},{4,12},{5,13},{6,14},{7,15},{8,0},{9,1},... | collective-permute-start | bytes 245768 | tf_op jit(solution)/shard_map/ppermute | solution.py:288
  51.8 5.1 %collective-permute-start.13 = (f32[160,128]{1,0:T(8,128)S(1)}, f32[160,128]{1,0:T(8,128)S(1)}, u32[]{:S(2)}, u32[]{:S(2)}) collective-permute-start(f32[160,128]{1,0:T(8,128)S(1)} %get-tuple-element.47.own_ref), channel_id=1, source_target_pairs={{0,2},{1,0},{2,6},{3,1},{4,12},{5,7},{6,4},{7,3},{8,16},{9,11},{10... | collective-permute-start | bytes 245768 | tf_op jit(solution)/shard_map/ppermute | solution.py:427
  52.9 4.0 %collective-permute-start.14 = (f32[32,128]{1,0:T(8,128)S(1)}, f32[32,128]{1,0:T(8,128)S(1)}, u32[]{:S(2)}, u32[]{:S(2)}) collective-permute-start(f32[32,128]{1,0:T(8,128)S(1)} %get-tuple-element.48.packed_ref), channel_id=1, source_target_pairs={{0,1},{1,3},{2,0},{3,7},{4,6},{5,13},{6,2},{7,5},{8,10},{9,17},{10... | collective-permute-start | bytes 49160 | tf_op jit(solution)/shard_map/ppermute | solution.py:427

commit v7 on v6

--- a/solution.py
+++ b/solution.py
@@ -342,10 +342,15 @@
     return keep_ref[e, sent_rows(keep_ref) // 2 + keep_ref.shape[1] // 6 :]
 
 
-def first_kernel(keep_ref, a_ref, b_ref):
+def first_upper_kernel(keep_ref, a_ref):
     core, u, v, z = uv_parts()
     for k in range(8):
         a_ref[k] = upper_rows(keep_ref, uv_slot(core, 1 - u, k // 4, k % 4))
+
+
+def first_lower_kernel(keep_ref, b_ref):
+    core, u, v, z = uv_parts()
+    for k in range(8):
         b_ref[k] = lower_rows(keep_ref, uv_slot(core, k // 4, 1 - v, k % 4))
 
 
@@ -403,8 +408,9 @@
     rows = 5 * full // 6
     half = rows // 2
     data = [keep]
-    a, b = summed(first_kernel, data, [(8, half, wide)] * 2)
-    data += [partner(a, U_BITS), partner(b, V_BITS)]
+    b1 = partner(summed(first_lower_kernel, data, [(8, half, wide)])[0], V_BITS)
+    a1 = partner(summed(first_upper_kernel, data, [(8, half, wide)])[0], U_BITS)
+    data += [a1, b1]
     a, b = summed(second_kernel, data, [(4, half, wide)] * 2)
     data += [partner(a, V_BITS), partner(b, U_BITS)]
     sends = summed(line_kernel, data, [(rows, wide)] * 3)

time: 91.5 us -> 91.5 us (level)
  no operation moved by 1% of the time
where the time goes in v7:
time: 91.5 us; the launch traced here: 91.3 us
  Pallas kernels  24.9 us (27%)
  starting transfers between devices  23.4 us (26%)
  blocking collectives  23.1 us (25%)
  waiting for transfers between devices  16.6 us (18%)
  local copies, waits for them, and re-layouts  2.96 us (3%)
    ppermute x11, starting transfers between devices, partner(): lax.ppermute(value, 'range', [(i, i ^ bits[i & 1]) for i in range(count)])  19.8 us
    ppermute x11, waiting for transfers between devices, partner(): lax.ppermute(value, 'range', [(i, i ^ bits[i & 1]) for i in range(count)])  16.6 us
    all_to_all x1, blocking collectives, on_device(): lax.all_to_all(mine, 'range', split_axis=0, concat_axis=0, tiled=True, ax...  13.4 us
    all_to_all x1, blocking collectives, on_device(): lax.all_to_all(outgoing.reshape(devices, CAP, 2 * BLOCK), 'range', split_...  9.77 us
    pallas_call x1, Pallas kernels, solve_outer(): pl.pallas_call(functools.partial(outer_kernel, total), out_shape=jax.Shap...  8.54 us
    pallas_call x1, Pallas kernels, spectra_first(): pl.pallas_call(spectra_first_kernel, out_shape=[jax.ShapeDtypeStruct((pul...  4.12 us
    pallas_call x1, Pallas kernels, solve_middle(): pl.pallas_call(functools.partial(middle_kernel, total), out_shape=[jax.Sh...  4 us
    ppermute x2, starting transfers between devices, on_device(): halos = [lax.ppermute(value, 'range', before) for value in slices]  2.58 us
  transfers between devices with their start and end apart: 15, of which 9 were waited for; matrix products, arithmetic and copies ran while one was open for 0% of the time, Pallas kernels for 12%

profile of v7, /device:TPU:0, one launch (start us, length us, event | category | flops | bytes accessed | tf_op | source)
XLA Modules:
  0.0 91.3 jit_solution(11392999614505347903)
XLA Ops:
  0.0 2.3 %shard_map.82 = (bf16[2,1024,128]{2,1,0:T(8,128)(2,1)}, bf16[2,1024,128]{2,1,0:T(8,128)(2,1)}, f32[8,128]{1,0:T(8,128)}) custom-call(bf16[2,2048,256]{2,1,0:T(8,128)(2,1)} %bitcast.3), custom_call_target="tpu_custom_call" | custom-call | tf_op jit(solution)/shard_map/pallas_call | solution.py:78
  2.3 1.3 %collective-permute-start.3 = (bf16[2,1024,128]{2,1,0:T(8,128)(2,1)}, bf16[2,1024,128]{2,1,0:T(8,128)(2,1)S(1)}, u32[]{:S(2)}, u32[]{:S(2)}) collective-permute-start(bf16[2,1024,128]{2,1,0:T(8,128)(2,1)} %get-tuple-element.34), channel_id=1, source_target_pairs={{1,0},{2,1},{3,2},{4,3},{5,4},{6,5},{7,6},{8,7},{9,8},{10,9},{11,1... | collective-permute-start | bytes 1572872 | tf_op jit(solution)/shard_map/ppermute | solution.py:779
  3.6 1.3 %collective-permute-start = (bf16[2,1024,128]{2,1,0:T(8,128)(2,1)}, bf16[2,1024,128]{2,1,0:T(8,128)(2,1)S(1)}, u32[]{:S(2)}, u32[]{:S(2)}) collective-permute-start(bf16[2,1024,128]{2,1,0:T(8,128)(2,1)} %get-tuple-element.29), channel_id=1, source_target_pairs={{1,0},{2,1},{3,2},{4,3},{5,4},{6,5},{7,6},{8,7},{9,8},{10,9},{11,1... | collective-permute-start | bytes 1572872 | tf_op jit(solution)/shard_map/ppermute | solution.py:779
  4.9 1.6 %copy-done = bf16[2,64,32,256]{3,2,1,0:T(8,128)(2,1)S(1)} copy-done((bf16[2,64,32,256]{3,2,1,0:T(8,128)(2,1)S(1)}, bf16[2,64,32,256]{3,2,1,0:T(8,128)(2,1)}, u32[]{:S(2)}) %copy-start) | copy-done | bytes 2097176
  7.2 4.1 %shard_map.83 = (bf16[32,2,64,128]{3,2,1,0:T(8,128)(2,1)S(1)}, f32[2048,256]{1,0:T(8,128)S(1)}, bf16[2,256,256]{2,1,0:T(8,128)(2,1)S(1)}, bf16[18,2,32,128]{3,2,...) custom-call(bf16[2,2048,256]{2,1,0:T(8,128)(2,1)S(1)} %bitcast.4, bf16[2,128]{1,0:T(2,128)(2,1)S(1)} %copy-done.4, ...), custom_call_target="tpu_custom_call" | custom-call | flops 1 | bytes 1 | tf_op jit(solution)/shard_map/pallas_call | solution.py:199
  11.3 1.8 %collective-permute-start.1 = (bf16[18,2,32,128]{3,2,1,0:T(8,128)(2,1)S(1)}, bf16[18,2,32,128]{3,2,1,0:T(8,128)(2,1)S(1)}, u32[]{:S(2)}, u32[]{:S(2)}) collective-permute-start(bf16[18,2,32,128]{3,2,1,0:T(8,128)(2,1)S(1)} %get-tuple-element.31), channel_id=1, source_target_pairs={{0,1},{1,0},{2,3},{3,2},{4,5},{5,4},{6,7},{7,6},{8,9},{9,8},{10,11... | collective-permute-start | bytes 884744 | tf_op jit(solution)/shard_map/ppermute | solution.py:288
  17.2 3.6 %collective-permute-start.4 = (bf16[18,2,32,128]{3,2,1,0:T(8,128)(2,1)S(1)}, bf16[18,2,32,128]{3,2,1,0:T(8,128)(2,1)S(1)}, u32[]{:S(2)}, u32[]{:S(2)}) collective-permute-start(bf16[18,2,32,128]{3,2,1,0:T(8,128)(2,1)S(1)} %get-tuple-element.36), channel_id=1, source_target_pairs={{0,1},{1,0},{2,3},{3,2},{4,5},{5,4},{6,7},{7,6},{8,9},{9,8},{10,11... | collective-permute-start | bytes 884744 | tf_op jit(solution)/shard_map/ppermute | solution.py:288
  22.7 2.4 %collective-permute-start.6 = (f32[8,80,128]{2,1,0:T(8,128)S(1)}, f32[8,80,128]{2,1,0:T(8,128)S(1)}, u32[]{:S(2)}, u32[]{:S(2)}) collective-permute-start(f32[8,80,128]{2,1,0:T(8,128)S(1)} %shard_map.90), channel_id=1, source_target_pairs={{0,2},{1,5},{2,0},{3,7},{4,6},{5,1},{6,4},{7,3},{8,10},{9,13},{10,... | collective-permute-start | bytes 983048 | tf_op jit(solution)/shard_map/ppermute | solution.py:288
  25.1 2.4 %collective-permute-start.7 = (f32[8,80,128]{2,1,0:T(8,128)S(1)}, f32[8,80,128]{2,1,0:T(8,128)S(1)}, u32[]{:S(2)}, u32[]{:S(2)}) collective-permute-start(f32[8,80,128]{2,1,0:T(8,128)S(1)} %shard_map.91), channel_id=1, source_target_pairs={{0,4},{1,3},{2,6},{3,1},{4,0},{5,7},{6,2},{7,5},{8,12},{9,11},{10,... | collective-permute-start | bytes 983048 | tf_op jit(solution)/shard_map/ppermute | solution.py:288
  27.5 4.3 %collective-permute-done.6.a1_ref.refs_1_ = f32[8,80,128]{2,1,0:T(8,128)S(1)} collective-permute-done((f32[8,80,128]{2,1,0:T(8,128)S(1)}, f32[8,80,128]{2,1,0:T(8,128)S(1)}, u32[]{:S(2)}, u32[]{:S(2)}) %collective-permute-start.6) | collective-permute-done | bytes 327712 | tf_op jit(solution)/shard_map/ppermute | solution.py:288
  31.8 0.9 %collective-permute-done.7.b1_ref.refs_2_ = f32[8,80,128]{2,1,0:T(8,128)S(1)} collective-permute-done((f32[8,80,128]{2,1,0:T(8,128)S(1)}, f32[8,80,128]{2,1,0:T(8,128)S(1)}, u32[]{:S(2)}, u32[]{:S(2)}) %collective-permute-start.7) | collective-permute-done | bytes 327712 | tf_op jit(solution)/shard_map/ppermute | solution.py:288
  32.9 3.2 %collective-permute-start.8 = (f32[4,80,128]{2,1,0:T(8,128)S(1)}, f32[4,80,128]{2,1,0:T(8,128)S(1)}, u32[]{:S(2)}, u32[]{:S(2)}) collective-permute-start(f32[4,80,128]{2,1,0:T(8,128)S(1)} %get-tuple-element.38), channel_id=1, source_target_pairs={{0,4},{1,3},{2,6},{3,1},{4,0},{5,7},{6,2},{7,5},{8,12},{9,11},{10,... | collective-permute-start | bytes 491528 | tf_op jit(solution)/shard_map/ppermute | solution.py:288
  36.1 1.7 %collective-permute-start.9 = (f32[4,80,128]{2,1,0:T(8,128)S(1)}, f32[4,80,128]{2,1,0:T(8,128)S(1)}, u32[]{:S(2)}, u32[]{:S(2)}) collective-permute-start(f32[4,80,128]{2,1,0:T(8,128)S(1)} %get-tuple-element.39), channel_id=1, source_target_pairs={{0,2},{1,5},{2,0},{3,7},{4,6},{5,1},{6,4},{7,3},{8,10},{9,13},{10,... | collective-permute-start | bytes 491528 | tf_op jit(solution)/shard_map/ppermute | solution.py:288
  37.8 2.7 %collective-permute-done.8.refs_3_ = f32[4,80,128]{2,1,0:T(8,128)S(1)} collective-permute-done((f32[4,80,128]{2,1,0:T(8,128)S(1)}, f32[4,80,128]{2,1,0:T(8,128)S(1)}, u32[]{:S(2)}, u32[]{:S(2)}) %collective-permute-start.8) | collective-permute-done | bytes 163872 | tf_op jit(solution)/shard_map/ppermute | solution.py:288
  40.5 0.9 collective-permute-done.9.refs_4_
  41.6 2.6 %collective-permute-start.10 = (f32[160,128]{1,0:T(8,128)S(1)}, f32[160,128]{1,0:T(8,128)S(1)}, u32[]{:S(2)}, u32[]{:S(2)}) collective-permute-start(f32[160,128]{1,0:T(8,128)S(1)} %get-tuple-element.40), channel_id=1, source_target_pairs={{0,16},{1,17},{2,18},{3,19},{4,20},{5,21},{6,22},{7,23},{8,24},{9,... | collective-permute-start | bytes 245768 | tf_op jit(solution)/shard_map/ppermute | solution.py:288
  44.2 1.3 %collective-permute-start.11 = (f32[160,128]{1,0:T(8,128)S(1)}, f32[160,128]{1,0:T(8,128)S(1)}, u32[]{:S(2)}, u32[]{:S(2)}) collective-permute-start(f32[160,128]{1,0:T(8,128)S(1)} %get-tuple-element.41), channel_id=1, source_target_pairs={{0,24},{1,25},{2,26},{3,27},{4,28},{5,29},{6,30},{7,31},{8,16},{9,... | collective-permute-start | bytes 245768 | tf_op jit(solution)/shard_map/ppermute | solution.py:288
  45.7 5.4 %collective-permute-done.10.refs_5_ = f32[160,128]{1,0:T(8,128)S(1)} collective-permute-done((f32[160,128]{1,0:T(8,128)S(1)}, f32[160,128]{1,0:T(8,128)S(1)}, u32[]{:S(2)}, u32[]{:S(2)}) %collective-permute-start.10) | collective-permute-done | bytes 81952 | tf_op jit(solution)/shard_map/ppermute | solution.py:288
  51.8 1.1 %collective-permute-start.13 = (f32[160,128]{1,0:T(8,128)S(1)}, f32[160,128]{1,0:T(8,128)S(1)}, u32[]{:S(2)}, u32[]{:S(2)}) collective-permute-start(f32[160,128]{1,0:T(8,128)S(1)} %get-tuple-element.43.own_ref), channel_id=1, source_target_pairs={{0,2},{1,0},{2,6},{3,1},{4,12},{5,7},{6,4},{7,3},{8,16},{9,11},{10... | collective-permute-start | bytes 245768 | tf_op jit(solution)/shard_map/ppermute | solution.py:433
  52.9 4.0 %shard_map.95 = (f32[64,128]{1,0:T(8,128)S(1)}, f32[8,128]{1,0:T(8,128)S(1)}) custom-call(f32[32,128]{1,0:T(8,128)S(1)} %get-tuple-element.44.packed_ref, f32[8,128]{1,0:T(8,128)S(1)} %copy-done.2), custom_call_target="tpu_custom_call" | custom-call | tf_op jit(solution)/shard_map/pallas_call | solution.py:685
  56.9 8.5 %shard_map.96 = bf16[32,8,384]{2,1,0:T(8,128)(2,1)S(1)} custom-call(f32[160,128]{1,0:T(8,128)S(1)} %get-tuple-element.43.own_ref, f32[160,128]{1,0:T(8,128)S(1)} %collective-permute-done.13.left_ref, f32[32,128]{1,0:T(8,128)S(1)} %collective-permute-done.14.right_ref, f32[8,128]{1,0:T(8,128)S(1)} %copy-done.2, f32[64,128]{1,0:T(8,128)S(1)} %get-tuple-element.45.inv_ref, ...), custom_call_target="tpu_custom_call" | custom-call | tf_op jit(solution)/shard_map/pallas_call | solution.py:699
  65.5 13.4 %all_to_all.10.w_ref = bf16[32,8,384]{2,1,0:T(8,128)(2,1)S(1)} all-to-all(bf16[32,8,384]{2,1,0:T(8,128)(2,1)S(1)} %shard_map.96), channel_id=1, replica_groups=mesh['range'=32] {'range'}, dimensions={0} | all-to-all | bytes 393216 | tf_op jit(solution)/shard_map/all_to_all | solution.py:800
  78.9 2.0 %shard_map.97 = bf16[64,256]{1,0:T(8,128)(2,1)S(1)} custom-call(s32[32]{0:T(128)S(1)} %copy-done.5, s32[32]{0:T(128)S(1)} %copy-done.6, s32[32]{0:T(128)S(1)} %copy-done.7, s32[32]{0:T(128)S(1)} %bitcast.6, bf16[32,128,128]{2,1,0:T(8,128)(2,1)S(1)} %bitcast.5, bf16[32,2,32,128]{3,2,1,0:T(8,128)(2,1)S(1)} %get-tuple-element.33.refs_0_.upper_ref, ...), custom_call_target="tpu_custom_call" | custom-call | tf_op jit(solution)/shard_map/pallas_call | solution.py:758
  80.9 9.8 %all_to_all.11 = bf16[32,2,256]{2,1,0:T(2,128)(2,1)S(1)} all-to-all(bf16[32,2,256]{2,1,0:T(2,128)(2,1)S(1)} %reshape.17), channel_id=1, replica_groups=mesh['range'=32] {'range'}, dimensions={0} | all-to-all | bytes 65536 | tf_op jit(solution)/shard_map/all_to_all | solution.py:808
  (44 shorter events, 8.5 us)
Async XLA Ops:
  0.0 4.9 %copy-start.1 = (bf16[512,512]{1,0:T(8,128)(2,1)S(1)}, bf16[512,512]{1,0:T(8,128)(2,1)}, u32[]{:S(2)}) copy-start(bf16[512,512]{1,0:T(8,128)(2,1)} %constant.4.clone.dft_ref) | copy-start | bytes 1572868
  0.0 4.9 %copy-start.4 = (bf16[2,128]{1,0:T(2,128)(2,1)S(1)}, bf16[2,128]{1,0:T(2,128)(2,1)}, u32[]{:S(2)}) copy-start(bf16[2,128]{1,0:T(2,128)(2,1)} %rep_ref.1) | copy-start | bytes 1540
  2.3 13.0 %collective-permute-start.3 = (bf16[2,1024,128]{2,1,0:T(8,128)(2,1)}, bf16[2,1024,128]{2,1,0:T(8,128)(2,1)S(1)}, u32[]{:S(2)}, u32[]{:S(2)}) collective-permute-start(bf16[2,1024,128]{2,1,0:T(8,128)(2,1)} %get-tuple-element.34), channel_id=1, source_target_pairs={{1,0},{2,1},{3,2},{4,3},{5,4},{6,5},{7,6},{8,7},{9,8},{10,9},{11,1... | collective-permute-start | bytes 1572872 | tf_op jit(solution)/shard_map/ppermute | solution.py:779
  3.6 12.8 %collective-permute-start = (bf16[2,1024,128]{2,1,0:T(8,128)(2,1)}, bf16[2,1024,128]{2,1,0:T(8,128)(2,1)S(1)}, u32[]{:S(2)}, u32[]{:S(2)}) collective-permute-start(bf16[2,1024,128]{2,1,0:T(8,128)(2,1)} %get-tuple-element.29), channel_id=1, source_target_pairs={{1,0},{2,1},{3,2},{4,3},{5,4},{6,5},{7,6},{8,7},{9,8},{10,9},{11,1... | collective-permute-start | bytes 1572872 | tf_op jit(solution)/shard_map/ppermute | solution.py:779
  4.9 1.6 %copy-start = (bf16[2,64,32,256]{3,2,1,0:T(8,128)(2,1)S(1)}, bf16[2,64,32,256]{3,2,1,0:T(8,128)(2,1)}, u32[]{:S(2)}) copy-start(bf16[2,64,32,256]{3,2,1,0:T(8,128)(2,1)} %param.8) | copy-start | bytes 6291460
  6.5 0.7 copy-start.3
  11.3 3.0 %collective-permute-start.1 = (bf16[18,2,32,128]{3,2,1,0:T(8,128)(2,1)S(1)}, bf16[18,2,32,128]{3,2,1,0:T(8,128)(2,1)S(1)}, u32[]{:S(2)}, u32[]{:S(2)}) collective-permute-start(bf16[18,2,32,128]{3,2,1,0:T(8,128)(2,1)S(1)} %get-tuple-element.31), channel_id=1, source_target_pairs={{0,1},{1,0},{2,3},{3,2},{4,5},{5,4},{6,7},{7,6},{8,9},{9,8},{10,11... | collective-permute-start | bytes 884744 | tf_op jit(solution)/shard_map/ppermute | solution.py:288
  13.1 1.6 %collective-permute-start.2 = (bf16[18,2,32,128]{3,2,1,0:T(8,128)(2,1)S(1)}, bf16[18,2,32,128]{3,2,1,0:T(8,128)(2,1)S(1)}, u32[]{:S(2)}, u32[]{:S(2)}) collective-permute-start(bf16[18,2,32,128]{3,2,1,0:T(8,128)(2,1)S(1)} %get-tuple-element.32), channel_id=1, source_target_pairs={{0,1},{1,0},{2,3},{3,2},{4,5},{5,4},{6,7},{7,6},{8,9},{9,8},{10,11... | collective-permute-start | bytes 884744 | tf_op jit(solution)/shard_map/ppermute | solution.py:288
  16.0 5.2 %collective-permute-start.5 = (bf16[18,2,32,128]{3,2,1,0:T(8,128)(2,1)S(1)}, bf16[18,2,32,128]{3,2,1,0:T(8,128)(2,1)S(1)}, u32[]{:S(2)}, u32[]{:S(2)}) collective-permute-start(bf16[18,2,32,128]{3,2,1,0:T(8,128)(2,1)S(1)} %get-tuple-element.37), channel_id=1, source_target_pairs={{0,1},{1,0},{2,3},{3,2},{4,5},{5,4},{6,7},{7,6},{8,9},{9,8},{10,11... | collective-permute-start | bytes 884744 | tf_op jit(solution)/shard_map/ppermute | solution.py:288
  17.2 4.8 %collective-permute-start.4 = (bf16[18,2,32,128]{3,2,1,0:T(8,128)(2,1)S(1)}, bf16[18,2,32,128]{3,2,1,0:T(8,128)(2,1)S(1)}, u32[]{:S(2)}, u32[]{:S(2)}) collective-permute-start(bf16[18,2,32,128]{3,2,1,0:T(8,128)(2,1)S(1)} %get-tuple-element.36), channel_id=1, source_target_pairs={{0,1},{1,0},{2,3},{3,2},{4,5},{5,4},{6,7},{7,6},{8,9},{9,8},{10,11... | collective-permute-start | bytes 884744 | tf_op jit(solution)/shard_map/ppermute | solution.py:288
  22.7 9.1 %collective-permute-start.6 = (f32[8,80,128]{2,1,0:T(8,128)S(1)}, f32[8,80,128]{2,1,0:T(8,128)S(1)}, u32[]{:S(2)}, u32[]{:S(2)}) collective-permute-start(f32[8,80,128]{2,1,0:T(8,128)S(1)} %shard_map.90), channel_id=1, source_target_pairs={{0,2},{1,5},{2,0},{3,7},{4,6},{5,1},{6,4},{7,3},{8,10},{9,13},{10,... | collective-permute-start | bytes 983048 | tf_op jit(solution)/shard_map/ppermute | solution.py:288
  25.1 7.6 %collective-permute-start.7 = (f32[8,80,128]{2,1,0:T(8,128)S(1)}, f32[8,80,128]{2,1,0:T(8,128)S(1)}, u32[]{:S(2)}, u32[]{:S(2)}) collective-permute-start(f32[8,80,128]{2,1,0:T(8,128)S(1)} %shard_map.91), channel_id=1, source_target_pairs={{0,4},{1,3},{2,6},{3,1},{4,0},{5,7},{6,2},{7,5},{8,12},{9,11},{10,... | collective-permute-start | bytes 983048 | tf_op jit(solution)/shard_map/ppermute | solution.py:288
  32.9 7.6 %collective-permute-start.8 = (f32[4,80,128]{2,1,0:T(8,128)S(1)}, f32[4,80,128]{2,1,0:T(8,128)S(1)}, u32[]{:S(2)}, u32[]{:S(2)}) collective-permute-start(f32[4,80,128]{2,1,0:T(8,128)S(1)} %get-tuple-element.38), channel_id=1, source_target_pairs={{0,4},{1,3},{2,6},{3,1},{4,0},{5,7},{6,2},{7,5},{8,12},{9,11},{10,... | collective-permute-start | bytes 491528 | tf_op jit(solution)/shard_map/ppermute | solution.py:288
  36.1 5.3 %collective-permute-start.9 = (f32[4,80,128]{2,1,0:T(8,128)S(1)}, f32[4,80,128]{2,1,0:T(8,128)S(1)}, u32[]{:S(2)}, u32[]{:S(2)}) collective-permute-start(f32[4,80,128]{2,1,0:T(8,128)S(1)} %get-tuple-element.39), channel_id=1, source_target_pairs={{0,2},{1,5},{2,0},{3,7},{4,6},{5,1},{6,4},{7,3},{8,10},{9,13},{10,... | collective-permute-start | bytes 491528 | tf_op jit(solution)/shard_map/ppermute | solution.py:288
  41.6 11.4 %copy-start.2 = (f32[8,128]{1,0:T(8,128)S(1)}, f32[8,128]{1,0:T(8,128)}, u32[]{:S(2)}) copy-start(f32[8,128]{1,0:T(8,128)} %constant.5.clone.steer_ref) | copy-start | bytes 12292
  41.6 9.5 %collective-permute-start.10 = (f32[160,128]{1,0:T(8,128)S(1)}, f32[160,128]{1,0:T(8,128)S(1)}, u32[]{:S(2)}, u32[]{:S(2)}) collective-permute-start(f32[160,128]{1,0:T(8,128)S(1)} %get-tuple-element.40), channel_id=1, source_target_pairs={{0,16},{1,17},{2,18},{3,19},{4,20},{5,21},{6,22},{7,23},{8,24},{9,... | collective-permute-start | bytes 245768 | tf_op jit(solution)/shard_map/ppermute | solution.py:288
  44.2 6.8 %collective-permute-start.11 = (f32[160,128]{1,0:T(8,128)S(1)}, f32[160,128]{1,0:T(8,128)S(1)}, u32[]{:S(2)}, u32[]{:S(2)}) collective-permute-start(f32[160,128]{1,0:T(8,128)S(1)} %get-tuple-element.41), channel_id=1, source_target_pairs={{0,24},{1,25},{2,26},{3,27},{4,28},{5,29},{6,30},{7,31},{8,16},{9,... | collective-permute-start | bytes 245768 | tf_op jit(solution)/shard_map/ppermute | solution.py:288
  45.6 33.3 %copy-start.5 = (s32[32]{0:T(128)S(1)}, s32[32]{0:T(128)}, u32[]{:S(2)}) copy-start(s32[32]{0:T(128)} %bin_ref.1) | copy-start | bytes 388
  45.6 33.3 %copy-start.6 = (s32[32]{0:T(128)S(1)}, s32[32]{0:T(128)}, u32[]{:S(2)}) copy-start(s32[32]{0:T(128)} %block_ref.1) | copy-start | bytes 388
  45.6 33.3 %copy-start.7 = (s32[32]{0:T(128)S(1)}, s32[32]{0:T(128)}, u32[]{:S(2)}) copy-start(s32[32]{0:T(128)} %beam_ref.1) | copy-start | bytes 388
  45.6 33.3 %copy-start.8 = (s32[32,1]{0,1:T(1,128)S(1)}, s32[32,1]{0,1:T(1,128)}, u32[]{:S(2)}) copy-start(s32[32,1]{0,1:T(1,128)} %param.13) | copy-start | bytes 388
  45.6 6.1 %collective-permute-start.12 = (f32[160,128]{1,0:T(8,128)S(1)}, f32[160,128]{1,0:T(8,128)S(1)}, u32[]{:S(2)}, u32[]{:S(2)}) collective-permute-start(f32[160,128]{1,0:T(8,128)S(1)} %get-tuple-element.42), channel_id=1, source_target_pairs={{0,8},{1,9},{2,10},{3,11},{4,12},{5,13},{6,14},{7,15},{8,0},{9,1},... | collective-permute-start | bytes 245768 | tf_op jit(solution)/shard_map/ppermute | solution.py:288
  51.8 5.1 %collective-permute-start.13 = (f32[160,128]{1,0:T(8,128)S(1)}, f32[160,128]{1,0:T(8,128)S(1)}, u32[]{:S(2)}, u32[]{:S(2)}) collective-permute-start(f32[160,128]{1,0:T(8,128)S(1)} %get-tuple-element.43.own_ref), channel_id=1, source_target_pairs={{0,2},{1,0},{2,6},{3,1},{4,12},{5,7},{6,4},{7,3},{8,16},{9,11},{10... | collective-permute-start | bytes 245768 | tf_op jit(solution)/shard_map/ppermute | solution.py:433
  52.9 4.0 %collective-permute-start.14 = (f32[32,128]{1,0:T(8,128)S(1)}, f32[32,128]{1,0:T(8,128)S(1)}, u32[]{:S(2)}, u32[]{:S(2)}) collective-permute-start(f32[32,128]{1,0:T(8,128)S(1)} %get-tuple-element.44.packed_ref), channel_id=1, source_target_pairs={{0,1},{1,3},{2,0},{3,7},{4,6},{5,13},{6,2},{7,5},{8,10},{9,17},{10... | collective-permute-start | bytes 49160 | tf_op jit(solution)/shard_map/ppermute | solution.py:433
